TPU v7x, 256 devices: a whole 4x4x8 slice. The times are simulated.
256 devices in a mesh: line: 16 (over x_hi, y, core), out: 16 (over x_lo, z).
Axes of the slice: x: 4 (x_hi: 2, x_lo: 2; x = x_hi * 2 + x_lo), y: 4, z: 8, core: 2. Of those that a mesh axis runs over, the one named last changes fastest.
Arguments:
- injections: float32 [8, 8192], P(None, 'out'), may hold values from -6 to 6
- transfer_factors: float32 [16384, 8192], P('line', 'out'), may hold values from -0.09375 to 0.09375
- outage_factors: float32 [16384, 16384], P('line', 'out'), may hold values from -3 to 3
- line_limits: float32 [16384], P('line'), may hold values from 0.5 to 2
- outage_lines: int32 [16384], replicated, may hold values from 0 to 16383, each once
Outputs:
- injection_gradient: float32 [8, 8192], P(None, ('out', 'line'))
Inputs may be any that keep to these rules, and one draw needn't show every extreme that they name: `outage_lines`: each of the 16384 lines is taken out in exactly one outage.
All inputs are finite; a program needn't handle non-finite values.
Results may differ from a plain program's by a relative error of at most 0.0001.
Values sent between devices are 32-bit elements; how exact they have to be, the bound alone decides.
No kernel may reach another device: no remote copies, remote signals or barrier semaphores. Data moves between devices by JAX's collectives and lax.ppermute only.
A program may use at most 128 MiB of HBM per device.

v0:
```python
import jax
import jax.numpy as jnp
from jax import lax
from jax.sharding import PartitionSpec as P

OUTAGES = 16384


SOFTNESS = 0.25


def overload_terms(factors, flow_rows, flow_out, limits, scale):
    rows, width = factors.shape
    hours = flow_rows.shape[0]
    block = min(256, rows)
    count = rows // block
    factor_blocks = factors.reshape(count, block, width)
    flow_blocks = jnp.transpose(flow_rows.reshape(hours, count, block), (1, 0, 2))
    limit_blocks = limits.reshape(count, block)

    def advance(column_total, pieces):
        factor_piece, flow_piece, limit_piece = pieces
        post = flow_piece[:, :, None] + factor_piece[None, :, :] * flow_out[:, None, :]
        bound = limit_piece[None, :, None]
        slope = (
            jax.nn.sigmoid((post - bound) / SOFTNESS) - jax.nn.sigmoid((-post - bound) / SOFTNESS)
        ) * scale
        row_total = jnp.sum(slope, axis=2)
        column_total = column_total + jnp.einsum(
            "hlk,lk->hk", slope, factor_piece, precision=lax.Precision.HIGHEST
        )
        return (column_total, row_total)

    column_total, row_blocks = lax.scan(
        advance, jnp.zeros((hours, width), jnp.float32), (factor_blocks, flow_blocks, limit_blocks)
    )
    row_total = jnp.transpose(row_blocks, (1, 0, 2)).reshape(hours, rows)
    return (row_total, column_total)


def local(injections, transfer_factors, outage_factors, line_limits, outage_lines):
    rows = transfer_factors.shape[0]
    hours = injections.shape[0]
    width = outage_factors.shape[1]
    total_lines = rows * lax.axis_size("line")
    line_start = lax.axis_index("line") * rows
    out_start = lax.axis_index("out") * width
    partial_flows = jnp.einsum(
        "hb,lb->hl", injections, transfer_factors, precision=lax.Precision.HIGHEST
    )
    flow_rows = lax.psum(partial_flows, "out")
    flows = lax.all_gather(flow_rows, "line", axis=1, tiled=True)
    local_outages = lax.dynamic_slice_in_dim(outage_lines, out_start, width, 0)
    flow_out = jnp.take(flows, local_outages, axis=1)
    row_part, column_part = overload_terms(
        outage_factors, flow_rows, flow_out, line_limits, 1.0 / OUTAGES
    )
    row_total = lax.psum(row_part, "out")
    column_total = lax.psum(column_part, "line")
    all_columns = lax.all_gather(column_total, "out", axis=1, tiled=True)
    spread = jnp.zeros((hours, total_lines), jnp.float32).at[:, outage_lines].add(all_columns)
    line_slopes = row_total + lax.dynamic_slice_in_dim(spread, line_start, rows, 1)
    bus_terms = jnp.einsum(
        "hl,lb->hb", line_slopes, transfer_factors, precision=lax.Precision.HIGHEST
    )
    return lax.psum_scatter(bus_terms, "line", scatter_dimension=1, tiled=True)


def solution(mesh):
    in_specs = (P(None, "out"), P("line", "out"), P("line", "out"), P("line"), P())
    out_specs = P(None, ("out", "line"))
    return jax.shard_map(local, mesh=mesh, in_specs=in_specs, out_specs=out_specs, check_vma=False)
```

profile of v0, /device:TPU:33, one launch (start us, length us, event | category | flops | bytes accessed | tf_op | source)
XLA Modules:
  0.0 507.7 jit_solution(7887158690204215590)
XLA Ops:
  6.5 0.8 fusion.5
  7.4 0.7 compare_and_fusion
  8.1 0.8 compare_select_fusion
  8.9 2.5 fusion.7
  11.5 48.7 %psum.21 = f32[8,1024]{1,0:T(8,128)S(1)} all-reduce(f32[8,1024]{1,0:T(8,128)S(1)} %fusion.7), channel_id=1, replica_groups=mesh['line'=16,'out'=16] {'out'}, use_global_device_ids=true, to_apply=%region_0.0 | all-reduce | flops 8192 | bytes 65536 | tf_op jit(solution)/shard_map/psum | solution.py:51
  60.1 39.6 %all_gather.6 = f32[8,16384]{1,0:T(8,128)S(1)} all-gather(f32[8,1024]{1,0:T(8,128)S(1)} %psum.21), channel_id=1, replica_groups=mesh['line'=16,'out'=16] {'line'}, dimensions={1}, use_global_device_ids=true | all-gather | bytes 557056 | tf_op jit(solution)/shard_map/all_gather | solution.py:52
  99.7 5.2 %copy.14 = f32[8,16384]{0,1:T(8,128)} copy(f32[8,16384]{1,0:T(8,128)S(1)} %all_gather.6) | data formatting | bytes 1048576 | tf_op jit(solution)/shard_map/all_gather | solution.py:52
  104.9 6.2 %gather_fusion = f32[1024,8]{1,0:T(8,128)S(1)} fusion(f32[8,16384]{0,1:T(8,128)} %copy.14, s32[1024]{0:T(1024)S(1)} %fusion.5), kind=kCustom, calls=%fused_computation | custom fusion | bytes 69632 | tf_op jit(solution)/shard_map/jit(_take)/gather | solution.py:54
  111.1 0.2 select_bitcast_fusion
  111.3 0.2 copy.15
  111.5 54.6 %while.13 = (s32[]{:T(128)}, f32[8,1024]{1,0:T(8,128)S(1)}, f32[4,8,256]{2,1,0:T(8,128)S(1)}, f32[4,256,1024]{2,1,0:T(8,128)}, f32[4,8,256]{2,1,0:T(8,128)S(1)},...) while((s32[]{:T(128)}, f32[8,1024]{1,0:T(8,128)S(1)}, ...), condition=%wide.region_3.4_spmd.clone, body=%wide.region_1.0_spmd.clone.sunk | while | flops 69212160 | bytes 6549623 | solution.py:34
  111.5 1.5 dynamic-slice_bitcast_fusion.5
  113.0 5.8 %multiply_reduce_fusion.2 = f32[1024,8]{0,1:T(8,128)S(1)} fusion(f32[1024,256]{0,1:T(8,128)S(1)} %get-tuple-element.151, f32[256]{0:T(256)S(1)} %bitcast.46, f32[8,1024]{1,0:T(8,128)S(1)} %get-tuple-element.176, f32[256,1024]{1,0:T(8,128)S(1)} %get-tuple-element.152, f32[8,256]{1,0:T(8,128)S(1)} %dynamic-slice_bitcast_fusion.6), kind=kLoop, calls=%fused_computation.2.clone.1 | loop fusion | flops 35643392 | bytes 2171904 | tf_op jit(solution)/shard_map/while/body/eval_jaxpr/hlk,lk->hk/dot_general | solution.py:29
  118.9 6.2 %fusion.12 = f32[8,256]{1,0:T(8,128)S(1)} fusion(f32[256]{0:T(256)S(1)} %bitcast.47, f32[8,1024]{1,0:T(8,128)S(1)} %get-tuple-element.176, f32[256,1024]{1,0:T(8,128)S(1)} %get-tuple-element.152, f32[8,256]{1,0:T(8,128)S(1)} %dynamic-slice_bitcast_fusion.6), kind=kLoop, calls=%fused_computation.4.clone.1 | loop fusion | flops 33552384 | bytes 1098752 | tf_op jit(solution)/shard_map/while/body/eval_jaxpr/reduce_sum | solution.py:28
  125.2 1.5 dynamic-slice_bitcast_fusion.5
  126.7 5.8 %multiply_reduce_fusion.2 = f32[1024,8]{0,1:T(8,128)S(1)} fusion(f32[1024,256]{0,1:T(8,128)S(1)} %get-tuple-element.151, f32[256]{0:T(256)S(1)} %bitcast.46, f32[8,1024]{1,0:T(8,128)S(1)} %get-tuple-element.176, f32[256,1024]{1,0:T(8,128)S(1)} %get-tuple-element.152, f32[8,256]{1,0:T(8,128)S(1)} %dynamic-slice_bitcast_fusion.6), kind=kLoop, calls=%fused_computation.2.clone.1 | loop fusion | flops 35643392 | bytes 2171904 | tf_op jit(solution)/shard_map/while/body/eval_jaxpr/hlk,lk->hk/dot_general | solution.py:29
  132.5 6.2 %fusion.12 = f32[8,256]{1,0:T(8,128)S(1)} fusion(f32[256]{0:T(256)S(1)} %bitcast.47, f32[8,1024]{1,0:T(8,128)S(1)} %get-tuple-element.176, f32[256,1024]{1,0:T(8,128)S(1)} %get-tuple-element.152, f32[8,256]{1,0:T(8,128)S(1)} %dynamic-slice_bitcast_fusion.6), kind=kLoop, calls=%fused_computation.4.clone.1 | loop fusion | flops 33552384 | bytes 1098752 | tf_op jit(solution)/shard_map/while/body/eval_jaxpr/reduce_sum | solution.py:28
  138.8 1.5 dynamic-slice_bitcast_fusion.5
  140.3 5.8 %multiply_reduce_fusion.2 = f32[1024,8]{0,1:T(8,128)S(1)} fusion(f32[1024,256]{0,1:T(8,128)S(1)} %get-tuple-element.151, f32[256]{0:T(256)S(1)} %bitcast.46, f32[8,1024]{1,0:T(8,128)S(1)} %get-tuple-element.176, f32[256,1024]{1,0:T(8,128)S(1)} %get-tuple-element.152, f32[8,256]{1,0:T(8,128)S(1)} %dynamic-slice_bitcast_fusion.6), kind=kLoop, calls=%fused_computation.2.clone.1 | loop fusion | flops 35643392 | bytes 2171904 | tf_op jit(solution)/shard_map/while/body/eval_jaxpr/hlk,lk->hk/dot_general | solution.py:29
  146.2 6.2 %fusion.12 = f32[8,256]{1,0:T(8,128)S(1)} fusion(f32[256]{0:T(256)S(1)} %bitcast.47, f32[8,1024]{1,0:T(8,128)S(1)} %get-tuple-element.176, f32[256,1024]{1,0:T(8,128)S(1)} %get-tuple-element.152, f32[8,256]{1,0:T(8,128)S(1)} %dynamic-slice_bitcast_fusion.6), kind=kLoop, calls=%fused_computation.4.clone.1 | loop fusion | flops 33552384 | bytes 1098752 | tf_op jit(solution)/shard_map/while/body/eval_jaxpr/reduce_sum | solution.py:28
  152.4 1.5 dynamic-slice_bitcast_fusion.5
  153.9 5.8 %multiply_reduce_fusion.2 = f32[1024,8]{0,1:T(8,128)S(1)} fusion(f32[1024,256]{0,1:T(8,128)S(1)} %get-tuple-element.151, f32[256]{0:T(256)S(1)} %bitcast.46, f32[8,1024]{1,0:T(8,128)S(1)} %get-tuple-element.176, f32[256,1024]{1,0:T(8,128)S(1)} %get-tuple-element.152, f32[8,256]{1,0:T(8,128)S(1)} %dynamic-slice_bitcast_fusion.6), kind=kLoop, calls=%fused_computation.2.clone.1 | loop fusion | flops 35643392 | bytes 2171904 | tf_op jit(solution)/shard_map/while/body/eval_jaxpr/hlk,lk->hk/dot_general | solution.py:29
  159.8 6.2 %fusion.12 = f32[8,256]{1,0:T(8,128)S(1)} fusion(f32[256]{0:T(256)S(1)} %bitcast.47, f32[8,1024]{1,0:T(8,128)S(1)} %get-tuple-element.176, f32[256,1024]{1,0:T(8,128)S(1)} %get-tuple-element.152, f32[8,256]{1,0:T(8,128)S(1)} %dynamic-slice_bitcast_fusion.6), kind=kLoop, calls=%fused_computation.4.clone.1 | loop fusion | flops 33552384 | bytes 1098752 | tf_op jit(solution)/shard_map/while/body/eval_jaxpr/reduce_sum | solution.py:28
  166.1 59.4 %psum.23 = f32[8,1024]{1,0:T(8,128)S(1)} all-reduce(f32[8,1024]{1,0:T(8,128)S(1)} %get-tuple-element.44), channel_id=1, replica_groups=mesh['line'=16,'out'=16] {'line'}, use_global_device_ids=true, to_apply=%region_5.6 | all-reduce | flops 8192 | bytes 65536 | tf_op jit(solution)/shard_map/psum | solution.py:59
  225.4 29.9 %all_gather.7 = f32[8,16384]{1,0:T(8,128)S(1)} all-gather(f32[8,1024]{1,0:T(8,128)S(1)} %psum.23), channel_id=1, replica_groups=mesh['line'=16,'out'=16] {'out'}, dimensions={1}, use_global_device_ids=true | all-gather | bytes 557056 | tf_op jit(solution)/shard_map/all_gather | solution.py:60
  255.4 5.3 %copy.17 = f32[16384,8]{1,0:T(8,128)} copy(f32[16384,8]{0,1:T(8,128)S(1)} %bitcast.42) | data formatting | bytes 1048576 | tf_op jit(solution)/shard_map/all_gather | solution.py:60
  260.6 0.2 copy.16
  260.8 51.0 %psum.22 = f32[8,1024]{0,1:T(8,128)S(1)} all-reduce(f32[8,1024]{0,1:T(8,128)S(1)} %bitcast.43), channel_id=1, replica_groups=mesh['line'=16,'out'=16] {'out'}, use_global_device_ids=true, to_apply=%region_4.5 | all-reduce | flops 8192 | bytes 65536 | tf_op jit(solution)/shard_map/psum | solution.py:58
  311.9 91.3 %scatter_custom_fusion = f32[8,16384]{0,1:T(8,128)} fusion(s32[16384]{0:T(1024)S(1)} %compare_select_fusion, f32[16384,8]{1,0:T(8,128)} %copy.17, f32[]{:T(128)} %constant.31.clone.1), kind=kCustom, calls=%fused_computation.11 | custom fusion | flops 131072 | bytes 524800 | tf_op jit(solution)/shard_map/scatter-add | solution.py:61
  403.2 5.2 %convolution_bitcast_fusion = f32[512,8]{1,0:T(8,128)} fusion(f32[1024,512]{1,0:T(8,128)S(1)} %copy-done, f32[8,1024]{0,1:T(8,128)S(1)} %psum.22, f32[8,16384]{0,1:T(8,128)} %scatter_custom_fusion, s32[]{:T(128)S(6)} %select_n.22), kind=kOutput, calls=%fused_computation.13 | convolution fusion | flops 50339840 | bytes 2670596
  408.4 91.0 %reduce-scatter.4.cloned.1.call-done = f32[32,8]{1,0:T(8,128)} async-done(((f32[512,8]{1,0:T(8,128)}), f32[32,8]{1,0:T(8,128)}) %reduce-scatter.4.cloned.1.call-update) | async-done | bytes 1040
  499.4 1.4 copy.25
  (25 shorter events, 0.2 us)
Async XLA Ops:
  6.5 2.4 copy-start
  6.5 105.0 %copy-start.1 = (f32[1024]{0:T(1024)S(1)}, f32[1024]{0:T(1024)}, u32[]{:S(2)}) copy-start(f32[1024]{0:T(1024)} %param.10) | copy-start | bytes 12292
  6.5 492.9 %reduce-scatter.4.cloned.1.call-start = ((), (), s32[]{:S(2)}) async-start(), calls=%async_computation.1 | async-start | bytes 278528
Sparse Core Ops, SparseCore 0:
  408.6 90.8 reduce-scatter.3
where the time goes:
time: 510 us; the launch traced here: 508 us
  blocking collectives  229 us (45%)
  other arithmetic  142 us (28%)
  waiting for transfers between devices  91 us (18%)
  local copies, waits for them, and re-layouts  24.4 us (5%)
  between operations  13.4 us (3%)
  matrix products  7.7 us (2%)
    scatter-add x1, other arithmetic, local(): jnp.zeros((hours, total_lines), jnp.float32).at[:, outage_lines]  91.3 us
    unnamed x2, waiting for transfers between devices  91 us
    psum x1, blocking collectives, local(): column_total = lax.psum(column_part, 'line')  59.4 us
    psum x1, blocking collectives, local(): row_total = lax.psum(row_part, 'out')  51 us
    psum x1, blocking collectives, local(): flow_rows = lax.psum(partial_flows, 'out')  48.7 us
    all_gather x1, blocking collectives, local(): flows = lax.all_gather(flow_rows, 'line', axis=1, tiled=True)  39.6 us
    all_gather x1, blocking collectives, local(): all_columns = lax.all_gather(column_total, 'out', axis=1, tiled=True)  29.9 us
    reduce_sum x4, other arithmetic, advance(): row_total = jnp.sum(slope, axis=2)  24.9 us
  transfers between devices with their start and end apart: 1, of which 1 were waited for; matrix products, arithmetic and copies ran while one was open for 0% of the time, Pallas kernels for 0%

commit v1 on v0

v1 whole, which is shorter than its diff:
```python
import functools

import jax
import jax.numpy as jnp
from jax import lax
from jax.experimental import pallas as pl
from jax.experimental.pallas import tpu as pltpu
from jax.sharding import PartitionSpec as P

OUTAGES = 16384
SOFTNESS = 0.25
LANES = 128
SUB = 8
VMEM = pl.BlockSpec(memory_space=pltpu.VMEM)


def params(mib):
    return pltpu.CompilerParams(vmem_limit_bytes=mib * 1024 * 1024)


def flows_kernel(injections_ref, factors_ref, out_ref):
    out_ref[...] = lax.dot_general(
        injections_ref[...],
        factors_ref[...],
        (((1,), (1,)), ((), ())),
        precision=lax.Precision.HIGHEST,
        preferred_element_type=jnp.float32,
    )


def bus_kernel(slopes_ref, factors_ref, out_ref):
    out_ref[...] = jnp.dot(
        slopes_ref[...],
        factors_ref[...],
        precision=lax.Precision.HIGHEST,
        preferred_element_type=jnp.float32,
    )


def inverse_kernel(index_ref, out_ref):
    width = index_ref.shape[1]
    lane = lax.broadcasted_iota(jnp.int32, (LANES, LANES), 1)
    row = lax.broadcasted_iota(jnp.int32, (LANES, LANES), 0)
    totals = [jnp.zeros((1, LANES), jnp.int32) for _ in range(out_ref.shape[1] // LANES)]
    for kb in range(width // LANES):
        piece = index_ref[:, kb * LANES : (kb + 1) * LANES].astype(jnp.float32)
        column = jnp.transpose(jnp.broadcast_to(piece, (LANES, LANES))).astype(jnp.int32)
        for lb in range(len(totals)):
            hit = jnp.where(column == lane + lb * LANES, row + (kb * LANES + 1), 0)
            totals[lb] = totals[lb] + jnp.sum(hit, axis=0, keepdims=True)
    for lb, total in enumerate(totals):
        out_ref[:, lb * LANES : (lb + 1) * LANES] = total - 1


def pick(values_ref, index_ref, kb):
    hours, width = values_ref.shape
    index = jnp.broadcast_to(index_ref[:, kb * LANES : (kb + 1) * LANES], (hours, LANES))
    low = jnp.bitwise_and(index, LANES - 1)
    high = jnp.right_shift(index, 7)
    result = jnp.zeros((hours, LANES), jnp.float32)
    for q in range(width // LANES):
        found = jnp.take_along_axis(values_ref[:, q * LANES : (q + 1) * LANES], low, axis=1)
        result = jnp.where(high == q, found, result)
    return result


def select_kernel(values_ref, index_ref, out_ref):
    for kb in range(out_ref.shape[1] // LANES):
        out_ref[:, kb * LANES : (kb + 1) * LANES] = pick(values_ref, index_ref, kb)


def place_kernel(values_ref, index_ref, rows_ref, out_ref):
    for kb in range(out_ref.shape[1] // LANES):
        here = slice(kb * LANES, (kb + 1) * LANES)
        out_ref[:, here] = pick(values_ref, index_ref, kb) + rows_ref[:, here]


def overload_kernel(
    factors_ref, flow_ref, out_flow_ref, limit_ref, row_ref, column_ref, up, down, wide, total, sums
):
    rows, width = factors_ref.shape
    hours = flow_ref.shape[0]
    blocks = width // LANES
    tile = 2 * SUB
    gain = 0.5 / SOFTNESS
    scale = 0.5 / OUTAGES
    pad = jnp.zeros((LANES - hours, LANES), jnp.float32)
    for lb in range(rows // LANES):
        here = slice(lb * LANES, (lb + 1) * LANES)
        flow = gain * flow_ref[:, here]
        limit = gain * limit_ref[:, here]
        up[here, :] = jnp.transpose(jnp.concatenate([flow + limit, pad], axis=0))
        down[here, :] = jnp.transpose(jnp.concatenate([flow - limit, pad], axis=0))
    for h in range(hours):
        for kb in range(blocks):
            piece = gain * out_flow_ref[h : h + 1, kb * LANES : (kb + 1) * LANES]
            wide[h * blocks + kb] = jnp.broadcast_to(piece, (SUB, LANES))
    total[...] = jnp.zeros_like(total)
    lane = lax.broadcasted_iota(jnp.int32, (SUB, LANES), 1)

    def advance(step, carry):
        start = pl.multiple_of(step * tile, tile)
        parts = range(tile // SUB)
        factor = [
            [factors_ref[pl.ds(start + r * SUB, SUB), kb * LANES : (kb + 1) * LANES] for kb in range(blocks)]
            for r in parts
        ]
        ups = [up[pl.ds(start + r * SUB, SUB), :] for r in parts]
        downs = [down[pl.ds(start + r * SUB, SUB), :] for r in parts]
        kept = [jnp.zeros((SUB, LANES), jnp.float32) for r in parts]
        for h in range(hours):
            plus = [jnp.broadcast_to(ups[r][:, h : h + 1], (SUB, LANES)) for r in parts]
            minus = [jnp.broadcast_to(downs[r][:, h : h + 1], (SUB, LANES)) for r in parts]
            across = [None for r in parts]
            for kb in range(blocks):
                out_flow = wide[h * blocks + kb]
                gathered = None
                for r in parts:
                    moved = factor[r][kb] * out_flow
                    slope = jnp.tanh(moved + plus[r]) + jnp.tanh(moved + minus[r])
                    across[r] = slope if across[r] is None else across[r] + slope
                    weighted = slope * factor[r][kb]
                    gathered = weighted if gathered is None else gathered + weighted
                total[h * blocks + kb] = total[h * blocks + kb] + gathered
            for r in parts:
                kept[r] = jnp.where(lane == h, jnp.sum(across[r], axis=1, keepdims=True), kept[r])
        for r in parts:
            sums[pl.ds(start + r * SUB, SUB), :] = kept[r]
        return carry

    lax.fori_loop(0, rows // tile, advance, 0)
    for lb in range(rows // LANES):
        here = slice(lb * LANES, (lb + 1) * LANES)
        row_ref[:, here] = scale * jnp.transpose(sums[here, :])[:hours, :]
    for h in range(hours):
        for kb in range(blocks):
            column_ref[h : h + 1, kb * LANES : (kb + 1) * LANES] = scale * jnp.sum(
                total[h * blocks + kb], axis=0, keepdims=True
            )


def call(kernel, shape, *operands, dtype=jnp.float32, mib=8, flops=0, scratch=()):
    size = sum(a.size * 4 for a in operands)
    out_shape = [jax.ShapeDtypeStruct(s, dtype) for s in shape]
    result = pl.pallas_call(
        kernel,
        out_shape=out_shape,
        in_specs=[VMEM] * len(operands),
        out_specs=[VMEM] * len(shape),
        scratch_shapes=list(scratch),
        compiler_params=params(mib),
        cost_estimate=pl.CostEstimate(flops=flops, bytes_accessed=size, transcendentals=0),
    )(*operands)
    return result[0] if len(shape) == 1 else result


def partner_sum(x, axis, partners):
    return x + lax.ppermute(x, axis, list(enumerate(partners)))


def out_steps(count):
    depth = count // 2
    steps = [[o ^ depth for o in range(count)]]
    bit = 1
    while bit < depth // 2:
        steps.append([o ^ bit for o in range(count)])
        bit *= 2
    if depth > 1:
        steps.append([(o & depth) | (depth - 1 - (o & (depth - 1))) for o in range(count)])
    return steps


def line_steps(count):
    steps = []
    bit = count // 2
    while bit:
        steps.append([i ^ bit for i in range(count)])
        bit //= 2
    return steps


def sum_over(x, axis, steps):
    for partners in steps:
        x = partner_sum(x, axis, partners)
    return x


def local(injections, transfer_factors, outage_factors, line_limits, outage_lines):
    rows, buses = transfer_factors.shape
    hours = injections.shape[0]
    width = outage_factors.shape[1]
    blocks = width // LANES
    over_out = out_steps(lax.axis_size("out"))
    over_line = line_steps(lax.axis_size("line"))
    line_start = lax.axis_index("line") * rows
    out_start = lax.axis_index("out") * width
    index = lax.dynamic_slice_in_dim(outage_lines, out_start, width, 0) - line_start
    index = index.reshape(1, width)
    limits = line_limits.reshape(1, rows)

    partial_flows = call(flows_kernel, [(hours, rows)], injections, transfer_factors, mib=16)
    inverse = call(inverse_kernel, [(1, rows)], index, dtype=jnp.int32)
    flow_rows = sum_over(partial_flows, "out", over_out)
    selected = call(select_kernel, [(hours, width)], flow_rows, index)
    flow_out = sum_over(selected, "line", over_line)
    row_part, column_part = call(
        overload_kernel,
        [(hours, rows), (hours, width)],
        outage_factors,
        flow_rows,
        flow_out,
        limits,
        mib=24,
        scratch=[
            pltpu.VMEM((rows, LANES), jnp.float32),
            pltpu.VMEM((rows, LANES), jnp.float32),
            pltpu.VMEM((hours * blocks, SUB, LANES), jnp.float32),
            pltpu.VMEM((hours * blocks, SUB, LANES), jnp.float32),
            pltpu.VMEM((rows, LANES), jnp.float32),
        ],
    )
    column_total = sum_over(column_part, "line", over_line)
    placed = call(place_kernel, [(hours, rows)], column_total, inverse, row_part)
    line_slopes = sum_over(placed, "out", over_out)
    bus_terms = call(bus_kernel, [(hours, buses)], line_slopes, transfer_factors, mib=16)
    gradient = sum_over(bus_terms, "line", over_line)
    own = buses // lax.axis_size("line")
    return lax.dynamic_slice_in_dim(gradient, lax.axis_index("line") * own, own, 1)


def solution(mesh):
    in_specs = (P(None, "out"), P("line", "out"), P("line", "out"), P("line"), P())
    out_specs = P(None, ("out", "line"))
    return jax.shard_map(local, mesh=mesh, in_specs=in_specs, out_specs=out_specs, check_vma=False)
```

time: 510 us -> 129 us (0.25)
  blocking collectives: 229 us -> 0 us
  other arithmetic: 142 us -> 1.45 us
  waiting for transfers between devices: 91 us -> 29.8 us
  starting transfers between devices: 0.01 us -> 56.7 us
  Pallas kernels: 0 us -> 35.8 us
  local copies, waits for them, and re-layouts: 24.4 us -> 5.18 us
  between operations: 13.4 us -> 0.07 us
  matrix products: 7.7 us -> 0 us
    psum x3 -> x0, blocking collectives: 159 us -> none  [the longest x1 59.4 us: local(): column_total = lax.psum(column_part, 'line')]
    scatter-add x1 -> x0, other arithmetic: 91.3 us -> none  [local(): jnp.zeros((hours, total_lines), jnp.float32).at[:, outage_lines]]
    unnamed x2 -> x0, waiting for transfers between devices: 91 us -> none
    all_gather x2 -> x0, blocking collectives: 69.5 us -> none  [the longest x1 39.6 us: local(): flows = lax.all_gather(flow_rows, 'line', axis=1, tiled=True)]
    ppermute x0 -> x20, starting transfers between devices: none -> 56.7 us  [partner_sum(): return x + lax.ppermute(x, axis, list(enumerate(partners)))]
    pallas_call x0 -> x6, Pallas kernels: none -> 35.8 us  [call(): pl.pallas_call(kernel, out_shape=out_shape, in_specs=[VMEM] * len(operand...]
    ppermute x0 -> x20, waiting for transfers between devices: none -> 29.8 us  [partner_sum(): return x + lax.ppermute(x, axis, list(enumerate(partners)))]
    reduce_sum x4 -> x0, other arithmetic: 24.9 us -> none  [advance(): row_total = jnp.sum(slope, axis=2)]
  transfers between devices with their start and end apart: 1 -> 20, of which waited for: 1 -> 20; matrix products, arithmetic and copies ran while one was open for 0% -> 1% of each run, Pallas kernels for 0% -> 1%
where the time goes in v1:
time: 129 us
  starting transfers between devices  56.7 us (44%)
  Pallas kernels  35.8 us (28%)
  waiting for transfers between devices  29.8 us (23%)
  local copies, waits for them, and re-layouts  5.18 us (4%)
  other arithmetic  1.45 us (1%)
    ppermute x20, starting transfers between devices, partner_sum(): return x + lax.ppermute(x, axis, list(enumerate(partners)))  56.7 us
    pallas_call x6, Pallas kernels, call(): pl.pallas_call(kernel, out_shape=out_shape, in_specs=[VMEM] * len(operand...  35.8 us
    ppermute x20, waiting for transfers between devices, partner_sum(): return x + lax.ppermute(x, axis, list(enumerate(partners)))  29.8 us
    unnamed x10, local copies, waits for them, and re-layouts  5.18 us
  transfers between devices with their start and end apart: 20, of which 20 were waited for; matrix products, arithmetic and copies ran while one was open for 1% of the time, Pallas kernels for 1%

profile of v1, /device:TPU:33, one launch (start us, length us, event | category | flops | bytes accessed | tf_op | source)
XLA Modules:
  0.0 129.1 jit_solution(18328764364822310275)
XLA Ops:
  0.0 1.6 %copy-done = f32[1024,512]{1,0:T(8,128)S(1)} copy-done((f32[1024,512]{1,0:T(8,128)S(1)}, f32[1024,512]{1,0:T(8,128)}, u32[]{:S(2)}) %copy-start) | copy-done | bytes 2097176
  2.3 1.7 %shard_map.55 = f32[8,1024]{1,0:T(8,128)S(1)} custom-call(f32[8,512]{1,0:T(8,128)S(1)} %copy-done.3, f32[1024,512]{1,0:T(8,128)S(1)} %copy-done), custom_call_target="tpu_custom_call" | custom-call | bytes 2113536 | tf_op jit(solution)/shard_map/pallas_call | solution.py:145
  5.3 1.6 %collective-permute-done = f32[8,1024]{1,0:T(8,128)S(1)} collective-permute-done((f32[8,1024]{1,0:T(8,128)S(1)}, f32[8,1024]{1,0:T(8,128)S(1)}, u32[]{:S(2)}, u32[]{:S(2)}) %collective-permute-start) | collective-permute-done | bytes 32800 | tf_op jit(solution)/shard_map/ppermute | solution.py:158
  6.8 2.8 %collective-permute-done.1 = f32[8,1024]{1,0:T(8,128)S(1)} collective-permute-done((f32[8,1024]{1,0:T(8,128)S(1)}, f32[8,1024]{1,0:T(8,128)S(1)}, u32[]{:S(2)}, u32[]{:S(2)}) %collective-permute-start.1) | collective-permute-done | bytes 32800 | tf_op jit(solution)/shard_map/ppermute | solution.py:158
  9.6 3.0 %collective-permute-start.2 = (f32[8,1024]{1,0:T(8,128)S(1)}, f32[8,1024]{1,0:T(8,128)S(1)}, u32[]{:S(2)}, u32[]{:S(2)}) collective-permute-start(f32[8,1024]{1,0:T(8,128)S(1)} %add.67), channel_id=1, source_target_pairs={{0,2},{1,3},{2,0},{3,1},{4,6},{5,7},{6,4},{7,5},{8,10},{9,11},{10,... | collective-permute-start | bytes 98312 | tf_op jit(solution)/shard_map/ppermute | solution.py:158
  12.6 1.3 %collective-permute-done.2 = f32[8,1024]{1,0:T(8,128)S(1)} collective-permute-done((f32[8,1024]{1,0:T(8,128)S(1)}, f32[8,1024]{1,0:T(8,128)S(1)}, u32[]{:S(2)}, u32[]{:S(2)}) %collective-permute-start.2) | collective-permute-done | bytes 32800 | tf_op jit(solution)/shard_map/ppermute | solution.py:158
  13.9 4.9 %collective-permute-start.3 = (f32[8,1024]{1,0:T(8,128)S(1)}, f32[8,1024]{1,0:T(8,128)S(1)}, u32[]{:S(2)}, u32[]{:S(2)}) collective-permute-start(f32[8,1024]{1,0:T(8,128)S(1)} %add.68), channel_id=1, source_target_pairs={{0,7},{1,6},{2,5},{3,4},{4,3},{5,2},{6,1},{7,0},{8,15},{9,14},{10,... | collective-permute-start | bytes 98312 | tf_op jit(solution)/shard_map/ppermute | solution.py:158
  20.3 2.8 %collective-permute-start.4 = (f32[8,1024]{1,0:T(8,128)S(1)}, f32[8,1024]{1,0:T(8,128)S(1)}, u32[]{:S(2)}, u32[]{:S(2)}) collective-permute-start(f32[8,1024]{1,0:T(8,128)S(1)} %shard_map.56), channel_id=1, source_target_pairs={{0,128},{16,144},{32,160},{48,176},{64,192},{80,208},{96,224},{112... | collective-permute-start | bytes 98312 | tf_op jit(solution)/shard_map/ppermute | solution.py:158
  23.1 1.6 %collective-permute-done.4 = f32[8,1024]{1,0:T(8,128)S(1)} collective-permute-done((f32[8,1024]{1,0:T(8,128)S(1)}, f32[8,1024]{1,0:T(8,128)S(1)}, u32[]{:S(2)}, u32[]{:S(2)}) %collective-permute-start.4) | collective-permute-done | bytes 32800 | tf_op jit(solution)/shard_map/ppermute | solution.py:158
  24.7 2.9 %collective-permute-start.5 = (f32[8,1024]{1,0:T(8,128)S(1)}, f32[8,1024]{1,0:T(8,128)S(1)}, u32[]{:S(2)}, u32[]{:S(2)}) collective-permute-start(f32[8,1024]{1,0:T(8,128)S(1)} %add.71), channel_id=1, source_target_pairs={{0,64},{16,80},{32,96},{48,112},{64,0},{80,16},{96,32},{112,48},{1... | collective-permute-start | bytes 98312 | tf_op jit(solution)/shard_map/ppermute | solution.py:158
  27.7 1.4 %collective-permute-done.5 = f32[8,1024]{1,0:T(8,128)S(1)} collective-permute-done((f32[8,1024]{1,0:T(8,128)S(1)}, f32[8,1024]{1,0:T(8,128)S(1)}, u32[]{:S(2)}, u32[]{:S(2)}) %collective-permute-start.5) | collective-permute-done | bytes 32800 | tf_op jit(solution)/shard_map/ppermute | solution.py:158
  29.0 1.3 %collective-permute-start.6 = (f32[8,1024]{1,0:T(8,128)S(1)}, f32[8,1024]{1,0:T(8,128)S(1)}, u32[]{:S(2)}, u32[]{:S(2)}) collective-permute-start(f32[8,1024]{1,0:T(8,128)S(1)} %add.72), channel_id=1, source_target_pairs={{0,32},{16,48},{32,0},{48,16},{64,96},{80,112},{96,64},{112,80},{1... | collective-permute-start | bytes 98312 | tf_op jit(solution)/shard_map/ppermute | solution.py:158
  30.3 1.5 %collective-permute-done.6 = f32[8,1024]{1,0:T(8,128)S(1)} collective-permute-done((f32[8,1024]{1,0:T(8,128)S(1)}, f32[8,1024]{1,0:T(8,128)S(1)}, u32[]{:S(2)}, u32[]{:S(2)}) %collective-permute-start.6) | collective-permute-done | bytes 32800 | tf_op jit(solution)/shard_map/ppermute | solution.py:158
  31.8 8.4 %collective-permute-start.7 = (f32[8,1024]{1,0:T(8,128)S(1)}, f32[8,1024]{1,0:T(8,128)S(1)}, u32[]{:S(2)}, u32[]{:S(2)}) collective-permute-start(f32[8,1024]{1,0:T(8,128)S(1)} %add.73), channel_id=1, source_target_pairs={{0,16},{16,0},{32,48},{48,32},{64,80},{80,64},{96,112},{112,96},{1... | collective-permute-start | bytes 98312 | tf_op jit(solution)/shard_map/ppermute | solution.py:158
  41.0 2.2 %copy-done.2 = f32[1024,1024]{1,0:T(8,128)S(1)} copy-done((f32[1024,1024]{1,0:T(8,128)S(1)}, f32[1024,1024]{1,0:T(8,128)}, u32[]{:S(2)}) %copy-start.2) | copy-done | bytes 4194328
  43.9 32.1 %shard_map.57 = (f32[8,1024]{1,0:T(8,128)S(1)}, f32[8,1024]{1,0:T(8,128)S(1)}) custom-call(f32[1024,1024]{1,0:T(8,128)S(1)} %copy-done.2, f32[8,1024]{1,0:T(8,128)S(1)} %add.69.values_ref.flow_ref, f32[8,1024]{1,0:T(8,128)S(1)} %add.74.out_flow_ref, f32[1,1024]{1,0:T(1,128)S(1)} %bitcast.4), custom_call_target="tpu_custom_call" | custom-call | bytes 4263936 | tf_op jit(solution)/shard_map/pallas_call | solution.py:145
  76.0 2.8 %collective-permute-start.8 = (f32[8,1024]{1,0:T(8,128)S(1)}, f32[8,1024]{1,0:T(8,128)S(1)}, u32[]{:S(2)}, u32[]{:S(2)}) collective-permute-start(f32[8,1024]{1,0:T(8,128)S(1)} %get-tuple-element.7), channel_id=1, source_target_pairs={{0,128},{16,144},{32,160},{48,176},{64,192},{80,208},{96,224},{112... | collective-permute-start | bytes 98312 | tf_op jit(solution)/shard_map/ppermute | solution.py:158
  78.8 1.5 %collective-permute-done.8 = f32[8,1024]{1,0:T(8,128)S(1)} collective-permute-done((f32[8,1024]{1,0:T(8,128)S(1)}, f32[8,1024]{1,0:T(8,128)S(1)}, u32[]{:S(2)}, u32[]{:S(2)}) %collective-permute-start.8) | collective-permute-done | bytes 32800 | tf_op jit(solution)/shard_map/ppermute | solution.py:158
  80.4 2.9 %collective-permute-start.9 = (f32[8,1024]{1,0:T(8,128)S(1)}, f32[8,1024]{1,0:T(8,128)S(1)}, u32[]{:S(2)}, u32[]{:S(2)}) collective-permute-start(f32[8,1024]{1,0:T(8,128)S(1)} %add.75), channel_id=1, source_target_pairs={{0,64},{16,80},{32,96},{48,112},{64,0},{80,16},{96,32},{112,48},{1... | collective-permute-start | bytes 98312 | tf_op jit(solution)/shard_map/ppermute | solution.py:158
  83.3 1.4 %collective-permute-done.9 = f32[8,1024]{1,0:T(8,128)S(1)} collective-permute-done((f32[8,1024]{1,0:T(8,128)S(1)}, f32[8,1024]{1,0:T(8,128)S(1)}, u32[]{:S(2)}, u32[]{:S(2)}) %collective-permute-start.9) | collective-permute-done | bytes 32800 | tf_op jit(solution)/shard_map/ppermute | solution.py:158
  85.9 1.5 %collective-permute-done.10 = f32[8,1024]{1,0:T(8,128)S(1)} collective-permute-done((f32[8,1024]{1,0:T(8,128)S(1)}, f32[8,1024]{1,0:T(8,128)S(1)}, u32[]{:S(2)}, u32[]{:S(2)}) %collective-permute-start.10) | collective-permute-done | bytes 32800 | tf_op jit(solution)/shard_map/ppermute | solution.py:158
  87.4 3.8 %collective-permute-start.11 = (f32[8,1024]{1,0:T(8,128)S(1)}, f32[8,1024]{1,0:T(8,128)S(1)}, u32[]{:S(2)}, u32[]{:S(2)}) collective-permute-start(f32[8,1024]{1,0:T(8,128)S(1)} %add.77), channel_id=1, source_target_pairs={{0,16},{16,0},{32,48},{48,32},{64,80},{80,64},{96,112},{112,96},{1... | collective-permute-start | bytes 98312 | tf_op jit(solution)/shard_map/ppermute | solution.py:158
  92.3 1.3 %collective-permute-start.12 = (f32[8,1024]{1,0:T(8,128)S(1)}, f32[8,1024]{1,0:T(8,128)S(1)}, u32[]{:S(2)}, u32[]{:S(2)}) collective-permute-start(f32[8,1024]{1,0:T(8,128)S(1)} %shard_map.59), channel_id=1, source_target_pairs={{0,8},{1,9},{2,10},{3,11},{4,12},{5,13},{6,14},{7,15},{8,0},{9,1},... | collective-permute-start | bytes 98312 | tf_op jit(solution)/shard_map/ppermute | solution.py:158
  93.6 1.6 %collective-permute-done.12 = f32[8,1024]{1,0:T(8,128)S(1)} collective-permute-done((f32[8,1024]{1,0:T(8,128)S(1)}, f32[8,1024]{1,0:T(8,128)S(1)}, u32[]{:S(2)}, u32[]{:S(2)}) %collective-permute-start.12) | collective-permute-done | bytes 32800 | tf_op jit(solution)/shard_map/ppermute | solution.py:158
  95.1 2.8 %collective-permute-done.13 = f32[8,1024]{1,0:T(8,128)S(1)} collective-permute-done((f32[8,1024]{1,0:T(8,128)S(1)}, f32[8,1024]{1,0:T(8,128)S(1)}, u32[]{:S(2)}, u32[]{:S(2)}) %collective-permute-start.13) | collective-permute-done | bytes 32800 | tf_op jit(solution)/shard_map/ppermute | solution.py:158
  98.4 3.1 %collective-permute-done.14 = f32[8,1024]{1,0:T(8,128)S(1)} collective-permute-done((f32[8,1024]{1,0:T(8,128)S(1)}, f32[8,1024]{1,0:T(8,128)S(1)}, u32[]{:S(2)}, u32[]{:S(2)}) %collective-permute-start.14) | collective-permute-done | bytes 32800 | tf_op jit(solution)/shard_map/ppermute | solution.py:158
  101.6 4.8 %collective-permute-start.15 = (f32[8,1024]{1,0:T(8,128)S(1)}, f32[8,1024]{1,0:T(8,128)S(1)}, u32[]{:S(2)}, u32[]{:S(2)}) collective-permute-start(f32[8,1024]{1,0:T(8,128)S(1)} %add.81), channel_id=1, source_target_pairs={{0,7},{1,6},{2,5},{3,4},{4,3},{5,2},{6,1},{7,0},{8,15},{9,14},{10,... | collective-permute-start | bytes 98312 | tf_op jit(solution)/shard_map/ppermute | solution.py:158
  106.3 1.7 %collective-permute-done.15 = f32[8,1024]{1,0:T(8,128)S(1)} collective-permute-done((f32[8,1024]{1,0:T(8,128)S(1)}, f32[8,1024]{1,0:T(8,128)S(1)}, u32[]{:S(2)}, u32[]{:S(2)}) %collective-permute-start.15) | collective-permute-done | bytes 32800 | tf_op jit(solution)/shard_map/ppermute | solution.py:158
  109.0 2.8 %collective-permute-start.16 = (f32[8,512]{1,0:T(8,128)S(1)}, f32[8,512]{1,0:T(8,128)S(1)}, u32[]{:S(2)}, u32[]{:S(2)}) collective-permute-start(f32[8,512]{1,0:T(8,128)S(1)} %shard_map.60), channel_id=1, source_target_pairs={{0,128},{16,144},{32,160},{48,176},{64,192},{80,208},{96,224},{112... | collective-permute-start | bytes 49160 | tf_op jit(solution)/shard_map/ppermute | solution.py:158
  111.7 1.3 %collective-permute-done.16 = f32[8,512]{1,0:T(8,128)S(1)} collective-permute-done((f32[8,512]{1,0:T(8,128)S(1)}, f32[8,512]{1,0:T(8,128)S(1)}, u32[]{:S(2)}, u32[]{:S(2)}) %collective-permute-start.16) | collective-permute-done | bytes 16416 | tf_op jit(solution)/shard_map/ppermute | solution.py:158
  113.1 2.9 %collective-permute-start.17 = (f32[8,512]{1,0:T(8,128)S(1)}, f32[8,512]{1,0:T(8,128)S(1)}, u32[]{:S(2)}, u32[]{:S(2)}) collective-permute-start(f32[8,512]{1,0:T(8,128)S(1)} %add.83), channel_id=1, source_target_pairs={{0,64},{16,80},{32,96},{48,112},{64,0},{80,16},{96,32},{112,48},{1... | collective-permute-start | bytes 49160 | tf_op jit(solution)/shard_map/ppermute | solution.py:158
  119.8 7.8 %collective-permute-start.19 = (f32[8,512]{1,0:T(8,128)S(1)}, f32[8,512]{1,0:T(8,128)S(1)}, u32[]{:S(2)}, u32[]{:S(2)}) collective-permute-start(f32[8,512]{1,0:T(8,128)S(1)} %add.85), channel_id=1, source_target_pairs={{0,16},{16,0},{32,48},{48,32},{64,80},{80,64},{96,112},{112,96},{1... | collective-permute-start | bytes 49160 | tf_op jit(solution)/shard_map/ppermute | solution.py:158
  (45 shorter events, 14.2 us)
Async XLA Ops:
  0.0 1.6 %copy-start = (f32[1024,512]{1,0:T(8,128)S(1)}, f32[1024,512]{1,0:T(8,128)}, u32[]{:S(2)}) copy-start(f32[1024,512]{1,0:T(8,128)} %factors_ref.5) | copy-start | bytes 6291460
  1.6 0.7 copy-start.3
  2.3 105.7 %copy-start.1 = (f32[1024,512]{1,0:T(8,128)S(1)}, f32[1024,512]{1,0:T(8,128)}, u32[]{:S(2)}) copy-start(f32[1024,512]{1,0:T(8,128)} %factors_ref.5) | copy-start | bytes 6291460
  4.0 2.8 %collective-permute-start = (f32[8,1024]{1,0:T(8,128)S(1)}, f32[8,1024]{1,0:T(8,128)S(1)}, u32[]{:S(2)}, u32[]{:S(2)}) collective-permute-start(f32[8,1024]{1,0:T(8,128)S(1)} %shard_map.55), channel_id=1, source_target_pairs={{0,8},{1,9},{2,10},{3,11},{4,12},{5,13},{6,14},{7,15},{8,0},{9,1},... | collective-permute-start | bytes 98312 | tf_op jit(solution)/shard_map/ppermute | solution.py:158
  6.8 2.8 %collective-permute-start.1 = (f32[8,1024]{1,0:T(8,128)S(1)}, f32[8,1024]{1,0:T(8,128)S(1)}, u32[]{:S(2)}, u32[]{:S(2)}) collective-permute-start(f32[8,1024]{1,0:T(8,128)S(1)} %add.66), channel_id=1, source_target_pairs={{0,1},{1,0},{2,3},{3,2},{4,5},{5,4},{6,7},{7,6},{8,9},{9,8},{10,11... | collective-permute-start | bytes 98312 | tf_op jit(solution)/shard_map/ppermute | solution.py:158
  9.6 4.3 %collective-permute-start.2 = (f32[8,1024]{1,0:T(8,128)S(1)}, f32[8,1024]{1,0:T(8,128)S(1)}, u32[]{:S(2)}, u32[]{:S(2)}) collective-permute-start(f32[8,1024]{1,0:T(8,128)S(1)} %add.67), channel_id=1, source_target_pairs={{0,2},{1,3},{2,0},{3,1},{4,6},{5,7},{6,4},{7,5},{8,10},{9,11},{10,... | collective-permute-start | bytes 98312 | tf_op jit(solution)/shard_map/ppermute | solution.py:158
  13.9 6.2 %collective-permute-start.3 = (f32[8,1024]{1,0:T(8,128)S(1)}, f32[8,1024]{1,0:T(8,128)S(1)}, u32[]{:S(2)}, u32[]{:S(2)}) collective-permute-start(f32[8,1024]{1,0:T(8,128)S(1)} %add.68), channel_id=1, source_target_pairs={{0,7},{1,6},{2,5},{3,4},{4,3},{5,2},{6,1},{7,0},{8,15},{9,14},{10,... | collective-permute-start | bytes 98312 | tf_op jit(solution)/shard_map/ppermute | solution.py:158
  20.3 4.4 %collective-permute-start.4 = (f32[8,1024]{1,0:T(8,128)S(1)}, f32[8,1024]{1,0:T(8,128)S(1)}, u32[]{:S(2)}, u32[]{:S(2)}) collective-permute-start(f32[8,1024]{1,0:T(8,128)S(1)} %shard_map.56), channel_id=1, source_target_pairs={{0,128},{16,144},{32,160},{48,176},{64,192},{80,208},{96,224},{112... | collective-permute-start | bytes 98312 | tf_op jit(solution)/shard_map/ppermute | solution.py:158
  24.7 4.3 %collective-permute-start.5 = (f32[8,1024]{1,0:T(8,128)S(1)}, f32[8,1024]{1,0:T(8,128)S(1)}, u32[]{:S(2)}, u32[]{:S(2)}) collective-permute-start(f32[8,1024]{1,0:T(8,128)S(1)} %add.71), channel_id=1, source_target_pairs={{0,64},{16,80},{32,96},{48,112},{64,0},{80,16},{96,32},{112,48},{1... | collective-permute-start | bytes 98312 | tf_op jit(solution)/shard_map/ppermute | solution.py:158
  29.0 2.8 %collective-permute-start.6 = (f32[8,1024]{1,0:T(8,128)S(1)}, f32[8,1024]{1,0:T(8,128)S(1)}, u32[]{:S(2)}, u32[]{:S(2)}) collective-permute-start(f32[8,1024]{1,0:T(8,128)S(1)} %add.72), channel_id=1, source_target_pairs={{0,32},{16,48},{32,0},{48,16},{64,96},{80,112},{96,64},{112,80},{1... | collective-permute-start | bytes 98312 | tf_op jit(solution)/shard_map/ppermute | solution.py:158
  31.8 9.2 %collective-permute-start.7 = (f32[8,1024]{1,0:T(8,128)S(1)}, f32[8,1024]{1,0:T(8,128)S(1)}, u32[]{:S(2)}, u32[]{:S(2)}) collective-permute-start(f32[8,1024]{1,0:T(8,128)S(1)} %add.73), channel_id=1, source_target_pairs={{0,16},{16,0},{32,48},{48,32},{64,80},{80,64},{96,112},{112,96},{1... | collective-permute-start | bytes 98312 | tf_op jit(solution)/shard_map/ppermute | solution.py:158
  41.0 2.2 %copy-start.2 = (f32[1024,1024]{1,0:T(8,128)S(1)}, f32[1024,1024]{1,0:T(8,128)}, u32[]{:S(2)}) copy-start(f32[1024,1024]{1,0:T(8,128)} %factors_ref.4) | copy-start | bytes 12582916
  43.2 0.7 copy-start.4
  76.0 4.3 %collective-permute-start.8 = (f32[8,1024]{1,0:T(8,128)S(1)}, f32[8,1024]{1,0:T(8,128)S(1)}, u32[]{:S(2)}, u32[]{:S(2)}) collective-permute-start(f32[8,1024]{1,0:T(8,128)S(1)} %get-tuple-element.7), channel_id=1, source_target_pairs={{0,128},{16,144},{32,160},{48,176},{64,192},{80,208},{96,224},{112... | collective-permute-start | bytes 98312 | tf_op jit(solution)/shard_map/ppermute | solution.py:158
  80.4 4.3 %collective-permute-start.9 = (f32[8,1024]{1,0:T(8,128)S(1)}, f32[8,1024]{1,0:T(8,128)S(1)}, u32[]{:S(2)}, u32[]{:S(2)}) collective-permute-start(f32[8,1024]{1,0:T(8,128)S(1)} %add.75), channel_id=1, source_target_pairs={{0,64},{16,80},{32,96},{48,112},{64,0},{80,16},{96,32},{112,48},{1... | collective-permute-start | bytes 98312 | tf_op jit(solution)/shard_map/ppermute | solution.py:158
  84.6 2.8 %collective-permute-start.10 = (f32[8,1024]{1,0:T(8,128)S(1)}, f32[8,1024]{1,0:T(8,128)S(1)}, u32[]{:S(2)}, u32[]{:S(2)}) collective-permute-start(f32[8,1024]{1,0:T(8,128)S(1)} %add.76), channel_id=1, source_target_pairs={{0,32},{16,48},{32,0},{48,16},{64,96},{80,112},{96,64},{112,80},{1... | collective-permute-start | bytes 98312 | tf_op jit(solution)/shard_map/ppermute | solution.py:158
  87.4 4.7 %collective-permute-start.11 = (f32[8,1024]{1,0:T(8,128)S(1)}, f32[8,1024]{1,0:T(8,128)S(1)}, u32[]{:S(2)}, u32[]{:S(2)}) collective-permute-start(f32[8,1024]{1,0:T(8,128)S(1)} %add.77), channel_id=1, source_target_pairs={{0,16},{16,0},{32,48},{48,32},{64,80},{80,64},{96,112},{112,96},{1... | collective-permute-start | bytes 98312 | tf_op jit(solution)/shard_map/ppermute | solution.py:158
  92.3 2.9 %collective-permute-start.12 = (f32[8,1024]{1,0:T(8,128)S(1)}, f32[8,1024]{1,0:T(8,128)S(1)}, u32[]{:S(2)}, u32[]{:S(2)}) collective-permute-start(f32[8,1024]{1,0:T(8,128)S(1)} %shard_map.59), channel_id=1, source_target_pairs={{0,8},{1,9},{2,10},{3,11},{4,12},{5,13},{6,14},{7,15},{8,0},{9,1},... | collective-permute-start | bytes 98312 | tf_op jit(solution)/shard_map/ppermute | solution.py:158
  95.1 2.8 %collective-permute-start.13 = (f32[8,1024]{1,0:T(8,128)S(1)}, f32[8,1024]{1,0:T(8,128)S(1)}, u32[]{:S(2)}, u32[]{:S(2)}) collective-permute-start(f32[8,1024]{1,0:T(8,128)S(1)} %add.79), channel_id=1, source_target_pairs={{0,1},{1,0},{2,3},{3,2},{4,5},{5,4},{6,7},{7,6},{8,9},{9,8},{10,11... | collective-permute-start | bytes 98312 | tf_op jit(solution)/shard_map/ppermute | solution.py:158
  97.9 3.7 %collective-permute-start.14 = (f32[8,1024]{1,0:T(8,128)S(1)}, f32[8,1024]{1,0:T(8,128)S(1)}, u32[]{:S(2)}, u32[]{:S(2)}) collective-permute-start(f32[8,1024]{1,0:T(8,128)S(1)} %add.80), channel_id=1, source_target_pairs={{0,2},{1,3},{2,0},{3,1},{4,6},{5,7},{6,4},{7,5},{8,10},{9,11},{10,... | collective-permute-start | bytes 98312 | tf_op jit(solution)/shard_map/ppermute | solution.py:158
  101.6 6.4 %collective-permute-start.15 = (f32[8,1024]{1,0:T(8,128)S(1)}, f32[8,1024]{1,0:T(8,128)S(1)}, u32[]{:S(2)}, u32[]{:S(2)}) collective-permute-start(f32[8,1024]{1,0:T(8,128)S(1)} %add.81), channel_id=1, source_target_pairs={{0,7},{1,6},{2,5},{3,4},{4,3},{5,2},{6,1},{7,0},{8,15},{9,14},{10,... | collective-permute-start | bytes 98312 | tf_op jit(solution)/shard_map/ppermute | solution.py:158
  109.0 4.1 %collective-permute-start.16 = (f32[8,512]{1,0:T(8,128)S(1)}, f32[8,512]{1,0:T(8,128)S(1)}, u32[]{:S(2)}, u32[]{:S(2)}) collective-permute-start(f32[8,512]{1,0:T(8,128)S(1)} %shard_map.60), channel_id=1, source_target_pairs={{0,128},{16,144},{32,160},{48,176},{64,192},{80,208},{96,224},{112... | collective-permute-start | bytes 49160 | tf_op jit(solution)/shard_map/ppermute | solution.py:158
  113.1 4.1 %collective-permute-start.17 = (f32[8,512]{1,0:T(8,128)S(1)}, f32[8,512]{1,0:T(8,128)S(1)}, u32[]{:S(2)}, u32[]{:S(2)}) collective-permute-start(f32[8,512]{1,0:T(8,128)S(1)} %add.83), channel_id=1, source_target_pairs={{0,64},{16,80},{32,96},{48,112},{64,0},{80,16},{96,32},{112,48},{1... | collective-permute-start | bytes 49160 | tf_op jit(solution)/shard_map/ppermute | solution.py:158
  117.2 2.6 %collective-permute-start.18 = (f32[8,512]{1,0:T(8,128)S(1)}, f32[8,512]{1,0:T(8,128)S(1)}, u32[]{:S(2)}, u32[]{:S(2)}) collective-permute-start(f32[8,512]{1,0:T(8,128)S(1)} %add.84), channel_id=1, source_target_pairs={{0,32},{16,48},{32,0},{48,16},{64,96},{80,112},{96,64},{112,80},{1... | collective-permute-start | bytes 49160 | tf_op jit(solution)/shard_map/ppermute | solution.py:158
  119.8 8.6 %collective-permute-start.19 = (f32[8,512]{1,0:T(8,128)S(1)}, f32[8,512]{1,0:T(8,128)S(1)}, u32[]{:S(2)}, u32[]{:S(2)}) collective-permute-start(f32[8,512]{1,0:T(8,128)S(1)} %add.85), channel_id=1, source_target_pairs={{0,16},{16,0},{32,48},{48,32},{64,80},{80,64},{96,112},{112,96},{1... | collective-permute-start | bytes 49160 | tf_op jit(solution)/shard_map/ppermute | solution.py:158

commit v2 on v1

v2 whole, which is shorter than its diff:
```python
import functools

import jax
import jax.numpy as jnp
from jax import lax
from jax.experimental import pallas as pl
from jax.experimental.pallas import tpu as pltpu
from jax.sharding import PartitionSpec as P

OUTAGES = 16384
SOFTNESS = 0.25
LANES = 128
SUB = 8
TILES = 4
CHUNKS = 8
VMEM = pl.BlockSpec(memory_space=pltpu.VMEM)
FAR = pl.BlockSpec(memory_space=pltpu.HBM)


def params(mib):
    return pltpu.CompilerParams(vmem_limit_bytes=mib * 1024 * 1024)


def thirds(x):
    high = x.astype(jnp.bfloat16)
    rest = x - high.astype(jnp.float32)
    middle = rest.astype(jnp.bfloat16)
    return high, middle, (rest - middle.astype(jnp.float32)).astype(jnp.bfloat16)


def stacked(x):
    parts = [part.astype(jnp.float32) for part in thirds(x)]
    return jnp.concatenate(parts + [jnp.zeros_like(x)], axis=0).astype(jnp.bfloat16)


def product(parts, right, dims):
    first, second, third = (
        lax.dot_general(parts, part, dims, preferred_element_type=jnp.float32) for part in thirds(right)
    )
    h = parts.shape[0] // 4
    small = first[2 * h : 3 * h] + second[h : 2 * h] + third[:h]
    return (small + (first[h : 2 * h] + second[:h])) + first[:h]


def flows_kernel(injections_hbm, factors_hbm, out_ref, injections, factors, sems):
    chunks = sems.shape[0] - 1
    rows = factors.shape[0] // chunks
    first = pltpu.make_async_copy(injections_hbm, injections, sems.at[chunks])
    first.start()
    copies = []
    for c in range(chunks):
        here = pl.ds(c * rows, rows)
        copies.append(pltpu.make_async_copy(factors_hbm.at[here, :], factors.at[here, :], sems.at[c]))
        copies[c].start()
    first.wait()
    parts = stacked(injections[...])
    for c in range(chunks):
        copies[c].wait()
        here = slice(c * rows, (c + 1) * rows)
        out_ref[:, here] = product(parts, factors[here, :], (((1,), (1,)), ((), ())))


def bus_kernel(slopes_ref, factors_ref, out_ref):
    out_ref[...] = product(stacked(slopes_ref[...]), factors_ref[...], (((1,), (0,)), ((), ())))


def inverse_kernel(index_ref, out_ref):
    width = index_ref.shape[1]
    lane = lax.broadcasted_iota(jnp.int32, (LANES, LANES), 1)
    row = lax.broadcasted_iota(jnp.int32, (LANES, LANES), 0)
    totals = [jnp.zeros((1, LANES), jnp.int32) for _ in range(out_ref.shape[1] // LANES)]
    for kb in range(width // LANES):
        piece = index_ref[:, kb * LANES : (kb + 1) * LANES].astype(jnp.float32)
        column = jnp.transpose(jnp.broadcast_to(piece, (LANES, LANES))).astype(jnp.int32)
        for lb in range(len(totals)):
            hit = jnp.where(column == lane + lb * LANES, row + (kb * LANES + 1), 0)
            totals[lb] = totals[lb] + jnp.sum(hit, axis=0, keepdims=True)
    for lb, total in enumerate(totals):
        out_ref[:, lb * LANES : (lb + 1) * LANES] = total - 1


def pick(values_ref, index_ref, kb):
    hours, width = values_ref.shape
    index = jnp.broadcast_to(index_ref[:, kb * LANES : (kb + 1) * LANES], (hours, LANES))
    low = jnp.bitwise_and(index, LANES - 1)
    high = jnp.right_shift(index, 7)
    result = jnp.zeros((hours, LANES), jnp.float32)
    for q in range(width // LANES):
        found = jnp.take_along_axis(values_ref[:, q * LANES : (q + 1) * LANES], low, axis=1)
        result = jnp.where(high == q, found, result)
    return result


def select_kernel(values_ref, index_ref, out_ref):
    for kb in range(out_ref.shape[1] // LANES):
        out_ref[:, kb * LANES : (kb + 1) * LANES] = pick(values_ref, index_ref, kb)


def place_kernel(values_ref, index_ref, rows_ref, out_ref):
    for kb in range(out_ref.shape[1] // LANES):
        here = slice(kb * LANES, (kb + 1) * LANES)
        out_ref[:, here] = pick(values_ref, index_ref, kb) + rows_ref[:, here]


def spread_kernel(flow_ref, out_ref):
    hours, rows = flow_ref.shape
    for h in range(hours):
        for lb in range(rows // LANES):
            here = slice(lb * LANES, (lb + 1) * LANES)
            flow = (0.5 / SOFTNESS) * flow_ref[h : h + 1, here]
            out_ref[h, here, :] = jnp.transpose(jnp.broadcast_to(flow, (LANES, LANES)))


def overload_kernel(
    factors_hbm, flow_ref, limit_ref, out_flow_ref, sums_ref, column_ref, factors, sems, wide, total
):
    rows, width = factors.shape
    hours = flow_ref.shape[0]
    blocks = width // LANES
    chunks = sems.shape[0]
    chunk_rows = rows // chunks
    parts = range(TILES)
    tile = TILES * SUB

    def copy(c):
        here = pl.ds(pl.multiple_of(c * chunk_rows, chunk_rows), chunk_rows)
        return pltpu.make_async_copy(factors_hbm.at[here, :], factors.at[here, :], sems.at[c])

    for c in range(chunks):
        copy(c).start()
    for h in range(hours):
        for kb in range(blocks):
            piece = (0.5 / SOFTNESS) * out_flow_ref[h : h + 1, kb * LANES : (kb + 1) * LANES]
            wide[h * blocks + kb] = jnp.broadcast_to(piece, (SUB, LANES))
    total[...] = jnp.zeros_like(total)

    def advance(start):
        at = [pl.ds(start + r * SUB, SUB) for r in parts]
        limit = [limit_ref[at[r], :] for r in parts]
        for h in range(hours):
            flow = [flow_ref[h, at[r], :] for r in parts]
            plus = [flow[r] + limit[r] for r in parts]
            minus = [flow[r] - limit[r] for r in parts]
            across = [None for r in parts]
            for kb in range(blocks):
                out_flow = wide[h * blocks + kb]
                gathered = None
                for r in parts:
                    factor = factors[at[r], kb * LANES : (kb + 1) * LANES]
                    moved = factor * out_flow
                    slope = jnp.tanh(moved + plus[r]) + jnp.tanh(moved + minus[r])
                    across[r] = slope if across[r] is None else across[r] + slope
                    weighted = slope * factor
                    gathered = weighted if gathered is None else gathered + weighted
                total[h * blocks + kb] = total[h * blocks + kb] + gathered
            for r in parts:
                sums_ref[h, at[r], :] = across[r]

    def chunk(c, carry):
        copy(c).wait()

        def step(s, inner):
            advance(pl.multiple_of(c * chunk_rows + s * tile, tile))
            return inner

        return lax.fori_loop(0, chunk_rows // tile, step, carry)

    lax.fori_loop(0, chunks, chunk, 0)
    for h in range(hours):
        for kb in range(blocks):
            column_ref[h : h + 1, kb * LANES : (kb + 1) * LANES] = (0.5 / OUTAGES) * jnp.sum(
                total[h * blocks + kb], axis=0, keepdims=True
            )


def row_kernel(sums_ref, out_ref):
    hours, rows = out_ref.shape
    for lb in range(rows // LANES):
        here = slice(lb * LANES, (lb + 1) * LANES)
        for h in range(hours):
            out_ref[h : h + 1, here] = (0.5 / OUTAGES) * jnp.sum(
                jnp.transpose(sums_ref[h, here, :]), axis=0, keepdims=True
            )


def call(kernel, shape, *operands, dtype=jnp.float32, mib=8, far=0, scratch=()):
    size = sum(a.size * 4 for a in operands)
    out_shape = [jax.ShapeDtypeStruct(s, dtype) for s in shape]
    result = pl.pallas_call(
        kernel,
        out_shape=out_shape,
        in_specs=[FAR] * far + [VMEM] * (len(operands) - far),
        out_specs=[VMEM] * len(shape),
        scratch_shapes=list(scratch),
        compiler_params=params(mib),
        cost_estimate=pl.CostEstimate(flops=0, bytes_accessed=size, transcendentals=0),
        name=kernel.__name__,
    )(*operands)
    return result[0] if len(shape) == 1 else result


def partner_sum(x, axis, partners):
    return x + lax.ppermute(x, axis, list(enumerate(partners)))


def out_steps(count):
    depth = count // 2
    steps = [[o ^ depth for o in range(count)]]
    bit = 1
    while bit < depth // 2:
        steps.append([o ^ bit for o in range(count)])
        bit *= 2
    if depth > 1:
        steps.append([(o & depth) | (depth - 1 - (o & (depth - 1))) for o in range(count)])
    return steps


def line_steps(count):
    steps = []
    bit = count // 2
    while bit:
        steps.append([i ^ bit for i in range(count)])
        bit //= 2
    return steps


def sum_over(x, axis, steps):
    for partners in steps:
        x = partner_sum(x, axis, partners)
    return x


def local(injections, transfer_factors, outage_factors, line_limits, outage_lines):
    rows, buses = transfer_factors.shape
    hours = injections.shape[0]
    width = outage_factors.shape[1]
    blocks = width // LANES
    over_out = out_steps(lax.axis_size("out"))
    over_line = line_steps(lax.axis_size("line"))
    line_start = lax.axis_index("line") * rows
    out_start = lax.axis_index("out") * width
    index = lax.dynamic_slice_in_dim(outage_lines, out_start, width, 0) - line_start
    index = index.reshape(1, width)
    limits = jnp.broadcast_to((0.5 / SOFTNESS) * line_limits[:, None], (rows, LANES))

    partial_flows = call(
        flows_kernel,
        [(hours, rows)],
        injections,
        transfer_factors,
        mib=60,
        far=2,
        scratch=[
            pltpu.VMEM((hours, buses), jnp.float32),
            pltpu.VMEM((rows, buses), jnp.float32),
            pltpu.SemaphoreType.DMA((4 + 1,)),
        ],
    )
    flow_rows = sum_over(partial_flows, "out", over_out)
    selected = call(select_kernel, [(hours, width)], flow_rows, index)
    flow_out = selected + lax.ppermute(selected, "line", list(enumerate(over_line[0])))
    flow_spread = call(spread_kernel, [(hours, rows, LANES)], flow_rows, mib=16)
    flow_out, flow_spread, limits = lax.optimization_barrier((flow_out, flow_spread, limits))
    flow_out = sum_over(flow_out, "line", over_line[1:])
    sums, column_part = call(
        overload_kernel,
        [(hours, rows, LANES), (hours, width)],
        outage_factors,
        flow_spread,
        limits,
        flow_out,
        mib=24,
        far=1,
        scratch=[
            pltpu.VMEM((rows, width), jnp.float32),
            pltpu.SemaphoreType.DMA((CHUNKS,)),
            pltpu.VMEM((hours * blocks, SUB, LANES), jnp.float32),
            pltpu.VMEM((hours * blocks, SUB, LANES), jnp.float32),
        ],
    )
    column_total = column_part + lax.ppermute(column_part, "line", list(enumerate(over_line[0])))
    row_part = call(row_kernel, [(hours, rows)], sums, mib=16)
    column_total, row_part = lax.optimization_barrier((column_total, row_part))
    column_total = partner_sum(column_total, "line", over_line[1])
    inverse = call(inverse_kernel, [(1, rows)], index, dtype=jnp.int32)
    column_total, inverse = lax.optimization_barrier((column_total, inverse))
    column_total = sum_over(column_total, "line", over_line[2:])
    placed = call(place_kernel, [(hours, rows)], column_total, inverse, row_part)
    line_slopes = sum_over(placed, "out", over_out)
    bus_terms = call(bus_kernel, [(hours, buses)], line_slopes, transfer_factors, mib=16)
    gradient = sum_over(bus_terms, "line", over_line)
    own = buses // lax.axis_size("line")
    return lax.dynamic_slice_in_dim(gradient, lax.axis_index("line") * own, own, 1)


def solution(mesh):
    in_specs = (P(None, "out"), P("line", "out"), P("line", "out"), P("line"), P())
    out_specs = P(None, ("out", "line"))
    return jax.shard_map(local, mesh=mesh, in_specs=in_specs, out_specs=out_specs, check_vma=False)
```

time: 129 us -> 105 us (0.81)
  Pallas kernels: 35.8 us -> 18 us
  local copies, waits for them, and re-layouts: 5.18 us -> 0.2 us
  waiting for transfers between devices: 29.8 us -> 27.1 us
  other arithmetic: 1.45 us -> 2.9 us
    pallas_call x6 -> x8, Pallas kernels: 35.8 us -> 18 us  [call(): pl.pallas_call(kernel, out_shape=out_shape, in_specs=[FAR] * far + [VMEM]...]
    ppermute x0 -> x2, starting transfers between devices: none -> 5.66 us  [the longest x1 2.83 us: local(): lax.ppermute(selected, 'line', list(enumerate(over_line[0])))]
    ppermute x20 -> x18, starting transfers between devices: 56.7 us -> 51.2 us  [partner_sum(): return x + lax.ppermute(x, axis, list(enumerate(partners)))]
    unnamed x10 -> x4, local copies, waits for them, and re-layouts: 5.18 us -> 0.01 us
    ppermute x20 -> x18, waiting for transfers between devices: 29.8 us -> 26.7 us  [partner_sum(): return x + lax.ppermute(x, axis, list(enumerate(partners)))]
  transfers between devices with their start and end apart: 20 -> 20, of which waited for: 20 -> 19; matrix products, arithmetic and copies ran while one was open for 1% -> 1% of each run, Pallas kernels for 1% -> 3%
where the time goes in v2:
time: 105 us
  starting transfers between devices  56.8 us (54%)
  waiting for transfers between devices  27.1 us (26%)
  Pallas kernels  18 us (17%)
  other arithmetic  2.9 us (3%)
    ppermute x18, starting transfers between devices, partner_sum(): return x + lax.ppermute(x, axis, list(enumerate(partners)))  51.2 us
    ppermute x18, waiting for transfers between devices, partner_sum(): return x + lax.ppermute(x, axis, list(enumerate(partners)))  26.7 us
    pallas_call x8, Pallas kernels, call(): pl.pallas_call(kernel, out_shape=out_shape, in_specs=[FAR] * far + [VMEM]...  18 us
    ppermute x1, starting transfers between devices, local(): lax.ppermute(selected, 'line', list(enumerate(over_line[0])))  2.83 us
    ppermute x1, starting transfers between devices, local(): lax.ppermute(column_part, 'line', list(enumerate(over_line[0])))  2.83 us
  transfers between devices with their start and end apart: 20, of which 19 were waited for; matrix products, arithmetic and copies ran while one was open for 1% of the time, Pallas kernels for 3%

profile of v2, /device:TPU:33, one launch (start us, length us, event | category | flops | bytes accessed | tf_op | source)
XLA Modules:
  0.0 105.1 jit_solution(5290817030943552417)
XLA Ops:
  0.0 3.1 %flows_kernel.1 = f32[8,1024]{1,0:T(8,128)} custom-call(f32[8,512]{1,0:T(8,128)} %injections_hbm.1, f32[1024,512]{1,0:T(8,128)} %factors_ref.1), custom_call_target="tpu_custom_call" | custom-call | bytes 2113536 | tf_op jit(solution)/shard_map/flows_kernel/pallas_call | solution.py:189
  3.1 1.3 %collective-permute-start = (f32[8,1024]{1,0:T(8,128)}, f32[8,1024]{1,0:T(8,128)S(1)}, u32[]{:S(2)}, u32[]{:S(2)}) collective-permute-start(f32[8,1024]{1,0:T(8,128)} %flows_kernel.1), channel_id=1, source_target_pairs={{0,8},{1,9},{2,10},{3,11},{4,12},{5,13},{6,14},{7,15},{8,0},{9,1},... | collective-permute-start | bytes 98312 | tf_op jit(solution)/shard_map/ppermute | solution.py:203
  4.4 1.8 %collective-permute-done = f32[8,1024]{1,0:T(8,128)S(1)} collective-permute-done((f32[8,1024]{1,0:T(8,128)}, f32[8,1024]{1,0:T(8,128)S(1)}, u32[]{:S(2)}, u32[]{:S(2)}) %collective-permute-start) | collective-permute-done | bytes 32800 | tf_op jit(solution)/shard_map/ppermute | solution.py:203
  6.9 2.8 %collective-permute-done.1 = f32[8,1024]{1,0:T(8,128)S(1)} collective-permute-done((f32[8,1024]{1,0:T(8,128)S(1)}, f32[8,1024]{1,0:T(8,128)S(1)}, u32[]{:S(2)}, u32[]{:S(2)}) %collective-permute-start.1) | collective-permute-done | bytes 32800 | tf_op jit(solution)/shard_map/ppermute | solution.py:203
  9.7 3.0 %collective-permute-start.2 = (f32[8,1024]{1,0:T(8,128)S(1)}, f32[8,1024]{1,0:T(8,128)S(1)}, u32[]{:S(2)}, u32[]{:S(2)}) collective-permute-start(f32[8,1024]{1,0:T(8,128)S(1)} %add.67), channel_id=1, source_target_pairs={{0,2},{1,3},{2,0},{3,1},{4,6},{5,7},{6,4},{7,5},{8,10},{9,11},{10,... | collective-permute-start | bytes 98312 | tf_op jit(solution)/shard_map/ppermute | solution.py:203
  12.7 1.3 %collective-permute-done.2 = f32[8,1024]{1,0:T(8,128)S(1)} collective-permute-done((f32[8,1024]{1,0:T(8,128)S(1)}, f32[8,1024]{1,0:T(8,128)S(1)}, u32[]{:S(2)}, u32[]{:S(2)}) %collective-permute-start.2) | collective-permute-done | bytes 32800 | tf_op jit(solution)/shard_map/ppermute | solution.py:203
  14.0 4.9 %collective-permute-start.3 = (f32[8,1024]{1,0:T(8,128)S(1)}, f32[8,1024]{1,0:T(8,128)S(1)}, u32[]{:S(2)}, u32[]{:S(2)}) collective-permute-start(f32[8,1024]{1,0:T(8,128)S(1)} %add.68), channel_id=1, source_target_pairs={{0,7},{1,6},{2,5},{3,4},{4,3},{5,2},{6,1},{7,0},{8,15},{9,14},{10,... | collective-permute-start | bytes 98312 | tf_op jit(solution)/shard_map/ppermute | solution.py:203
  20.4 2.8 %collective-permute-start.4 = (f32[8,1024]{1,0:T(8,128)S(1)}, f32[8,1024]{1,0:T(8,128)S(1)}, u32[]{:S(2)}, u32[]{:S(2)}) collective-permute-start(f32[8,1024]{1,0:T(8,128)S(1)} %select_kernel.1), channel_id=1, source_target_pairs={{0,128},{16,144},{32,160},{48,176},{64,192},{80,208},{96,224},{112... | collective-permute-start | bytes 98312 | tf_op jit(solution)/shard_map/ppermute | solution.py:261
  25.3 3.0 %collective-permute-start.5 = (f32[8,1024]{1,0:T(8,128)S(1)}, f32[8,1024]{1,0:T(8,128)S(1)}, u32[]{:S(2)}, u32[]{:S(2)}) collective-permute-start(f32[8,1024]{1,0:T(8,128)S(1)} %add.71), channel_id=1, source_target_pairs={{0,64},{16,80},{32,96},{48,112},{64,0},{80,16},{96,32},{112,48},{1... | collective-permute-start | bytes 98312 | tf_op jit(solution)/shard_map/ppermute | solution.py:203
  28.3 1.4 %collective-permute-done.5 = f32[8,1024]{1,0:T(8,128)S(1)} collective-permute-done((f32[8,1024]{1,0:T(8,128)S(1)}, f32[8,1024]{1,0:T(8,128)S(1)}, u32[]{:S(2)}, u32[]{:S(2)}) %collective-permute-start.5) | collective-permute-done | bytes 32800 | tf_op jit(solution)/shard_map/ppermute | solution.py:203
  29.7 1.6 %collective-permute-start.6 = (f32[8,1024]{1,0:T(8,128)S(1)}, f32[8,1024]{1,0:T(8,128)S(1)}, u32[]{:S(2)}, u32[]{:S(2)}) collective-permute-start(f32[8,1024]{1,0:T(8,128)S(1)} %add.72), channel_id=1, source_target_pairs={{0,32},{16,48},{32,0},{48,16},{64,96},{80,112},{96,64},{112,80},{1... | collective-permute-start | bytes 98312 | tf_op jit(solution)/shard_map/ppermute | solution.py:203
  31.2 1.3 %collective-permute-done.6 = f32[8,1024]{1,0:T(8,128)S(1)} collective-permute-done((f32[8,1024]{1,0:T(8,128)S(1)}, f32[8,1024]{1,0:T(8,128)S(1)}, u32[]{:S(2)}, u32[]{:S(2)}) %collective-permute-start.6) | collective-permute-done | bytes 32800 | tf_op jit(solution)/shard_map/ppermute | solution.py:203
  32.6 8.0 %collective-permute-start.7 = (f32[8,1024]{1,0:T(8,128)S(1)}, f32[8,1024]{1,0:T(8,128)S(1)}, u32[]{:S(2)}, u32[]{:S(2)}) collective-permute-start(f32[8,1024]{1,0:T(8,128)S(1)} %add.73), channel_id=1, source_target_pairs={{0,16},{16,0},{32,48},{48,32},{64,80},{80,64},{96,112},{112,96},{1... | collective-permute-start | bytes 98312 | tf_op jit(solution)/shard_map/ppermute | solution.py:203
  41.4 10.8 %overload_kernel.1 = (f32[8,1024,128]{2,1,0:T(8,128)S(1)}, f32[8,1024]{1,0:T(8,128)S(1)}) custom-call(f32[1024,1024]{1,0:T(8,128)S(1)} %copy-done.1, f32[8,1024,128]{2,1,0:T(8,128)S(1)} %spread_kernel.1.flow_ref, f32[1024,128]{1,0:T(8,128)S(1)} %broadcast_in_dim.2.limit_ref, f32[8,1024]{1,0:T(8,128)S(1)} %add.74.out_flow_ref), custom_call_target="tpu_custom_call" | custom-call | bytes 8945664 | tf_op jit(solution)/shard_map/overload_kernel/pallas_call | solution.py:189
  52.3 2.8 %collective-permute-start.8 = (f32[8,1024]{1,0:T(8,128)S(1)}, f32[8,1024]{1,0:T(8,128)S(1)}, u32[]{:S(2)}, u32[]{:S(2)}) collective-permute-start(f32[8,1024]{1,0:T(8,128)S(1)} %get-tuple-element.17), channel_id=1, source_target_pairs={{0,128},{16,144},{32,160},{48,176},{64,192},{80,208},{96,224},{112... | collective-permute-start | bytes 98312 | tf_op jit(solution)/shard_map/ppermute | solution.py:281
  56.6 2.9 %collective-permute-start.9 = (f32[8,1024]{1,0:T(8,128)S(1)}, f32[8,1024]{1,0:T(8,128)S(1)}, u32[]{:S(2)}, u32[]{:S(2)}) collective-permute-start(f32[8,1024]{1,0:T(8,128)S(1)} %add.75), channel_id=1, source_target_pairs={{0,64},{16,80},{32,96},{48,112},{64,0},{80,16},{96,32},{112,48},{1... | collective-permute-start | bytes 98312 | tf_op jit(solution)/shard_map/ppermute | solution.py:203
  60.9 1.3 %collective-permute-start.10 = (f32[8,1024]{1,0:T(8,128)S(1)}, f32[8,1024]{1,0:T(8,128)S(1)}, u32[]{:S(2)}, u32[]{:S(2)}) collective-permute-start(f32[8,1024]{1,0:T(8,128)S(1)} %add.76), channel_id=1, source_target_pairs={{0,32},{16,48},{32,0},{48,16},{64,96},{80,112},{96,64},{112,80},{1... | collective-permute-start | bytes 98312 | tf_op jit(solution)/shard_map/ppermute | solution.py:203
  62.2 1.5 %collective-permute-done.10 = f32[8,1024]{1,0:T(8,128)S(1)} collective-permute-done((f32[8,1024]{1,0:T(8,128)S(1)}, f32[8,1024]{1,0:T(8,128)S(1)}, u32[]{:S(2)}, u32[]{:S(2)}) %collective-permute-start.10) | collective-permute-done | bytes 32800 | tf_op jit(solution)/shard_map/ppermute | solution.py:203
  63.7 3.8 %collective-permute-start.11 = (f32[8,1024]{1,0:T(8,128)S(1)}, f32[8,1024]{1,0:T(8,128)S(1)}, u32[]{:S(2)}, u32[]{:S(2)}) collective-permute-start(f32[8,1024]{1,0:T(8,128)S(1)} %add.77), channel_id=1, source_target_pairs={{0,16},{16,0},{32,48},{48,32},{64,80},{80,64},{96,112},{112,96},{1... | collective-permute-start | bytes 98312 | tf_op jit(solution)/shard_map/ppermute | solution.py:203
  68.5 1.3 %collective-permute-start.12 = (f32[8,1024]{1,0:T(8,128)S(1)}, f32[8,1024]{1,0:T(8,128)S(1)}, u32[]{:S(2)}, u32[]{:S(2)}) collective-permute-start(f32[8,1024]{1,0:T(8,128)S(1)} %place_kernel.1), channel_id=1, source_target_pairs={{0,8},{1,9},{2,10},{3,11},{4,12},{5,13},{6,14},{7,15},{8,0},{9,1},... | collective-permute-start | bytes 98312 | tf_op jit(solution)/shard_map/ppermute | solution.py:203
  69.8 1.6 %collective-permute-done.12 = f32[8,1024]{1,0:T(8,128)S(1)} collective-permute-done((f32[8,1024]{1,0:T(8,128)S(1)}, f32[8,1024]{1,0:T(8,128)S(1)}, u32[]{:S(2)}, u32[]{:S(2)}) %collective-permute-start.12) | collective-permute-done | bytes 32800 | tf_op jit(solution)/shard_map/ppermute | solution.py:203
  71.4 2.8 %collective-permute-done.13 = f32[8,1024]{1,0:T(8,128)S(1)} collective-permute-done((f32[8,1024]{1,0:T(8,128)S(1)}, f32[8,1024]{1,0:T(8,128)S(1)}, u32[]{:S(2)}, u32[]{:S(2)}) %collective-permute-start.13) | collective-permute-done | bytes 32800 | tf_op jit(solution)/shard_map/ppermute | solution.py:203
  74.7 3.1 %collective-permute-done.14 = f32[8,1024]{1,0:T(8,128)S(1)} collective-permute-done((f32[8,1024]{1,0:T(8,128)S(1)}, f32[8,1024]{1,0:T(8,128)S(1)}, u32[]{:S(2)}, u32[]{:S(2)}) %collective-permute-start.14) | collective-permute-done | bytes 32800 | tf_op jit(solution)/shard_map/ppermute | solution.py:203
  77.8 4.8 %collective-permute-start.15 = (f32[8,1024]{1,0:T(8,128)S(1)}, f32[8,1024]{1,0:T(8,128)S(1)}, u32[]{:S(2)}, u32[]{:S(2)}) collective-permute-start(f32[8,1024]{1,0:T(8,128)S(1)} %add.81), channel_id=1, source_target_pairs={{0,7},{1,6},{2,5},{3,4},{4,3},{5,2},{6,1},{7,0},{8,15},{9,14},{10,... | collective-permute-start | bytes 98312 | tf_op jit(solution)/shard_map/ppermute | solution.py:203
  82.6 1.7 %collective-permute-done.15 = f32[8,1024]{1,0:T(8,128)S(1)} collective-permute-done((f32[8,1024]{1,0:T(8,128)S(1)}, f32[8,1024]{1,0:T(8,128)S(1)}, u32[]{:S(2)}, u32[]{:S(2)}) %collective-permute-start.15) | collective-permute-done | bytes 32800 | tf_op jit(solution)/shard_map/ppermute | solution.py:203
  85.0 2.8 %collective-permute-start.16 = (f32[8,512]{1,0:T(8,128)S(1)}, f32[8,512]{1,0:T(8,128)S(1)}, u32[]{:S(2)}, u32[]{:S(2)}) collective-permute-start(f32[8,512]{1,0:T(8,128)S(1)} %bus_kernel.1), channel_id=1, source_target_pairs={{0,128},{16,144},{32,160},{48,176},{64,192},{80,208},{96,224},{112... | collective-permute-start | bytes 49160 | tf_op jit(solution)/shard_map/ppermute | solution.py:203
  87.8 1.4 %collective-permute-done.16 = f32[8,512]{1,0:T(8,128)S(1)} collective-permute-done((f32[8,512]{1,0:T(8,128)S(1)}, f32[8,512]{1,0:T(8,128)S(1)}, u32[]{:S(2)}, u32[]{:S(2)}) %collective-permute-start.16) | collective-permute-done | bytes 16416 | tf_op jit(solution)/shard_map/ppermute | solution.py:203
  89.2 2.9 %collective-permute-start.17 = (f32[8,512]{1,0:T(8,128)S(1)}, f32[8,512]{1,0:T(8,128)S(1)}, u32[]{:S(2)}, u32[]{:S(2)}) collective-permute-start(f32[8,512]{1,0:T(8,128)S(1)} %add.83), channel_id=1, source_target_pairs={{0,64},{16,80},{32,96},{48,112},{64,0},{80,16},{96,32},{112,48},{1... | collective-permute-start | bytes 49160 | tf_op jit(solution)/shard_map/ppermute | solution.py:203
  92.1 1.2 %collective-permute-done.17 = f32[8,512]{1,0:T(8,128)S(1)} collective-permute-done((f32[8,512]{1,0:T(8,128)S(1)}, f32[8,512]{1,0:T(8,128)S(1)}, u32[]{:S(2)}, u32[]{:S(2)}) %collective-permute-start.17) | collective-permute-done | bytes 16416 | tf_op jit(solution)/shard_map/ppermute | solution.py:203
  93.3 1.3 %collective-permute-start.18 = (f32[8,512]{1,0:T(8,128)S(1)}, f32[8,512]{1,0:T(8,128)S(1)}, u32[]{:S(2)}, u32[]{:S(2)}) collective-permute-start(f32[8,512]{1,0:T(8,128)S(1)} %add.84), channel_id=1, source_target_pairs={{0,32},{16,48},{32,0},{48,16},{64,96},{80,112},{96,64},{112,80},{1... | collective-permute-start | bytes 49160 | tf_op jit(solution)/shard_map/ppermute | solution.py:203
  94.6 1.3 %collective-permute-done.18 = f32[8,512]{1,0:T(8,128)S(1)} collective-permute-done((f32[8,512]{1,0:T(8,128)S(1)}, f32[8,512]{1,0:T(8,128)S(1)}, u32[]{:S(2)}, u32[]{:S(2)}) %collective-permute-start.18) | collective-permute-done | bytes 16416 | tf_op jit(solution)/shard_map/ppermute | solution.py:203
  95.9 7.8 %collective-permute-start.19 = (f32[8,512]{1,0:T(8,128)S(1)}, f32[8,512]{1,0:T(8,128)S(1)}, u32[]{:S(2)}, u32[]{:S(2)}) collective-permute-start(f32[8,512]{1,0:T(8,128)S(1)} %add.85), channel_id=1, source_target_pairs={{0,16},{16,0},{32,48},{48,32},{64,80},{80,64},{96,112},{112,96},{1... | collective-permute-start | bytes 49160 | tf_op jit(solution)/shard_map/ppermute | solution.py:203
  (43 shorter events, 11.9 us)
Async XLA Ops:
  3.1 3.1 %collective-permute-start = (f32[8,1024]{1,0:T(8,128)}, f32[8,1024]{1,0:T(8,128)S(1)}, u32[]{:S(2)}, u32[]{:S(2)}) collective-permute-start(f32[8,1024]{1,0:T(8,128)} %flows_kernel.1), channel_id=1, source_target_pairs={{0,8},{1,9},{2,10},{3,11},{4,12},{5,13},{6,14},{7,15},{8,0},{9,1},... | collective-permute-start | bytes 98312 | tf_op jit(solution)/shard_map/ppermute | solution.py:203
  6.9 2.8 %collective-permute-start.1 = (f32[8,1024]{1,0:T(8,128)S(1)}, f32[8,1024]{1,0:T(8,128)S(1)}, u32[]{:S(2)}, u32[]{:S(2)}) collective-permute-start(f32[8,1024]{1,0:T(8,128)S(1)} %add.66), channel_id=1, source_target_pairs={{0,1},{1,0},{2,3},{3,2},{4,5},{5,4},{6,7},{7,6},{8,9},{9,8},{10,11... | collective-permute-start | bytes 98312 | tf_op jit(solution)/shard_map/ppermute | solution.py:203
  9.7 4.3 %collective-permute-start.2 = (f32[8,1024]{1,0:T(8,128)S(1)}, f32[8,1024]{1,0:T(8,128)S(1)}, u32[]{:S(2)}, u32[]{:S(2)}) collective-permute-start(f32[8,1024]{1,0:T(8,128)S(1)} %add.67), channel_id=1, source_target_pairs={{0,2},{1,3},{2,0},{3,1},{4,6},{5,7},{6,4},{7,5},{8,10},{9,11},{10,... | collective-permute-start | bytes 98312 | tf_op jit(solution)/shard_map/ppermute | solution.py:203
  12.7 28.7 %copy-start.1 = (f32[1024,1024]{1,0:T(8,128)S(1)}, f32[1024,1024]{1,0:T(8,128)}, u32[]{:S(2)}) copy-start(f32[1024,1024]{1,0:T(8,128)} %factors_hbm.3) | copy-start | bytes 12582916
  14.0 6.2 %collective-permute-start.3 = (f32[8,1024]{1,0:T(8,128)S(1)}, f32[8,1024]{1,0:T(8,128)S(1)}, u32[]{:S(2)}, u32[]{:S(2)}) collective-permute-start(f32[8,1024]{1,0:T(8,128)S(1)} %add.68), channel_id=1, source_target_pairs={{0,7},{1,6},{2,5},{3,4},{4,3},{5,2},{6,1},{7,0},{8,15},{9,14},{10,... | collective-permute-start | bytes 98312 | tf_op jit(solution)/shard_map/ppermute | solution.py:203
  20.4 4.7 %collective-permute-start.4 = (f32[8,1024]{1,0:T(8,128)S(1)}, f32[8,1024]{1,0:T(8,128)S(1)}, u32[]{:S(2)}, u32[]{:S(2)}) collective-permute-start(f32[8,1024]{1,0:T(8,128)S(1)} %select_kernel.1), channel_id=1, source_target_pairs={{0,128},{16,144},{32,160},{48,176},{64,192},{80,208},{96,224},{112... | collective-permute-start | bytes 98312 | tf_op jit(solution)/shard_map/ppermute | solution.py:261
  25.3 4.4 %collective-permute-start.5 = (f32[8,1024]{1,0:T(8,128)S(1)}, f32[8,1024]{1,0:T(8,128)S(1)}, u32[]{:S(2)}, u32[]{:S(2)}) collective-permute-start(f32[8,1024]{1,0:T(8,128)S(1)} %add.71), channel_id=1, source_target_pairs={{0,64},{16,80},{32,96},{48,112},{64,0},{80,16},{96,32},{112,48},{1... | collective-permute-start | bytes 98312 | tf_op jit(solution)/shard_map/ppermute | solution.py:203
  29.7 2.9 %collective-permute-start.6 = (f32[8,1024]{1,0:T(8,128)S(1)}, f32[8,1024]{1,0:T(8,128)S(1)}, u32[]{:S(2)}, u32[]{:S(2)}) collective-permute-start(f32[8,1024]{1,0:T(8,128)S(1)} %add.72), channel_id=1, source_target_pairs={{0,32},{16,48},{32,0},{48,16},{64,96},{80,112},{96,64},{112,80},{1... | collective-permute-start | bytes 98312 | tf_op jit(solution)/shard_map/ppermute | solution.py:203
  32.6 8.8 %collective-permute-start.7 = (f32[8,1024]{1,0:T(8,128)S(1)}, f32[8,1024]{1,0:T(8,128)S(1)}, u32[]{:S(2)}, u32[]{:S(2)}) collective-permute-start(f32[8,1024]{1,0:T(8,128)S(1)} %add.73), channel_id=1, source_target_pairs={{0,16},{16,0},{32,48},{48,32},{64,80},{80,64},{96,112},{112,96},{1... | collective-permute-start | bytes 98312 | tf_op jit(solution)/shard_map/ppermute | solution.py:203
  52.3 32.0 %copy-start = (f32[1024,512]{1,0:T(8,128)S(1)}, f32[1024,512]{1,0:T(8,128)}, u32[]{:S(2)}) copy-start(f32[1024,512]{1,0:T(8,128)} %factors_ref.1) | copy-start | bytes 6291460
  52.3 4.4 %collective-permute-start.8 = (f32[8,1024]{1,0:T(8,128)S(1)}, f32[8,1024]{1,0:T(8,128)S(1)}, u32[]{:S(2)}, u32[]{:S(2)}) collective-permute-start(f32[8,1024]{1,0:T(8,128)S(1)} %get-tuple-element.17), channel_id=1, source_target_pairs={{0,128},{16,144},{32,160},{48,176},{64,192},{80,208},{96,224},{112... | collective-permute-start | bytes 98312 | tf_op jit(solution)/shard_map/ppermute | solution.py:281
  56.6 4.3 %collective-permute-start.9 = (f32[8,1024]{1,0:T(8,128)S(1)}, f32[8,1024]{1,0:T(8,128)S(1)}, u32[]{:S(2)}, u32[]{:S(2)}) collective-permute-start(f32[8,1024]{1,0:T(8,128)S(1)} %add.75), channel_id=1, source_target_pairs={{0,64},{16,80},{32,96},{48,112},{64,0},{80,16},{96,32},{112,48},{1... | collective-permute-start | bytes 98312 | tf_op jit(solution)/shard_map/ppermute | solution.py:203
  60.9 2.8 %collective-permute-start.10 = (f32[8,1024]{1,0:T(8,128)S(1)}, f32[8,1024]{1,0:T(8,128)S(1)}, u32[]{:S(2)}, u32[]{:S(2)}) collective-permute-start(f32[8,1024]{1,0:T(8,128)S(1)} %add.76), channel_id=1, source_target_pairs={{0,32},{16,48},{32,0},{48,16},{64,96},{80,112},{96,64},{112,80},{1... | collective-permute-start | bytes 98312 | tf_op jit(solution)/shard_map/ppermute | solution.py:203
  63.7 4.7 %collective-permute-start.11 = (f32[8,1024]{1,0:T(8,128)S(1)}, f32[8,1024]{1,0:T(8,128)S(1)}, u32[]{:S(2)}, u32[]{:S(2)}) collective-permute-start(f32[8,1024]{1,0:T(8,128)S(1)} %add.77), channel_id=1, source_target_pairs={{0,16},{16,0},{32,48},{48,32},{64,80},{80,64},{96,112},{112,96},{1... | collective-permute-start | bytes 98312 | tf_op jit(solution)/shard_map/ppermute | solution.py:203
  68.5 2.9 %collective-permute-start.12 = (f32[8,1024]{1,0:T(8,128)S(1)}, f32[8,1024]{1,0:T(8,128)S(1)}, u32[]{:S(2)}, u32[]{:S(2)}) collective-permute-start(f32[8,1024]{1,0:T(8,128)S(1)} %place_kernel.1), channel_id=1, source_target_pairs={{0,8},{1,9},{2,10},{3,11},{4,12},{5,13},{6,14},{7,15},{8,0},{9,1},... | collective-permute-start | bytes 98312 | tf_op jit(solution)/shard_map/ppermute | solution.py:203
  71.4 2.8 %collective-permute-start.13 = (f32[8,1024]{1,0:T(8,128)S(1)}, f32[8,1024]{1,0:T(8,128)S(1)}, u32[]{:S(2)}, u32[]{:S(2)}) collective-permute-start(f32[8,1024]{1,0:T(8,128)S(1)} %add.79), channel_id=1, source_target_pairs={{0,1},{1,0},{2,3},{3,2},{4,5},{5,4},{6,7},{7,6},{8,9},{9,8},{10,11... | collective-permute-start | bytes 98312 | tf_op jit(solution)/shard_map/ppermute | solution.py:203
  74.2 3.7 %collective-permute-start.14 = (f32[8,1024]{1,0:T(8,128)S(1)}, f32[8,1024]{1,0:T(8,128)S(1)}, u32[]{:S(2)}, u32[]{:S(2)}) collective-permute-start(f32[8,1024]{1,0:T(8,128)S(1)} %add.80), channel_id=1, source_target_pairs={{0,2},{1,3},{2,0},{3,1},{4,6},{5,7},{6,4},{7,5},{8,10},{9,11},{10,... | collective-permute-start | bytes 98312 | tf_op jit(solution)/shard_map/ppermute | solution.py:203
  77.8 6.4 %collective-permute-start.15 = (f32[8,1024]{1,0:T(8,128)S(1)}, f32[8,1024]{1,0:T(8,128)S(1)}, u32[]{:S(2)}, u32[]{:S(2)}) collective-permute-start(f32[8,1024]{1,0:T(8,128)S(1)} %add.81), channel_id=1, source_target_pairs={{0,7},{1,6},{2,5},{3,4},{4,3},{5,2},{6,1},{7,0},{8,15},{9,14},{10,... | collective-permute-start | bytes 98312 | tf_op jit(solution)/shard_map/ppermute | solution.py:203
  85.0 4.2 %collective-permute-start.16 = (f32[8,512]{1,0:T(8,128)S(1)}, f32[8,512]{1,0:T(8,128)S(1)}, u32[]{:S(2)}, u32[]{:S(2)}) collective-permute-start(f32[8,512]{1,0:T(8,128)S(1)} %bus_kernel.1), channel_id=1, source_target_pairs={{0,128},{16,144},{32,160},{48,176},{64,192},{80,208},{96,224},{112... | collective-permute-start | bytes 49160 | tf_op jit(solution)/shard_map/ppermute | solution.py:203
  89.2 4.1 %collective-permute-start.17 = (f32[8,512]{1,0:T(8,128)S(1)}, f32[8,512]{1,0:T(8,128)S(1)}, u32[]{:S(2)}, u32[]{:S(2)}) collective-permute-start(f32[8,512]{1,0:T(8,128)S(1)} %add.83), channel_id=1, source_target_pairs={{0,64},{16,80},{32,96},{48,112},{64,0},{80,16},{96,32},{112,48},{1... | collective-permute-start | bytes 49160 | tf_op jit(solution)/shard_map/ppermute | solution.py:203
  93.3 2.6 %collective-permute-start.18 = (f32[8,512]{1,0:T(8,128)S(1)}, f32[8,512]{1,0:T(8,128)S(1)}, u32[]{:S(2)}, u32[]{:S(2)}) collective-permute-start(f32[8,512]{1,0:T(8,128)S(1)} %add.84), channel_id=1, source_target_pairs={{0,32},{16,48},{32,0},{48,16},{64,96},{80,112},{96,64},{112,80},{1... | collective-permute-start | bytes 49160 | tf_op jit(solution)/shard_map/ppermute | solution.py:203
  95.9 8.6 %collective-permute-start.19 = (f32[8,512]{1,0:T(8,128)S(1)}, f32[8,512]{1,0:T(8,128)S(1)}, u32[]{:S(2)}, u32[]{:S(2)}) collective-permute-start(f32[8,512]{1,0:T(8,128)S(1)} %add.85), channel_id=1, source_target_pairs={{0,16},{16,0},{32,48},{48,32},{64,80},{80,64},{96,112},{112,96},{1... | collective-permute-start | bytes 49160 | tf_op jit(solution)/shard_map/ppermute | solution.py:203

commit v3 on v2

--- a/solution.py
+++ b/solution.py
@@ -12,7 +12,7 @@
 LANES = 128
 SUB = 8
 TILES = 4
-CHUNKS = 8
+CHUNKS = 4
 VMEM = pl.BlockSpec(memory_space=pltpu.VMEM)
 FAR = pl.BlockSpec(memory_space=pltpu.HBM)
 
@@ -61,7 +61,12 @@
 
 
 def bus_kernel(slopes_ref, factors_ref, out_ref):
-    out_ref[...] = product(stacked(slopes_ref[...]), factors_ref[...], (((1,), (0,)), ((), ())))
+    terms = product(stacked(slopes_ref[...]), factors_ref[...], (((1,), (0,)), ((), ())))
+    pieces, hours, lanes = out_ref.shape
+    own = terms.shape[1] // pieces
+    out_ref[...] = jnp.zeros_like(out_ref)
+    for p in range(pieces):
+        out_ref[p, :, :own] = terms[:, p * own : (p + 1) * own]
 
 
 def inverse_kernel(index_ref, out_ref):
@@ -112,29 +117,21 @@
 
 
 def overload_kernel(
-    factors_hbm, flow_ref, limit_ref, out_flow_ref, sums_ref, column_ref, factors, sems, wide, total
+    factors_ref, flow_ref, limit_ref, out_flow_ref, sums_ref, column_ref, wide, total
 ):
-    rows, width = factors.shape
+    rows, width = factors_ref.shape
     hours = flow_ref.shape[0]
     blocks = width // LANES
-    chunks = sems.shape[0]
-    chunk_rows = rows // chunks
     parts = range(TILES)
     tile = TILES * SUB
-
-    def copy(c):
-        here = pl.ds(pl.multiple_of(c * chunk_rows, chunk_rows), chunk_rows)
-        return pltpu.make_async_copy(factors_hbm.at[here, :], factors.at[here, :], sems.at[c])
-
-    for c in range(chunks):
-        copy(c).start()
     for h in range(hours):
         for kb in range(blocks):
             piece = (0.5 / SOFTNESS) * out_flow_ref[h : h + 1, kb * LANES : (kb + 1) * LANES]
             wide[h * blocks + kb] = jnp.broadcast_to(piece, (SUB, LANES))
     total[...] = jnp.zeros_like(total)
 
-    def advance(start):
+    def advance(step, carry):
+        start = pl.multiple_of(step * tile, tile)
         at = [pl.ds(start + r * SUB, SUB) for r in parts]
         limit = [limit_ref[at[r], :] for r in parts]
         for h in range(hours):
@@ -146,7 +143,7 @@
                 out_flow = wide[h * blocks + kb]
                 gathered = None
                 for r in parts:
-                    factor = factors[at[r], kb * LANES : (kb + 1) * LANES]
+                    factor = factors_ref[at[r], kb * LANES : (kb + 1) * LANES]
                     moved = factor * out_flow
                     slope = jnp.tanh(moved + plus[r]) + jnp.tanh(moved + minus[r])
                     across[r] = slope if across[r] is None else across[r] + slope
@@ -155,17 +152,9 @@
                 total[h * blocks + kb] = total[h * blocks + kb] + gathered
             for r in parts:
                 sums_ref[h, at[r], :] = across[r]
-
-    def chunk(c, carry):
-        copy(c).wait()
-
-        def step(s, inner):
-            advance(pl.multiple_of(c * chunk_rows + s * tile, tile))
-            return inner
-
-        return lax.fori_loop(0, chunk_rows // tile, step, carry)
-
-    lax.fori_loop(0, chunks, chunk, 0)
+        return carry
+
+    lax.fori_loop(0, rows // tile, advance, 0)
     for h in range(hours):
         for kb in range(blocks):
             column_ref[h : h + 1, kb * LANES : (kb + 1) * LANES] = (0.5 / OUTAGES) * jnp.sum(
@@ -199,11 +188,40 @@
     return result[0] if len(shape) == 1 else result
 
 
-def partner_sum(x, axis, partners):
-    return x + lax.ppermute(x, axis, list(enumerate(partners)))
-
-
-def out_steps(count):
+def received(x, axis, partners):
+    return lax.ppermute(x, axis, list(enumerate(partners)))
+
+
+def group_sum(x, axis, groups):
+    copies = jnp.broadcast_to(x, (len(groups[0]),) + x.shape)
+    return lax.all_to_all(copies, axis, 0, 0, axis_index_groups=groups, tiled=True).sum(0)
+
+
+BWD_LINE = "a2a"
+BWD_OUT = "rd"
+FIN = "a2a"
+
+
+def out_sum(x):
+    count = lax.axis_size("out")
+    depth = count // 2
+    x = x + received(x, "out", [o ^ depth for o in range(count)])
+    return group_sum(x, "out", [[g * depth + z for z in range(depth)] for g in range(2)])
+
+
+def line_pair_steps(count):
+    half = count // 2
+    steps = [[i ^ half for i in range(count)]]
+    if half > 2:
+        steps.append([i ^ (half - 2) for i in range(count)])
+    bit = 2
+    while bit < half // 2:
+        steps.append([i ^ bit for i in range(count)])
+        bit *= 2
+    return steps + [cores(count)]
+
+
+def out_pair_steps(count):
     depth = count // 2
     steps = [[o ^ depth for o in range(count)]]
     bit = 1
@@ -215,19 +233,12 @@
     return steps
 
 
-def line_steps(count):
-    steps = []
-    bit = count // 2
-    while bit:
-        steps.append([i ^ bit for i in range(count)])
-        bit //= 2
-    return steps
-
-
-def sum_over(x, axis, steps):
-    for partners in steps:
-        x = partner_sum(x, axis, partners)
-    return x
+def cores(count):
+    return [i ^ 1 for i in range(count)]
+
+
+def chips(count):
+    return [[i for i in range(count) if i % 2 == core] for core in range(2)]
 
 
 def local(injections, transfer_factors, outage_factors, line_limits, outage_lines):
@@ -235,8 +246,7 @@
     hours = injections.shape[0]
     width = outage_factors.shape[1]
     blocks = width // LANES
-    over_out = out_steps(lax.axis_size("out"))
-    over_line = line_steps(lax.axis_size("line"))
+    lines = lax.axis_size("line")
     line_start = lax.axis_index("line") * rows
     out_start = lax.axis_index("out") * width
     index = lax.dynamic_slice_in_dim(outage_lines, out_start, width, 0) - line_start
@@ -253,15 +263,21 @@
         scratch=[
             pltpu.VMEM((hours, buses), jnp.float32),
             pltpu.VMEM((rows, buses), jnp.float32),
-            pltpu.SemaphoreType.DMA((4 + 1,)),
+            pltpu.SemaphoreType.DMA((CHUNKS + 1,)),
         ],
     )
-    flow_rows = sum_over(partial_flows, "out", over_out)
+    inverse = call(inverse_kernel, [(1, rows)], index, dtype=jnp.int32)
+    flow_rows = partial_flows
+    for partners in out_pair_steps(lax.axis_size("out")):
+        flow_rows = flow_rows + received(flow_rows, "out", partners)
+    flow_rows, inverse, limits = lax.optimization_barrier((flow_rows, inverse, limits))
     selected = call(select_kernel, [(hours, width)], flow_rows, index)
-    flow_out = selected + lax.ppermute(selected, "line", list(enumerate(over_line[0])))
+    first, *others = line_pair_steps(lines)
+    flow_out = selected + received(selected, "line", first)
     flow_spread = call(spread_kernel, [(hours, rows, LANES)], flow_rows, mib=16)
-    flow_out, flow_spread, limits = lax.optimization_barrier((flow_out, flow_spread, limits))
-    flow_out = sum_over(flow_out, "line", over_line[1:])
+    flow_out, flow_spread = lax.optimization_barrier((flow_out, flow_spread))
+    for partners in others:
+        flow_out = flow_out + received(flow_out, "line", partners)
     sums, column_part = call(
         overload_kernel,
         [(hours, rows, LANES), (hours, width)],
@@ -270,27 +286,37 @@
         limits,
         flow_out,
         mib=24,
-        far=1,
         scratch=[
-            pltpu.VMEM((rows, width), jnp.float32),
-            pltpu.SemaphoreType.DMA((CHUNKS,)),
             pltpu.VMEM((hours * blocks, SUB, LANES), jnp.float32),
             pltpu.VMEM((hours * blocks, SUB, LANES), jnp.float32),
         ],
     )
-    column_total = column_part + lax.ppermute(column_part, "line", list(enumerate(over_line[0])))
+    if BWD_LINE == "a2a":
+        column_total = column_part + received(column_part, "line", cores(lines))
+    else:
+        column_total = column_part + received(column_part, "line", first)
     row_part = call(row_kernel, [(hours, rows)], sums, mib=16)
     column_total, row_part = lax.optimization_barrier((column_total, row_part))
-    column_total = partner_sum(column_total, "line", over_line[1])
-    inverse = call(inverse_kernel, [(1, rows)], index, dtype=jnp.int32)
-    column_total, inverse = lax.optimization_barrier((column_total, inverse))
-    column_total = sum_over(column_total, "line", over_line[2:])
+    if BWD_LINE == "a2a":
+        column_total = group_sum(column_total, "line", chips(lines))
+    else:
+        for partners in others:
+            column_total = column_total + received(column_total, "line", partners)
     placed = call(place_kernel, [(hours, rows)], column_total, inverse, row_part)
-    line_slopes = sum_over(placed, "out", over_out)
-    bus_terms = call(bus_kernel, [(hours, buses)], line_slopes, transfer_factors, mib=16)
-    gradient = sum_over(bus_terms, "line", over_line)
-    own = buses // lax.axis_size("line")
-    return lax.dynamic_slice_in_dim(gradient, lax.axis_index("line") * own, own, 1)
+    if BWD_OUT == "a2a":
+        line_slopes = out_sum(placed)
+    else:
+        line_slopes = placed
+        for partners in out_pair_steps(lax.axis_size("out")):
+            line_slopes = line_slopes + received(line_slopes, "out", partners)
+    pieces = call(bus_kernel, [(lines, hours, LANES)], line_slopes, transfer_factors, mib=16)
+    if FIN == "a2a":
+        gradient = lax.all_to_all(pieces, "line", 0, 0, tiled=True).sum(0)
+    else:
+        for partners in line_pair_steps(lines):
+            pieces = pieces + received(pieces, "line", partners)
+        gradient = lax.dynamic_index_in_dim(pieces, lax.axis_index("line"), 0, keepdims=False)
+    return gradient[:, : buses // lines]
 
 
 def solution(mesh):

time: 105 us -> 101 us (0.962)
  blocking collectives: 0 us -> 30.2 us
  starting transfers between devices: 56.8 us -> 29.2 us
  waiting for transfers between devices: 27.1 us -> 20.1 us
    all_to_all x0 -> x2, blocking collectives: none -> 30.2 us  [the longest x1 16.3 us: local(): gradient = lax.all_to_all(pieces, 'line', 0, 0, tiled=True).sum(0)]
    ppermute x20 -> x13, starting transfers between devices: 56.8 us -> 29.2 us  [received(): return lax.ppermute(x, axis, list(enumerate(partners)))]
    ppermute x20 -> x13, waiting for transfers between devices: 27.1 us -> 20.1 us  [received(): return lax.ppermute(x, axis, list(enumerate(partners)))]
  transfers between devices with their start and end apart: 20 -> 13, of which waited for: 19 -> 11; matrix products, arithmetic and copies ran while one was open for 1% -> 1% of each run, Pallas kernels for 3% -> 3%
where the time goes in v3:
time: 101 us; the launch traced here: 100 us
  blocking collectives  30.2 us (30%)
  starting transfers between devices  29.2 us (29%)
  waiting for transfers between devices  20.1 us (20%)
  Pallas kernels  17.5 us (17%)
  other arithmetic  2.84 us (3%)
    ppermute x13, starting transfers between devices, received(): return lax.ppermute(x, axis, list(enumerate(partners)))  29.2 us
    ppermute x13, waiting for transfers between devices, received(): return lax.ppermute(x, axis, list(enumerate(partners)))  20.1 us
    pallas_call x8, Pallas kernels, call(): pl.pallas_call(kernel, out_shape=out_shape, in_specs=[FAR] * far + [VMEM]...  17.5 us
    all_to_all x1, blocking collectives, local(): gradient = lax.all_to_all(pieces, 'line', 0, 0, tiled=True).sum(0)  16.3 us
    all_to_all x1, blocking collectives, group_sum(): lax.all_to_all(copies, axis, 0, 0, axis_index_groups=groups, tiled=True)  13.8 us
  transfers between devices with their start and end apart: 13, of which 11 were waited for; matrix products, arithmetic and copies ran while one was open for 1% of the time, Pallas kernels for 3%

profile of v3, /device:TPU:33, one launch (start us, length us, event | category | flops | bytes accessed | tf_op | source)
XLA Modules:
  0.0 100.2 jit_solution(4204282029163707660)
XLA Ops:
  0.0 3.1 %flows_kernel.1 = f32[8,1024]{1,0:T(8,128)} custom-call(f32[8,512]{1,0:T(8,128)} %injections_hbm.1, f32[1024,512]{1,0:T(8,128)} %factors_ref.3), custom_call_target="tpu_custom_call" | custom-call | bytes 2113536 | tf_op jit(solution)/shard_map/flows_kernel/pallas_call | solution.py:178
  3.1 1.3 %collective-permute-start = (f32[8,1024]{1,0:T(8,128)}, f32[8,1024]{1,0:T(8,128)S(1)}, u32[]{:S(2)}, u32[]{:S(2)}) collective-permute-start(f32[8,1024]{1,0:T(8,128)} %flows_kernel.1), channel_id=1, source_target_pairs={{0,8},{1,9},{2,10},{3,11},{4,12},{5,13},{6,14},{7,15},{8,0},{9,1},... | collective-permute-start | bytes 98312 | tf_op jit(solution)/shard_map/ppermute | solution.py:192
  4.4 1.8 %collective-permute-done = f32[8,1024]{1,0:T(8,128)S(1)} collective-permute-done((f32[8,1024]{1,0:T(8,128)}, f32[8,1024]{1,0:T(8,128)S(1)}, u32[]{:S(2)}, u32[]{:S(2)}) %collective-permute-start) | collective-permute-done | bytes 32800 | tf_op jit(solution)/shard_map/ppermute | solution.py:192
  6.2 0.8 add.42
  6.9 2.8 %collective-permute-done.1 = f32[8,1024]{1,0:T(8,128)S(1)} collective-permute-done((f32[8,1024]{1,0:T(8,128)S(1)}, f32[8,1024]{1,0:T(8,128)S(1)}, u32[]{:S(2)}, u32[]{:S(2)}) %collective-permute-start.1) | collective-permute-done | bytes 32800 | tf_op jit(solution)/shard_map/ppermute | solution.py:192
  9.7 3.0 %collective-permute-start.2 = (f32[8,1024]{1,0:T(8,128)S(1)}, f32[8,1024]{1,0:T(8,128)S(1)}, u32[]{:S(2)}, u32[]{:S(2)}) collective-permute-start(f32[8,1024]{1,0:T(8,128)S(1)} %add.43), channel_id=1, source_target_pairs={{0,2},{1,3},{2,0},{3,1},{4,6},{5,7},{6,4},{7,5},{8,10},{9,11},{10,... | collective-permute-start | bytes 98312 | tf_op jit(solution)/shard_map/ppermute | solution.py:192
  12.7 0.7 broadcast_multiply_fusion
  13.4 0.6 collective-permute-done.2
  14.0 4.9 %collective-permute-start.3 = (f32[8,1024]{1,0:T(8,128)S(1)}, f32[8,1024]{1,0:T(8,128)S(1)}, u32[]{:S(2)}, u32[]{:S(2)}) collective-permute-start(f32[8,1024]{1,0:T(8,128)S(1)} %add.44), channel_id=1, source_target_pairs={{0,7},{1,6},{2,5},{3,4},{4,3},{5,2},{6,1},{7,0},{8,15},{9,14},{10,... | collective-permute-start | bytes 98312 | tf_op jit(solution)/shard_map/ppermute | solution.py:192
  18.9 0.7 dynamic-slice_subtract_fusion
  19.6 0.7 inverse_kernel.1.index_ref
  20.7 2.8 %collective-permute-start.4 = (f32[8,1024]{1,0:T(8,128)S(1)}, f32[8,1024]{1,0:T(8,128)S(1)}, u32[]{:S(2)}, u32[]{:S(2)}) collective-permute-start(f32[8,1024]{1,0:T(8,128)S(1)} %select_kernel.1), channel_id=1, source_target_pairs={{0,128},{16,144},{32,160},{48,176},{64,192},{80,208},{96,224},{112... | collective-permute-start | bytes 98312 | tf_op jit(solution)/shard_map/ppermute | solution.py:192
  23.5 1.1 %spread_kernel.1.flow_ref = f32[8,1024,128]{2,1,0:T(8,128)S(1)} custom-call(f32[8,1024]{1,0:T(8,128)S(1)} %add.45.values_ref.flow_ref), custom_call_target="tpu_custom_call" | custom-call | bytes 32768 | tf_op jit(solution)/shard_map/spread_kernel/pallas_call | solution.py:178
  25.1 2.7 %collective-permute-start.5 = (f32[8,1024]{1,0:T(8,128)S(1)}, f32[8,1024]{1,0:T(8,128)S(1)}, u32[]{:S(2)}, u32[]{:S(2)}) collective-permute-start(f32[8,1024]{1,0:T(8,128)S(1)} %add.47), channel_id=1, source_target_pairs={{0,96},{16,112},{32,64},{48,80},{64,32},{80,48},{96,0},{112,16},{1... | collective-permute-start | bytes 98312 | tf_op jit(solution)/shard_map/ppermute | solution.py:192
  27.8 1.3 %collective-permute-done.5 = f32[8,1024]{1,0:T(8,128)S(1)} collective-permute-done((f32[8,1024]{1,0:T(8,128)S(1)}, f32[8,1024]{1,0:T(8,128)S(1)}, u32[]{:S(2)}, u32[]{:S(2)}) %collective-permute-start.5) | collective-permute-done | bytes 32800 | tf_op jit(solution)/shard_map/ppermute | solution.py:192
  29.1 2.7 %collective-permute-done.6 = f32[8,1024]{1,0:T(8,128)S(1)} collective-permute-done((f32[8,1024]{1,0:T(8,128)S(1)}, f32[8,1024]{1,0:T(8,128)S(1)}, u32[]{:S(2)}, u32[]{:S(2)}) %collective-permute-start.6) | collective-permute-done | bytes 32800 | tf_op jit(solution)/shard_map/ppermute | solution.py:192
  31.9 8.3 %collective-permute-start.7 = (f32[8,1024]{1,0:T(8,128)S(1)}, f32[8,1024]{1,0:T(8,128)S(1)}, u32[]{:S(2)}, u32[]{:S(2)}) collective-permute-start(f32[8,1024]{1,0:T(8,128)S(1)} %add.49), channel_id=1, source_target_pairs={{0,16},{16,0},{32,48},{48,32},{64,80},{80,64},{96,112},{112,96},{1... | collective-permute-start | bytes 98312 | tf_op jit(solution)/shard_map/ppermute | solution.py:192
  40.2 0.9 collective-permute-done.7
  41.0 10.3 %overload_kernel.1 = (f32[8,1024,128]{2,1,0:T(8,128)S(1)}, f32[8,1024]{1,0:T(8,128)S(1)}) custom-call(f32[1024,1024]{1,0:T(8,128)S(1)} %copy-done.1, f32[8,1024,128]{2,1,0:T(8,128)S(1)} %spread_kernel.1.flow_ref, f32[1024,128]{1,0:T(8,128)S(1)} %broadcast_in_dim.4.limit_ref, f32[8,1024]{1,0:T(8,128)S(1)} %add.50.out_flow_ref), custom_call_target="tpu_custom_call" | custom-call | bytes 8945664 | tf_op jit(solution)/shard_map/overload_kernel/pallas_call | solution.py:178
  51.3 0.4 collective-permute-start.8
  51.8 1.1 %row_kernel.1.rows_ref = f32[8,1024]{1,0:T(8,128)S(1)} custom-call(f32[8,1024,128]{2,1,0:T(8,128)S(1)} %get-tuple-element.19.sums_ref), custom_call_target="tpu_custom_call" | custom-call | bytes 4194304 | tf_op jit(solution)/shard_map/row_kernel/pallas_call | solution.py:178
  53.0 13.8 %all_to_all.10 = f32[8,8,1024]{2,1,0:T(8,128)S(1)} all-to-all(f32[8,8,1024]{2,1,0:T(8,128)S(1)} %broadcast_in_dim.10), channel_id=1, replica_groups={{0,32,64,96,128,160,192,224},{16,48,80,112,144,176,208,240},{1,33,65,97..., dimensions={0} | all-to-all | bytes 524288 | tf_op jit(solution)/shard_map/all_to_all | solution.py:197
  67.0 0.4 collective-permute-start.9
  67.4 2.5 %collective-permute-done.9 = f32[8,1024]{1,0:T(8,128)S(1)} collective-permute-done((f32[8,1024]{1,0:T(8,128)S(1)}, f32[8,1024]{1,0:T(8,128)S(1)}, u32[]{:S(2)}, u32[]{:S(2)}) %collective-permute-start.9) | collective-permute-done | bytes 32800 | tf_op jit(solution)/shard_map/ppermute | solution.py:192
  69.9 2.8 %collective-permute-done.10 = f32[8,1024]{1,0:T(8,128)S(1)} collective-permute-done((f32[8,1024]{1,0:T(8,128)S(1)}, f32[8,1024]{1,0:T(8,128)S(1)}, u32[]{:S(2)}, u32[]{:S(2)}) %collective-permute-start.10) | collective-permute-done | bytes 32800 | tf_op jit(solution)/shard_map/ppermute | solution.py:192
  72.7 0.5 collective-permute-start.11
  73.2 3.1 %collective-permute-done.11 = f32[8,1024]{1,0:T(8,128)S(1)} collective-permute-done((f32[8,1024]{1,0:T(8,128)S(1)}, f32[8,1024]{1,0:T(8,128)S(1)}, u32[]{:S(2)}, u32[]{:S(2)}) %collective-permute-start.11) | collective-permute-done | bytes 32800 | tf_op jit(solution)/shard_map/ppermute | solution.py:192
  76.4 4.8 %collective-permute-start.12 = (f32[8,1024]{1,0:T(8,128)S(1)}, f32[8,1024]{1,0:T(8,128)S(1)}, u32[]{:S(2)}, u32[]{:S(2)}) collective-permute-start(f32[8,1024]{1,0:T(8,128)S(1)} %add.54), channel_id=1, source_target_pairs={{0,7},{1,6},{2,5},{3,4},{4,3},{5,2},{6,1},{7,0},{8,15},{9,14},{10,... | collective-permute-start | bytes 98312 | tf_op jit(solution)/shard_map/ppermute | solution.py:192
  81.1 1.3 %collective-permute-done.12 = f32[8,1024]{1,0:T(8,128)S(1)} collective-permute-done((f32[8,1024]{1,0:T(8,128)S(1)}, f32[8,1024]{1,0:T(8,128)S(1)}, u32[]{:S(2)}, u32[]{:S(2)}) %collective-permute-start.12) | collective-permute-done | bytes 32800 | tf_op jit(solution)/shard_map/ppermute | solution.py:192
  82.4 0.9 bus_kernel.1
  83.3 16.3 %all_to_all.11 = f32[16,8,128]{2,1,0:T(8,128)S(1)} all-to-all(f32[16,8,128]{2,1,0:T(8,128)S(1)} %bus_kernel.1), channel_id=1, replica_groups=mesh['line'=16,'out'=16] {'line'}, dimensions={0} | all-to-all | bytes 131072 | tf_op jit(solution)/shard_map/all_to_all | solution.py:314
  99.6 0.6 reduce_sum.19
  (27 shorter events, 1.1 us)
Async XLA Ops:
  3.1 3.1 %collective-permute-start = (f32[8,1024]{1,0:T(8,128)}, f32[8,1024]{1,0:T(8,128)S(1)}, u32[]{:S(2)}, u32[]{:S(2)}) collective-permute-start(f32[8,1024]{1,0:T(8,128)} %flows_kernel.1), channel_id=1, source_target_pairs={{0,8},{1,9},{2,10},{3,11},{4,12},{5,13},{6,14},{7,15},{8,0},{9,1},... | collective-permute-start | bytes 98312 | tf_op jit(solution)/shard_map/ppermute | solution.py:192
  6.9 2.8 %collective-permute-start.1 = (f32[8,1024]{1,0:T(8,128)S(1)}, f32[8,1024]{1,0:T(8,128)S(1)}, u32[]{:S(2)}, u32[]{:S(2)}) collective-permute-start(f32[8,1024]{1,0:T(8,128)S(1)} %add.42), channel_id=1, source_target_pairs={{0,1},{1,0},{2,3},{3,2},{4,5},{5,4},{6,7},{7,6},{8,9},{9,8},{10,11... | collective-permute-start | bytes 98312 | tf_op jit(solution)/shard_map/ppermute | solution.py:192
  9.7 4.3 %collective-permute-start.2 = (f32[8,1024]{1,0:T(8,128)S(1)}, f32[8,1024]{1,0:T(8,128)S(1)}, u32[]{:S(2)}, u32[]{:S(2)}) collective-permute-start(f32[8,1024]{1,0:T(8,128)S(1)} %add.43), channel_id=1, source_target_pairs={{0,2},{1,3},{2,0},{3,1},{4,6},{5,7},{6,4},{7,5},{8,10},{9,11},{10,... | collective-permute-start | bytes 98312 | tf_op jit(solution)/shard_map/ppermute | solution.py:192
  13.4 27.7 %copy-start.1 = (f32[1024,1024]{1,0:T(8,128)S(1)}, f32[1024,1024]{1,0:T(8,128)}, u32[]{:S(2)}) copy-start(f32[1024,1024]{1,0:T(8,128)} %factors_ref.2) | copy-start | bytes 12582916
  14.0 6.3 %collective-permute-start.3 = (f32[8,1024]{1,0:T(8,128)S(1)}, f32[8,1024]{1,0:T(8,128)S(1)}, u32[]{:S(2)}, u32[]{:S(2)}) collective-permute-start(f32[8,1024]{1,0:T(8,128)S(1)} %add.44), channel_id=1, source_target_pairs={{0,7},{1,6},{2,5},{3,4},{4,3},{5,2},{6,1},{7,0},{8,15},{9,14},{10,... | collective-permute-start | bytes 98312 | tf_op jit(solution)/shard_map/ppermute | solution.py:192
  20.7 4.4 %collective-permute-start.4 = (f32[8,1024]{1,0:T(8,128)S(1)}, f32[8,1024]{1,0:T(8,128)S(1)}, u32[]{:S(2)}, u32[]{:S(2)}) collective-permute-start(f32[8,1024]{1,0:T(8,128)S(1)} %select_kernel.1), channel_id=1, source_target_pairs={{0,128},{16,144},{32,160},{48,176},{64,192},{80,208},{96,224},{112... | collective-permute-start | bytes 98312 | tf_op jit(solution)/shard_map/ppermute | solution.py:192
  25.1 4.0 %collective-permute-start.5 = (f32[8,1024]{1,0:T(8,128)S(1)}, f32[8,1024]{1,0:T(8,128)S(1)}, u32[]{:S(2)}, u32[]{:S(2)}) collective-permute-start(f32[8,1024]{1,0:T(8,128)S(1)} %add.47), channel_id=1, source_target_pairs={{0,96},{16,112},{32,64},{48,80},{64,32},{80,48},{96,0},{112,16},{1... | collective-permute-start | bytes 98312 | tf_op jit(solution)/shard_map/ppermute | solution.py:192
  29.1 2.8 %collective-permute-start.6 = (f32[8,1024]{1,0:T(8,128)S(1)}, f32[8,1024]{1,0:T(8,128)S(1)}, u32[]{:S(2)}, u32[]{:S(2)}) collective-permute-start(f32[8,1024]{1,0:T(8,128)S(1)} %add.48), channel_id=1, source_target_pairs={{0,32},{16,48},{32,0},{48,16},{64,96},{80,112},{96,64},{112,80},{1... | collective-permute-start | bytes 98312 | tf_op jit(solution)/shard_map/ppermute | solution.py:192
  31.9 9.2 %collective-permute-start.7 = (f32[8,1024]{1,0:T(8,128)S(1)}, f32[8,1024]{1,0:T(8,128)S(1)}, u32[]{:S(2)}, u32[]{:S(2)}) collective-permute-start(f32[8,1024]{1,0:T(8,128)S(1)} %add.49), channel_id=1, source_target_pairs={{0,16},{16,0},{32,48},{48,32},{64,80},{80,64},{96,112},{112,96},{1... | collective-permute-start | bytes 98312 | tf_op jit(solution)/shard_map/ppermute | solution.py:192
  51.3 31.1 %copy-start = (f32[1024,512]{1,0:T(8,128)S(1)}, f32[1024,512]{1,0:T(8,128)}, u32[]{:S(2)}) copy-start(f32[1024,512]{1,0:T(8,128)} %factors_ref.3) | copy-start | bytes 6291460
  51.3 1.6 %collective-permute-start.8 = (f32[8,1024]{1,0:T(8,128)S(1)}, f32[8,1024]{1,0:T(8,128)S(1)}, u32[]{:S(2)}, u32[]{:S(2)}) collective-permute-start(f32[8,1024]{1,0:T(8,128)S(1)} %get-tuple-element.18), channel_id=1, source_target_pairs={{0,16},{16,0},{32,48},{48,32},{64,80},{80,64},{96,112},{112,96},{1... | collective-permute-start | bytes 98312 | tf_op jit(solution)/shard_map/ppermute | solution.py:192
  67.0 2.9 %collective-permute-start.9 = (f32[8,1024]{1,0:T(8,128)S(1)}, f32[8,1024]{1,0:T(8,128)S(1)}, u32[]{:S(2)}, u32[]{:S(2)}) collective-permute-start(f32[8,1024]{1,0:T(8,128)S(1)} %place_kernel.1), channel_id=1, source_target_pairs={{0,8},{1,9},{2,10},{3,11},{4,12},{5,13},{6,14},{7,15},{8,0},{9,1},... | collective-permute-start | bytes 98312 | tf_op jit(solution)/shard_map/ppermute | solution.py:192
  69.9 2.8 %collective-permute-start.10 = (f32[8,1024]{1,0:T(8,128)S(1)}, f32[8,1024]{1,0:T(8,128)S(1)}, u32[]{:S(2)}, u32[]{:S(2)}) collective-permute-start(f32[8,1024]{1,0:T(8,128)S(1)} %add.52), channel_id=1, source_target_pairs={{0,1},{1,0},{2,3},{3,2},{4,5},{5,4},{6,7},{7,6},{8,9},{9,8},{10,11... | collective-permute-start | bytes 98312 | tf_op jit(solution)/shard_map/ppermute | solution.py:192
  72.7 3.7 %collective-permute-start.11 = (f32[8,1024]{1,0:T(8,128)S(1)}, f32[8,1024]{1,0:T(8,128)S(1)}, u32[]{:S(2)}, u32[]{:S(2)}) collective-permute-start(f32[8,1024]{1,0:T(8,128)S(1)} %add.53), channel_id=1, source_target_pairs={{0,2},{1,3},{2,0},{3,1},{4,6},{5,7},{6,4},{7,5},{8,10},{9,11},{10,... | collective-permute-start | bytes 98312 | tf_op jit(solution)/shard_map/ppermute | solution.py:192
  76.4 6.1 %collective-permute-start.12 = (f32[8,1024]{1,0:T(8,128)S(1)}, f32[8,1024]{1,0:T(8,128)S(1)}, u32[]{:S(2)}, u32[]{:S(2)}) collective-permute-start(f32[8,1024]{1,0:T(8,128)S(1)} %add.54), channel_id=1, source_target_pairs={{0,7},{1,6},{2,5},{3,4},{4,3},{5,2},{6,1},{7,0},{8,15},{9,14},{10,... | collective-permute-start | bytes 98312 | tf_op jit(solution)/shard_map/ppermute | solution.py:192

commit v4 on v3

--- a/solution.py
+++ b/solution.py
@@ -188,57 +188,38 @@
     return result[0] if len(shape) == 1 else result
 
 
-def received(x, axis, partners):
-    return lax.ppermute(x, axis, list(enumerate(partners)))
-
-
-def group_sum(x, axis, groups):
-    copies = jnp.broadcast_to(x, (len(groups[0]),) + x.shape)
-    return lax.all_to_all(copies, axis, 0, 0, axis_index_groups=groups, tiled=True).sum(0)
-
-
-BWD_LINE = "a2a"
-BWD_OUT = "rd"
-FIN = "a2a"
-
-
-def out_sum(x):
-    count = lax.axis_size("out")
-    depth = count // 2
-    x = x + received(x, "out", [o ^ depth for o in range(count)])
-    return group_sum(x, "out", [[g * depth + z for z in range(depth)] for g in range(2)])
-
-
-def line_pair_steps(count):
-    half = count // 2
-    steps = [[i ^ half for i in range(count)]]
+def pairs_over(dims, moves):
+    lines, outs = dims
+    pairs = []
+    for i in range(lines):
+        for o in range(outs):
+            to_line, to_out = moves(i, o)
+            pairs.append((i * outs + o, to_line * outs + to_out))
+    return pairs
+
+
+def out_moves(outs):
+    depth = outs // 2
+    moves = [lambda i, o: (i, o ^ depth)]
+    bit = 1
+    while bit < depth // 2:
+        moves.append(lambda i, o, bit=bit: (i, o ^ bit))
+        bit *= 2
+    if depth > 1:
+        moves.append(lambda i, o: (i, (o & depth) | (depth - 1 - (o & (depth - 1)))))
+    return moves
+
+
+def line_moves(lines):
+    half = lines // 2
+    moves = [lambda i, o: (i ^ half ^ 1, o)]
     if half > 2:
-        steps.append([i ^ (half - 2) for i in range(count)])
+        moves.append(lambda i, o: (i ^ (half - 2) ^ 1, o))
     bit = 2
     while bit < half // 2:
-        steps.append([i ^ bit for i in range(count)])
+        moves.append(lambda i, o, bit=bit: (i ^ bit ^ 1, o))
         bit *= 2
-    return steps + [cores(count)]
-
-
-def out_pair_steps(count):
-    depth = count // 2
-    steps = [[o ^ depth for o in range(count)]]
-    bit = 1
-    while bit < depth // 2:
-        steps.append([o ^ bit for o in range(count)])
-        bit *= 2
-    if depth > 1:
-        steps.append([(o & depth) | (depth - 1 - (o & (depth - 1))) for o in range(count)])
-    return steps
-
-
-def cores(count):
-    return [i ^ 1 for i in range(count)]
-
-
-def chips(count):
-    return [[i for i in range(count) if i % 2 == core] for core in range(2)]
+    return moves
 
 
 def local(injections, transfer_factors, outage_factors, line_limits, outage_lines):
@@ -246,14 +227,21 @@
     hours = injections.shape[0]
     width = outage_factors.shape[1]
     blocks = width // LANES
-    lines = lax.axis_size("line")
-    line_start = lax.axis_index("line") * rows
+    lines, outs = lax.axis_size("line"), lax.axis_size("out")
+    line = lax.axis_index("line")
     out_start = lax.axis_index("out") * width
-    index = lax.dynamic_slice_in_dim(outage_lines, out_start, width, 0) - line_start
+    index = lax.dynamic_slice_in_dim(outage_lines, out_start, width, 0) - line * rows
     index = index.reshape(1, width)
     limits = jnp.broadcast_to((0.5 / SOFTNESS) * line_limits[:, None], (rows, LANES))
 
-    partial_flows = call(
+    def add_move(x, move):
+        return x + lax.ppermute(x, ("line", "out"), pairs_over((lines, outs), move))
+
+    def other_core(x):
+        return lax.ppermute(x, "line", [(i, i ^ 1) for i in range(lines)])
+
+    over_out, over_line = out_moves(outs), line_moves(lines)
+    flows = call(
         flows_kernel,
         [(hours, rows)],
         injections,
@@ -267,17 +255,15 @@
         ],
     )
     inverse = call(inverse_kernel, [(1, rows)], index, dtype=jnp.int32)
-    flow_rows = partial_flows
-    for partners in out_pair_steps(lax.axis_size("out")):
-        flow_rows = flow_rows + received(flow_rows, "out", partners)
-    flow_rows, inverse, limits = lax.optimization_barrier((flow_rows, inverse, limits))
-    selected = call(select_kernel, [(hours, width)], flow_rows, index)
-    first, *others = line_pair_steps(lines)
-    flow_out = selected + received(selected, "line", first)
-    flow_spread = call(spread_kernel, [(hours, rows, LANES)], flow_rows, mib=16)
+    for move in over_out:
+        flows = add_move(flows, move)
+    flows, inverse, limits = lax.optimization_barrier((flows, inverse, limits))
+    flow_out = call(select_kernel, [(hours, width)], flows, index)
+    flow_out = flow_out + other_core(flow_out)
+    flow_spread = call(spread_kernel, [(hours, rows, LANES)], flows, mib=16)
     flow_out, flow_spread = lax.optimization_barrier((flow_out, flow_spread))
-    for partners in others:
-        flow_out = flow_out + received(flow_out, "line", partners)
+    for move in over_line:
+        flow_out = add_move(flow_out, move)
     sums, column_part = call(
         overload_kernel,
         [(hours, rows, LANES), (hours, width)],
@@ -291,31 +277,18 @@
             pltpu.VMEM((hours * blocks, SUB, LANES), jnp.float32),
         ],
     )
-    if BWD_LINE == "a2a":
-        column_total = column_part + received(column_part, "line", cores(lines))
-    else:
-        column_total = column_part + received(column_part, "line", first)
+    column_total = column_part + other_core(column_part)
     row_part = call(row_kernel, [(hours, rows)], sums, mib=16)
     column_total, row_part = lax.optimization_barrier((column_total, row_part))
-    if BWD_LINE == "a2a":
-        column_total = group_sum(column_total, "line", chips(lines))
-    else:
-        for partners in others:
-            column_total = column_total + received(column_total, "line", partners)
-    placed = call(place_kernel, [(hours, rows)], column_total, inverse, row_part)
-    if BWD_OUT == "a2a":
-        line_slopes = out_sum(placed)
-    else:
-        line_slopes = placed
-        for partners in out_pair_steps(lax.axis_size("out")):
-            line_slopes = line_slopes + received(line_slopes, "out", partners)
-    pieces = call(bus_kernel, [(lines, hours, LANES)], line_slopes, transfer_factors, mib=16)
-    if FIN == "a2a":
-        gradient = lax.all_to_all(pieces, "line", 0, 0, tiled=True).sum(0)
-    else:
-        for partners in line_pair_steps(lines):
-            pieces = pieces + received(pieces, "line", partners)
-        gradient = lax.dynamic_index_in_dim(pieces, lax.axis_index("line"), 0, keepdims=False)
+    copies = jnp.broadcast_to(column_total, (lines // 2,) + column_total.shape)
+    column_total = lax.all_to_all(
+        copies, "line", 0, 0, axis_index_groups=[list(range(c, lines, 2)) for c in range(2)], tiled=True
+    ).sum(0)
+    slopes = call(place_kernel, [(hours, rows)], column_total, inverse, row_part)
+    for move in over_out:
+        slopes = add_move(slopes, move)
+    pieces = call(bus_kernel, [(lines, hours, LANES)], slopes, transfer_factors, mib=16)
+    gradient = lax.all_to_all(pieces, "line", 0, 0, tiled=True).sum(0)
     return gradient[:, : buses // lines]
 
 

time: 101 us -> 98.9 us (0.979)
  starting transfers between devices: 29.2 us -> 25.5 us
  waiting for transfers between devices: 20.1 us -> 22.4 us
    ppermute x13, starting transfers between devices: 29.2 us -> 25.5 us  [the longest x11 20.2 us: add_move(): return x + lax.ppermute(x, ('line', 'out'), pairs_over((lines, outs), move))]
    ppermute x13, waiting for transfers between devices: 20.1 us -> 22.4 us  [the longest x11 22.4 us: add_move(): return x + lax.ppermute(x, ('line', 'out'), pairs_over((lines, outs), move))]
  transfers between devices with their start and end apart: 13 -> 13, of which waited for: 11 -> 10; matrix products, arithmetic and copies ran while one was open for 1% -> 1% of each run, Pallas kernels for 3% -> 3%
where the time goes in v4:
time: 98.9 us; the launch traced here: 98.6 us
  blocking collectives  30 us (30%)
  starting transfers between devices  25.5 us (26%)
  waiting for transfers between devices  22.4 us (23%)
  Pallas kernels  17.6 us (18%)
  other arithmetic  2.84 us (3%)
    ppermute x11, waiting for transfers between devices, add_move(): return x + lax.ppermute(x, ('line', 'out'), pairs_over((lines, outs), move))  22.4 us
    ppermute x11, starting transfers between devices, add_move(): return x + lax.ppermute(x, ('line', 'out'), pairs_over((lines, outs), move))  20.2 us
    pallas_call x8, Pallas kernels, call(): pl.pallas_call(kernel, out_shape=out_shape, in_specs=[FAR] * far + [VMEM]...  17.6 us
    all_to_all x1, blocking collectives, local(): gradient = lax.all_to_all(pieces, 'line', 0, 0, tiled=True).sum(0)  16.3 us
    all_to_all x1, blocking collectives, local(): lax.all_to_all(copies, 'line', 0, 0, axis_index_groups=[list(range(c, lin...  13.7 us
    ppermute x2, starting transfers between devices, other_core(): return lax.ppermute(x, 'line', [(i, i ^ 1) for i in range(lines)])  5.27 us
  transfers between devices with their start and end apart: 13, of which 10 were waited for; matrix products, arithmetic and copies ran while one was open for 1% of the time, Pallas kernels for 3%

profile of v4, /device:TPU:33, one launch (start us, length us, event | category | flops | bytes accessed | tf_op | source)
XLA Modules:
  0.0 98.6 jit_solution(17604432637579942562)
XLA Ops:
  0.0 3.1 %flows_kernel.1 = f32[8,1024]{1,0:T(8,128)} custom-call(f32[8,512]{1,0:T(8,128)} %injections_hbm.1, f32[1024,512]{1,0:T(8,128)} %factors_ref.3), custom_call_target="tpu_custom_call" | custom-call | bytes 2113536 | tf_op jit(solution)/shard_map/flows_kernel/pallas_call | solution.py:178
  3.1 1.3 %collective-permute-start = (f32[8,1024]{1,0:T(8,128)}, f32[8,1024]{1,0:T(8,128)S(1)}, u32[]{:S(2)}, u32[]{:S(2)}) collective-permute-start(f32[8,1024]{1,0:T(8,128)} %flows_kernel.1), channel_id=1, source_target_pairs={{0,8},{1,9},{2,10},{3,11},{4,12},{5,13},{6,14},{7,15},{8,0},{9,1},... | collective-permute-start | bytes 98312 | tf_op jit(solution)/shard_map/ppermute | solution.py:238
  4.4 1.8 %collective-permute-done = f32[8,1024]{1,0:T(8,128)S(1)} collective-permute-done((f32[8,1024]{1,0:T(8,128)}, f32[8,1024]{1,0:T(8,128)S(1)}, u32[]{:S(2)}, u32[]{:S(2)}) %collective-permute-start) | collective-permute-done | bytes 32800 | tf_op jit(solution)/shard_map/ppermute | solution.py:238
  6.2 0.8 add.42
  6.9 2.8 %collective-permute-done.1 = f32[8,1024]{1,0:T(8,128)S(1)} collective-permute-done((f32[8,1024]{1,0:T(8,128)S(1)}, f32[8,1024]{1,0:T(8,128)S(1)}, u32[]{:S(2)}, u32[]{:S(2)}) %collective-permute-start.1) | collective-permute-done | bytes 32800 | tf_op jit(solution)/shard_map/ppermute | solution.py:238
  9.7 3.0 %collective-permute-start.2 = (f32[8,1024]{1,0:T(8,128)S(1)}, f32[8,1024]{1,0:T(8,128)S(1)}, u32[]{:S(2)}, u32[]{:S(2)}) collective-permute-start(f32[8,1024]{1,0:T(8,128)S(1)} %add.43), channel_id=1, source_target_pairs={{0,2},{1,3},{2,0},{3,1},{4,6},{5,7},{6,4},{7,5},{8,10},{9,11},{10,... | collective-permute-start | bytes 98312 | tf_op jit(solution)/shard_map/ppermute | solution.py:238
  12.7 0.7 broadcast_multiply_fusion
  13.4 0.6 collective-permute-done.2
  14.0 4.9 %collective-permute-start.3 = (f32[8,1024]{1,0:T(8,128)S(1)}, f32[8,1024]{1,0:T(8,128)S(1)}, u32[]{:S(2)}, u32[]{:S(2)}) collective-permute-start(f32[8,1024]{1,0:T(8,128)S(1)} %add.44), channel_id=1, source_target_pairs={{0,7},{1,6},{2,5},{3,4},{4,3},{5,2},{6,1},{7,0},{8,15},{9,14},{10,... | collective-permute-start | bytes 98312 | tf_op jit(solution)/shard_map/ppermute | solution.py:238
  18.9 0.7 dynamic-slice_subtract_fusion
  19.6 0.7 inverse_kernel.1.index_ref
  20.7 5.0 %collective-permute-start.4 = (f32[8,1024]{1,0:T(8,128)S(1)}, f32[8,1024]{1,0:T(8,128)S(1)}, u32[]{:S(2)}, u32[]{:S(2)}) collective-permute-start(f32[8,1024]{1,0:T(8,128)S(1)} %select_kernel.1), channel_id=1, source_target_pairs={{0,16},{16,0},{32,48},{48,32},{64,80},{80,64},{96,112},{112,96},{1... | collective-permute-start | bytes 98312 | tf_op jit(solution)/shard_map/ppermute | solution.py:241
  25.7 1.1 %spread_kernel.1.flow_ref = f32[8,1024,128]{2,1,0:T(8,128)S(1)} custom-call(f32[8,1024]{1,0:T(8,128)S(1)} %add.45.values_ref.flow_ref), custom_call_target="tpu_custom_call" | custom-call | bytes 32768 | tf_op jit(solution)/shard_map/spread_kernel/pallas_call | solution.py:178
  26.9 2.7 %collective-permute-start.5 = (f32[8,1024]{1,0:T(8,128)S(1)}, f32[8,1024]{1,0:T(8,128)S(1)}, u32[]{:S(2)}, u32[]{:S(2)}) collective-permute-start(f32[8,1024]{1,0:T(8,128)S(1)} %add.47), channel_id=1, source_target_pairs={{0,144},{1,145},{2,146},{3,147},{4,148},{5,149},{6,150},{7,151},{8... | collective-permute-start | bytes 98312 | tf_op jit(solution)/shard_map/ppermute | solution.py:238
  29.6 2.2 %collective-permute-done.5 = f32[8,1024]{1,0:T(8,128)S(1)} collective-permute-done((f32[8,1024]{1,0:T(8,128)S(1)}, f32[8,1024]{1,0:T(8,128)S(1)}, u32[]{:S(2)}, u32[]{:S(2)}) %collective-permute-start.5) | collective-permute-done | bytes 32800 | tf_op jit(solution)/shard_map/ppermute | solution.py:238
  31.8 2.6 %collective-permute-start.6 = (f32[8,1024]{1,0:T(8,128)S(1)}, f32[8,1024]{1,0:T(8,128)S(1)}, u32[]{:S(2)}, u32[]{:S(2)}) collective-permute-start(f32[8,1024]{1,0:T(8,128)S(1)} %add.48), channel_id=1, source_target_pairs={{0,112},{1,113},{2,114},{3,115},{4,116},{5,117},{6,118},{7,119},{8... | collective-permute-start | bytes 98312 | tf_op jit(solution)/shard_map/ppermute | solution.py:238
  34.4 1.9 %collective-permute-done.6 = f32[8,1024]{1,0:T(8,128)S(1)} collective-permute-done((f32[8,1024]{1,0:T(8,128)S(1)}, f32[8,1024]{1,0:T(8,128)S(1)}, u32[]{:S(2)}, u32[]{:S(2)}) %collective-permute-start.6) | collective-permute-done | bytes 32800 | tf_op jit(solution)/shard_map/ppermute | solution.py:238
  36.4 3.3 %collective-permute-done.7 = f32[8,1024]{1,0:T(8,128)S(1)} collective-permute-done((f32[8,1024]{1,0:T(8,128)S(1)}, f32[8,1024]{1,0:T(8,128)S(1)}, u32[]{:S(2)}, u32[]{:S(2)}) %collective-permute-start.7) | collective-permute-done | bytes 32800 | tf_op jit(solution)/shard_map/ppermute | solution.py:238
  39.7 10.3 %overload_kernel.1 = (f32[8,1024,128]{2,1,0:T(8,128)S(1)}, f32[8,1024]{1,0:T(8,128)S(1)}) custom-call(f32[1024,1024]{1,0:T(8,128)S(1)} %copy-done.1, f32[8,1024,128]{2,1,0:T(8,128)S(1)} %spread_kernel.1.flow_ref, f32[1024,128]{1,0:T(8,128)S(1)} %broadcast_in_dim.4.limit_ref, f32[8,1024]{1,0:T(8,128)S(1)} %add.50.out_flow_ref), custom_call_target="tpu_custom_call" | custom-call | bytes 8945664 | tf_op jit(solution)/shard_map/overload_kernel/pallas_call | solution.py:178
  50.0 0.3 collective-permute-start.8
  50.3 1.1 %row_kernel.1.rows_ref = f32[8,1024]{1,0:T(8,128)S(1)} custom-call(f32[8,1024,128]{2,1,0:T(8,128)S(1)} %get-tuple-element.19.sums_ref), custom_call_target="tpu_custom_call" | custom-call | bytes 4194304 | tf_op jit(solution)/shard_map/row_kernel/pallas_call | solution.py:178
  51.5 13.7 %all_to_all.10 = f32[8,8,1024]{2,1,0:T(8,128)S(1)} all-to-all(f32[8,8,1024]{2,1,0:T(8,128)S(1)} %broadcast_in_dim.10), channel_id=1, replica_groups={{0,32,64,96,128,160,192,224},{16,48,80,112,144,176,208,240},{1,33,65,97..., dimensions={0} | all-to-all | bytes 524288 | tf_op jit(solution)/shard_map/all_to_all | solution.py:284
  65.4 0.4 collective-permute-start.9
  65.8 2.5 %collective-permute-done.9 = f32[8,1024]{1,0:T(8,128)S(1)} collective-permute-done((f32[8,1024]{1,0:T(8,128)S(1)}, f32[8,1024]{1,0:T(8,128)S(1)}, u32[]{:S(2)}, u32[]{:S(2)}) %collective-permute-start.9) | collective-permute-done | bytes 32800 | tf_op jit(solution)/shard_map/ppermute | solution.py:238
  68.2 2.8 %collective-permute-done.10 = f32[8,1024]{1,0:T(8,128)S(1)} collective-permute-done((f32[8,1024]{1,0:T(8,128)S(1)}, f32[8,1024]{1,0:T(8,128)S(1)}, u32[]{:S(2)}, u32[]{:S(2)}) %collective-permute-start.10) | collective-permute-done | bytes 32800 | tf_op jit(solution)/shard_map/ppermute | solution.py:238
  71.1 0.5 collective-permute-start.11
  71.6 3.2 %collective-permute-done.11 = f32[8,1024]{1,0:T(8,128)S(1)} collective-permute-done((f32[8,1024]{1,0:T(8,128)S(1)}, f32[8,1024]{1,0:T(8,128)S(1)}, u32[]{:S(2)}, u32[]{:S(2)}) %collective-permute-start.11) | collective-permute-done | bytes 32800 | tf_op jit(solution)/shard_map/ppermute | solution.py:238
  74.8 4.8 %collective-permute-start.12 = (f32[8,1024]{1,0:T(8,128)S(1)}, f32[8,1024]{1,0:T(8,128)S(1)}, u32[]{:S(2)}, u32[]{:S(2)}) collective-permute-start(f32[8,1024]{1,0:T(8,128)S(1)} %add.54), channel_id=1, source_target_pairs={{0,7},{1,6},{2,5},{3,4},{4,3},{5,2},{6,1},{7,0},{8,15},{9,14},{10,... | collective-permute-start | bytes 98312 | tf_op jit(solution)/shard_map/ppermute | solution.py:238
  79.5 1.3 %collective-permute-done.12 = f32[8,1024]{1,0:T(8,128)S(1)} collective-permute-done((f32[8,1024]{1,0:T(8,128)S(1)}, f32[8,1024]{1,0:T(8,128)S(1)}, u32[]{:S(2)}, u32[]{:S(2)}) %collective-permute-start.12) | collective-permute-done | bytes 32800 | tf_op jit(solution)/shard_map/ppermute | solution.py:238
  80.8 0.9 bus_kernel.1
  81.7 16.3 %all_to_all.11 = f32[16,8,128]{2,1,0:T(8,128)S(1)} all-to-all(f32[16,8,128]{2,1,0:T(8,128)S(1)} %bus_kernel.1), channel_id=1, replica_groups=mesh['line'=16,'out'=16] {'line'}, dimensions={0} | all-to-all | bytes 131072 | tf_op jit(solution)/shard_map/all_to_all | solution.py:291
  98.0 0.6 reduce_sum.19
  (27 shorter events, 0.7 us)
Async XLA Ops:
  3.1 3.1 %collective-permute-start = (f32[8,1024]{1,0:T(8,128)}, f32[8,1024]{1,0:T(8,128)S(1)}, u32[]{:S(2)}, u32[]{:S(2)}) collective-permute-start(f32[8,1024]{1,0:T(8,128)} %flows_kernel.1), channel_id=1, source_target_pairs={{0,8},{1,9},{2,10},{3,11},{4,12},{5,13},{6,14},{7,15},{8,0},{9,1},... | collective-permute-start | bytes 98312 | tf_op jit(solution)/shard_map/ppermute | solution.py:238
  6.9 2.8 %collective-permute-start.1 = (f32[8,1024]{1,0:T(8,128)S(1)}, f32[8,1024]{1,0:T(8,128)S(1)}, u32[]{:S(2)}, u32[]{:S(2)}) collective-permute-start(f32[8,1024]{1,0:T(8,128)S(1)} %add.42), channel_id=1, source_target_pairs={{0,1},{1,0},{2,3},{3,2},{4,5},{5,4},{6,7},{7,6},{8,9},{9,8},{10,11... | collective-permute-start | bytes 98312 | tf_op jit(solution)/shard_map/ppermute | solution.py:238
  9.7 4.3 %collective-permute-start.2 = (f32[8,1024]{1,0:T(8,128)S(1)}, f32[8,1024]{1,0:T(8,128)S(1)}, u32[]{:S(2)}, u32[]{:S(2)}) collective-permute-start(f32[8,1024]{1,0:T(8,128)S(1)} %add.43), channel_id=1, source_target_pairs={{0,2},{1,3},{2,0},{3,1},{4,6},{5,7},{6,4},{7,5},{8,10},{9,11},{10,... | collective-permute-start | bytes 98312 | tf_op jit(solution)/shard_map/ppermute | solution.py:238
  13.4 26.3 %copy-start.1 = (f32[1024,1024]{1,0:T(8,128)S(1)}, f32[1024,1024]{1,0:T(8,128)}, u32[]{:S(2)}) copy-start(f32[1024,1024]{1,0:T(8,128)} %factors_ref.2) | copy-start | bytes 12582916
  14.0 6.3 %collective-permute-start.3 = (f32[8,1024]{1,0:T(8,128)S(1)}, f32[8,1024]{1,0:T(8,128)S(1)}, u32[]{:S(2)}, u32[]{:S(2)}) collective-permute-start(f32[8,1024]{1,0:T(8,128)S(1)} %add.44), channel_id=1, source_target_pairs={{0,7},{1,6},{2,5},{3,4},{4,3},{5,2},{6,1},{7,0},{8,15},{9,14},{10,... | collective-permute-start | bytes 98312 | tf_op jit(solution)/shard_map/ppermute | solution.py:238
  20.7 6.2 %collective-permute-start.4 = (f32[8,1024]{1,0:T(8,128)S(1)}, f32[8,1024]{1,0:T(8,128)S(1)}, u32[]{:S(2)}, u32[]{:S(2)}) collective-permute-start(f32[8,1024]{1,0:T(8,128)S(1)} %select_kernel.1), channel_id=1, source_target_pairs={{0,16},{16,0},{32,48},{48,32},{64,80},{80,64},{96,112},{112,96},{1... | collective-permute-start | bytes 98312 | tf_op jit(solution)/shard_map/ppermute | solution.py:241
  26.9 4.9 %collective-permute-start.5 = (f32[8,1024]{1,0:T(8,128)S(1)}, f32[8,1024]{1,0:T(8,128)S(1)}, u32[]{:S(2)}, u32[]{:S(2)}) collective-permute-start(f32[8,1024]{1,0:T(8,128)S(1)} %add.47), channel_id=1, source_target_pairs={{0,144},{1,145},{2,146},{3,147},{4,148},{5,149},{6,150},{7,151},{8... | collective-permute-start | bytes 98312 | tf_op jit(solution)/shard_map/ppermute | solution.py:238
  31.8 4.6 %collective-permute-start.6 = (f32[8,1024]{1,0:T(8,128)S(1)}, f32[8,1024]{1,0:T(8,128)S(1)}, u32[]{:S(2)}, u32[]{:S(2)}) collective-permute-start(f32[8,1024]{1,0:T(8,128)S(1)} %add.48), channel_id=1, source_target_pairs={{0,112},{1,113},{2,114},{3,115},{4,116},{5,117},{6,118},{7,119},{8... | collective-permute-start | bytes 98312 | tf_op jit(solution)/shard_map/ppermute | solution.py:238
  36.4 3.3 %collective-permute-start.7 = (f32[8,1024]{1,0:T(8,128)S(1)}, f32[8,1024]{1,0:T(8,128)S(1)}, u32[]{:S(2)}, u32[]{:S(2)}) collective-permute-start(f32[8,1024]{1,0:T(8,128)S(1)} %add.49), channel_id=1, source_target_pairs={{0,48},{1,49},{2,50},{3,51},{4,52},{5,53},{6,54},{7,55},{8,56},{9,... | collective-permute-start | bytes 98312 | tf_op jit(solution)/shard_map/ppermute | solution.py:238
  50.0 30.8 %copy-start = (f32[1024,512]{1,0:T(8,128)S(1)}, f32[1024,512]{1,0:T(8,128)}, u32[]{:S(2)}) copy-start(f32[1024,512]{1,0:T(8,128)} %factors_ref.3) | copy-start | bytes 6291460
  50.0 1.4 %collective-permute-start.8 = (f32[8,1024]{1,0:T(8,128)S(1)}, f32[8,1024]{1,0:T(8,128)S(1)}, u32[]{:S(2)}, u32[]{:S(2)}) collective-permute-start(f32[8,1024]{1,0:T(8,128)S(1)} %get-tuple-element.18), channel_id=1, source_target_pairs={{0,16},{16,0},{32,48},{48,32},{64,80},{80,64},{96,112},{112,96},{1... | collective-permute-start | bytes 98312 | tf_op jit(solution)/shard_map/ppermute | solution.py:241
  65.4 2.9 %collective-permute-start.9 = (f32[8,1024]{1,0:T(8,128)S(1)}, f32[8,1024]{1,0:T(8,128)S(1)}, u32[]{:S(2)}, u32[]{:S(2)}) collective-permute-start(f32[8,1024]{1,0:T(8,128)S(1)} %place_kernel.1), channel_id=1, source_target_pairs={{0,8},{1,9},{2,10},{3,11},{4,12},{5,13},{6,14},{7,15},{8,0},{9,1},... | collective-permute-start | bytes 98312 | tf_op jit(solution)/shard_map/ppermute | solution.py:238
  68.2 2.8 %collective-permute-start.10 = (f32[8,1024]{1,0:T(8,128)S(1)}, f32[8,1024]{1,0:T(8,128)S(1)}, u32[]{:S(2)}, u32[]{:S(2)}) collective-permute-start(f32[8,1024]{1,0:T(8,128)S(1)} %add.52), channel_id=1, source_target_pairs={{0,1},{1,0},{2,3},{3,2},{4,5},{5,4},{6,7},{7,6},{8,9},{9,8},{10,11... | collective-permute-start | bytes 98312 | tf_op jit(solution)/shard_map/ppermute | solution.py:238
  71.1 3.7 %collective-permute-start.11 = (f32[8,1024]{1,0:T(8,128)S(1)}, f32[8,1024]{1,0:T(8,128)S(1)}, u32[]{:S(2)}, u32[]{:S(2)}) collective-permute-start(f32[8,1024]{1,0:T(8,128)S(1)} %add.53), channel_id=1, source_target_pairs={{0,2},{1,3},{2,0},{3,1},{4,6},{5,7},{6,4},{7,5},{8,10},{9,11},{10,... | collective-permute-start | bytes 98312 | tf_op jit(solution)/shard_map/ppermute | solution.py:238
  74.8 6.1 %collective-permute-start.12 = (f32[8,1024]{1,0:T(8,128)S(1)}, f32[8,1024]{1,0:T(8,128)S(1)}, u32[]{:S(2)}, u32[]{:S(2)}) collective-permute-start(f32[8,1024]{1,0:T(8,128)S(1)} %add.54), channel_id=1, source_target_pairs={{0,7},{1,6},{2,5},{3,4},{4,3},{5,2},{6,1},{7,0},{8,15},{9,14},{10,... | collective-permute-start | bytes 98312 | tf_op jit(solution)/shard_map/ppermute | solution.py:238

commit v5 on v4

--- a/solution.py
+++ b/solution.py
@@ -12,7 +12,7 @@
 LANES = 128
 SUB = 8
 TILES = 4
-CHUNKS = 4
+CHUNKS = 2
 VMEM = pl.BlockSpec(memory_space=pltpu.VMEM)
 FAR = pl.BlockSpec(memory_space=pltpu.HBM)
 
@@ -35,7 +35,7 @@
 
 def product(parts, right, dims):
     first, second, third = (
-        lax.dot_general(parts, part, dims, preferred_element_type=jnp.float32) for part in thirds(right)
+        lax.dot_general(parts, part, dims, preferred_element_type=jnp.float32) for part in right
     )
     h = parts.shape[0] // 4
     small = first[2 * h : 3 * h] + second[h : 2 * h] + third[:h]
@@ -57,11 +57,21 @@
     for c in range(chunks):
         copies[c].wait()
         here = slice(c * rows, (c + 1) * rows)
-        out_ref[:, here] = product(parts, factors[here, :], (((1,), (1,)), ((), ())))
+        out_ref[:, here] = product(parts, thirds(factors[here, :]), (((1,), (1,)), ((), ())))
+
+
+def copy_kernel(x_ref, out_ref):
+    out_ref[...] = x_ref[...]
+
+
+def thirds_kernel(x_ref, out_ref):
+    for part, third in enumerate(thirds(x_ref[...])):
+        out_ref[part] = third
 
 
 def bus_kernel(slopes_ref, factors_ref, out_ref):
-    terms = product(stacked(slopes_ref[...]), factors_ref[...], (((1,), (0,)), ((), ())))
+    parts = [factors_ref[part] for part in range(factors_ref.shape[0])]
+    terms = product(stacked(slopes_ref[...]), parts, (((1,), (0,)), ((), ())))
     pieces, hours, lanes = out_ref.shape
     own = terms.shape[1] // pieces
     out_ref[...] = jnp.zeros_like(out_ref)
@@ -234,8 +244,11 @@
     index = index.reshape(1, width)
     limits = jnp.broadcast_to((0.5 / SOFTNESS) * line_limits[:, None], (rows, LANES))
 
+    def moved(x, move):
+        return lax.ppermute(x, ("line", "out"), pairs_over((lines, outs), move))
+
     def add_move(x, move):
-        return x + lax.ppermute(x, ("line", "out"), pairs_over((lines, outs), move))
+        return x + moved(x, move)
 
     def other_core(x):
         return lax.ppermute(x, "line", [(i, i ^ 1) for i in range(lines)])
@@ -255,15 +268,19 @@
         ],
     )
     inverse = call(inverse_kernel, [(1, rows)], index, dtype=jnp.int32)
-    for move in over_out:
+    flows = call(copy_kernel, [(hours, rows)], flows) + moved(flows, over_out[0])
+    for move in over_out[1:]:
         flows = add_move(flows, move)
     flows, inverse, limits = lax.optimization_barrier((flows, inverse, limits))
     flow_out = call(select_kernel, [(hours, width)], flows, index)
     flow_out = flow_out + other_core(flow_out)
     flow_spread = call(spread_kernel, [(hours, rows, LANES)], flows, mib=16)
     flow_out, flow_spread = lax.optimization_barrier((flow_out, flow_spread))
-    for move in over_line:
+    for move in over_line[:-1]:
         flow_out = add_move(flow_out, move)
+    flow_out = add_move(flow_out, over_line[-1])
+    parts = call(thirds_kernel, [(3, rows, buses)], transfer_factors, dtype=jnp.bfloat16, mib=16)
+    flow_out, parts = lax.optimization_barrier((flow_out, parts))
     sums, column_part = call(
         overload_kernel,
         [(hours, rows, LANES), (hours, width)],
@@ -287,7 +304,7 @@
     slopes = call(place_kernel, [(hours, rows)], column_total, inverse, row_part)
     for move in over_out:
         slopes = add_move(slopes, move)
-    pieces = call(bus_kernel, [(lines, hours, LANES)], slopes, transfer_factors, mib=16)
+    pieces = call(bus_kernel, [(lines, hours, LANES)], slopes, parts, mib=16)
     gradient = lax.all_to_all(pieces, "line", 0, 0, tiled=True).sum(0)
     return gradient[:, : buses // lines]
 

time: 98.9 us -> 97.9 us (0.990)
  waiting for transfers between devices: 22.4 us -> 21 us
    ppermute x11, waiting for transfers between devices: 22.4 us -> 21 us  [moved(): return lax.ppermute(x, ('line', 'out'), pairs_over((lines, outs), move))]
    pallas_call x8 -> x10, Pallas kernels: 17.6 us -> 17.8 us  [call(): pl.pallas_call(kernel, out_shape=out_shape, in_specs=[FAR] * far + [VMEM]...]
  transfers between devices with their start and end apart: 13 -> 13, of which waited for: 10 -> 10; matrix products, arithmetic and copies ran while one was open for 1% -> 1% of each run, Pallas kernels for 3% -> 4%
where the time goes in v5:
time: 97.9 us; the launch traced here: 97.6 us
  blocking collectives  30 us (31%)
  starting transfers between devices  25.5 us (26%)
  waiting for transfers between devices  21 us (21%)
  Pallas kernels  17.8 us (18%)
  other arithmetic  2.08 us (2%)
  local copies, waits for them, and re-layouts  1.01 us (1%)
    ppermute x11, waiting for transfers between devices, moved(): return lax.ppermute(x, ('line', 'out'), pairs_over((lines, outs), move))  21 us
    ppermute x11, starting transfers between devices, moved(): return lax.ppermute(x, ('line', 'out'), pairs_over((lines, outs), move))  20.2 us
    pallas_call x10, Pallas kernels, call(): pl.pallas_call(kernel, out_shape=out_shape, in_specs=[FAR] * far + [VMEM]...  17.8 us
    all_to_all x1, blocking collectives, local(): gradient = lax.all_to_all(pieces, 'line', 0, 0, tiled=True).sum(0)  16.3 us
    all_to_all x1, blocking collectives, local(): lax.all_to_all(copies, 'line', 0, 0, axis_index_groups=[list(range(c, lin...  13.7 us
    ppermute x2, starting transfers between devices, other_core(): return lax.ppermute(x, 'line', [(i, i ^ 1) for i in range(lines)])  5.27 us
  transfers between devices with their start and end apart: 13, of which 10 were waited for; matrix products, arithmetic and copies ran while one was open for 1% of the time, Pallas kernels for 4%

profile of v5, /device:TPU:33, one launch (start us, length us, event | category | flops | bytes accessed | tf_op | source)
XLA Modules:
  0.0 97.6 jit_solution(9907174777406312324)
XLA Ops:
  0.0 3.0 %flows_kernel.1.x_ref = f32[8,1024]{1,0:T(8,128)} custom-call(f32[8,512]{1,0:T(8,128)} %injections_hbm.1, f32[1024,512]{1,0:T(8,128)} %x_ref.1), custom_call_target="tpu_custom_call" | custom-call | bytes 2113536 | tf_op jit(solution)/shard_map/flows_kernel/pallas_call | solution.py:188
  3.0 1.3 %collective-permute-start = (f32[8,1024]{1,0:T(8,128)}, f32[8,1024]{1,0:T(8,128)S(1)}, u32[]{:S(2)}, u32[]{:S(2)}) collective-permute-start(f32[8,1024]{1,0:T(8,128)} %flows_kernel.1.x_ref), channel_id=1, source_target_pairs={{0,8},{1,9},{2,10},{3,11},{4,12},{5,13},{6,14},{7,15},{8,0},{9,1},... | collective-permute-start | bytes 98312 | tf_op jit(solution)/shard_map/ppermute | solution.py:248
  4.3 0.8 copy-done.2
  5.1 1.0 collective-permute-done
  6.1 2.8 %collective-permute-done.1 = f32[8,1024]{1,0:T(8,128)S(1)} collective-permute-done((f32[8,1024]{1,0:T(8,128)S(1)}, f32[8,1024]{1,0:T(8,128)S(1)}, u32[]{:S(2)}, u32[]{:S(2)}) %collective-permute-start.1) | collective-permute-done | bytes 32800 | tf_op jit(solution)/shard_map/ppermute | solution.py:248
  8.9 3.0 %collective-permute-start.2 = (f32[8,1024]{1,0:T(8,128)S(1)}, f32[8,1024]{1,0:T(8,128)S(1)}, u32[]{:S(2)}, u32[]{:S(2)}) collective-permute-start(f32[8,1024]{1,0:T(8,128)S(1)} %add.43), channel_id=1, source_target_pairs={{0,2},{1,3},{2,0},{3,1},{4,6},{5,7},{6,4},{7,5},{8,10},{9,11},{10,... | collective-permute-start | bytes 98312 | tf_op jit(solution)/shard_map/ppermute | solution.py:248
  11.9 0.7 broadcast_multiply_fusion
  12.6 0.6 collective-permute-done.2
  13.2 4.9 %collective-permute-start.3 = (f32[8,1024]{1,0:T(8,128)S(1)}, f32[8,1024]{1,0:T(8,128)S(1)}, u32[]{:S(2)}, u32[]{:S(2)}) collective-permute-start(f32[8,1024]{1,0:T(8,128)S(1)} %add.44), channel_id=1, source_target_pairs={{0,7},{1,6},{2,5},{3,4},{4,3},{5,2},{6,1},{7,0},{8,15},{9,14},{10,... | collective-permute-start | bytes 98312 | tf_op jit(solution)/shard_map/ppermute | solution.py:248
  18.1 0.7 dynamic-slice_subtract_fusion
  18.8 0.7 inverse_kernel.1.index_ref
  19.9 5.0 %collective-permute-start.4 = (f32[8,1024]{1,0:T(8,128)S(1)}, f32[8,1024]{1,0:T(8,128)S(1)}, u32[]{:S(2)}, u32[]{:S(2)}) collective-permute-start(f32[8,1024]{1,0:T(8,128)S(1)} %select_kernel.1), channel_id=1, source_target_pairs={{0,16},{16,0},{32,48},{48,32},{64,80},{80,64},{96,112},{112,96},{1... | collective-permute-start | bytes 98312 | tf_op jit(solution)/shard_map/ppermute | solution.py:254
  24.9 1.1 %spread_kernel.1.flow_ref = f32[8,1024,128]{2,1,0:T(8,128)S(1)} custom-call(f32[8,1024]{1,0:T(8,128)S(1)} %add.45.values_ref.flow_ref), custom_call_target="tpu_custom_call" | custom-call | bytes 32768 | tf_op jit(solution)/shard_map/spread_kernel/pallas_call | solution.py:188
  26.0 2.7 %collective-permute-start.5 = (f32[8,1024]{1,0:T(8,128)S(1)}, f32[8,1024]{1,0:T(8,128)S(1)}, u32[]{:S(2)}, u32[]{:S(2)}) collective-permute-start(f32[8,1024]{1,0:T(8,128)S(1)} %add.47), channel_id=1, source_target_pairs={{0,144},{1,145},{2,146},{3,147},{4,148},{5,149},{6,150},{7,151},{8... | collective-permute-start | bytes 98312 | tf_op jit(solution)/shard_map/ppermute | solution.py:248
  28.8 2.2 %collective-permute-done.5 = f32[8,1024]{1,0:T(8,128)S(1)} collective-permute-done((f32[8,1024]{1,0:T(8,128)S(1)}, f32[8,1024]{1,0:T(8,128)S(1)}, u32[]{:S(2)}, u32[]{:S(2)}) %collective-permute-start.5) | collective-permute-done | bytes 32800 | tf_op jit(solution)/shard_map/ppermute | solution.py:248
  31.0 2.6 %collective-permute-start.6 = (f32[8,1024]{1,0:T(8,128)S(1)}, f32[8,1024]{1,0:T(8,128)S(1)}, u32[]{:S(2)}, u32[]{:S(2)}) collective-permute-start(f32[8,1024]{1,0:T(8,128)S(1)} %add.48), channel_id=1, source_target_pairs={{0,112},{1,113},{2,114},{3,115},{4,116},{5,117},{6,118},{7,119},{8... | collective-permute-start | bytes 98312 | tf_op jit(solution)/shard_map/ppermute | solution.py:248
  33.6 1.9 %collective-permute-done.6 = f32[8,1024]{1,0:T(8,128)S(1)} collective-permute-done((f32[8,1024]{1,0:T(8,128)S(1)}, f32[8,1024]{1,0:T(8,128)S(1)}, u32[]{:S(2)}, u32[]{:S(2)}) %collective-permute-start.6) | collective-permute-done | bytes 32800 | tf_op jit(solution)/shard_map/ppermute | solution.py:248
  35.6 0.5 thirds_kernel.1.factors_ref
  36.1 2.8 %collective-permute-done.7 = f32[8,1024]{1,0:T(8,128)S(1)} collective-permute-done((f32[8,1024]{1,0:T(8,128)S(1)}, f32[8,1024]{1,0:T(8,128)S(1)}, u32[]{:S(2)}, u32[]{:S(2)}) %collective-permute-start.7) | collective-permute-done | bytes 32800 | tf_op jit(solution)/shard_map/ppermute | solution.py:248
  38.9 10.3 %overload_kernel.1 = (f32[8,1024,128]{2,1,0:T(8,128)S(1)}, f32[8,1024]{1,0:T(8,128)S(1)}) custom-call(f32[1024,1024]{1,0:T(8,128)S(1)} %copy-done.1, f32[8,1024,128]{2,1,0:T(8,128)S(1)} %spread_kernel.1.flow_ref, f32[1024,128]{1,0:T(8,128)S(1)} %broadcast_in_dim.4.limit_ref, f32[8,1024]{1,0:T(8,128)S(1)} %add.50.out_flow_ref), custom_call_target="tpu_custom_call" | custom-call | bytes 8945664 | tf_op jit(solution)/shard_map/overload_kernel/pallas_call | solution.py:188
  49.5 1.1 %row_kernel.1.rows_ref = f32[8,1024]{1,0:T(8,128)S(1)} custom-call(f32[8,1024,128]{2,1,0:T(8,128)S(1)} %get-tuple-element.22.sums_ref), custom_call_target="tpu_custom_call" | custom-call | bytes 4194304 | tf_op jit(solution)/shard_map/row_kernel/pallas_call | solution.py:188
  50.7 13.7 %all_to_all.10 = f32[8,8,1024]{2,1,0:T(8,128)S(1)} all-to-all(f32[8,8,1024]{2,1,0:T(8,128)S(1)} %broadcast_in_dim.10), channel_id=1, replica_groups={{0,32,64,96,128,160,192,224},{16,48,80,112,144,176,208,240},{1,33,65,97..., dimensions={0} | all-to-all | bytes 524288 | tf_op jit(solution)/shard_map/all_to_all | solution.py:301
  64.6 0.4 collective-permute-start.9
  65.0 2.5 %collective-permute-done.9 = f32[8,1024]{1,0:T(8,128)S(1)} collective-permute-done((f32[8,1024]{1,0:T(8,128)S(1)}, f32[8,1024]{1,0:T(8,128)S(1)}, u32[]{:S(2)}, u32[]{:S(2)}) %collective-permute-start.9) | collective-permute-done | bytes 32800 | tf_op jit(solution)/shard_map/ppermute | solution.py:248
  67.4 2.8 %collective-permute-done.10 = f32[8,1024]{1,0:T(8,128)S(1)} collective-permute-done((f32[8,1024]{1,0:T(8,128)S(1)}, f32[8,1024]{1,0:T(8,128)S(1)}, u32[]{:S(2)}, u32[]{:S(2)}) %collective-permute-start.10) | collective-permute-done | bytes 32800 | tf_op jit(solution)/shard_map/ppermute | solution.py:248
  70.3 0.5 collective-permute-start.11
  70.7 3.2 %collective-permute-done.11 = f32[8,1024]{1,0:T(8,128)S(1)} collective-permute-done((f32[8,1024]{1,0:T(8,128)S(1)}, f32[8,1024]{1,0:T(8,128)S(1)}, u32[]{:S(2)}, u32[]{:S(2)}) %collective-permute-start.11) | collective-permute-done | bytes 32800 | tf_op jit(solution)/shard_map/ppermute | solution.py:248
  73.9 4.8 %collective-permute-start.12 = (f32[8,1024]{1,0:T(8,128)S(1)}, f32[8,1024]{1,0:T(8,128)S(1)}, u32[]{:S(2)}, u32[]{:S(2)}) collective-permute-start(f32[8,1024]{1,0:T(8,128)S(1)} %add.54), channel_id=1, source_target_pairs={{0,7},{1,6},{2,5},{3,4},{4,3},{5,2},{6,1},{7,0},{8,15},{9,14},{10,... | collective-permute-start | bytes 98312 | tf_op jit(solution)/shard_map/ppermute | solution.py:248
  78.7 1.3 %collective-permute-done.12 = f32[8,1024]{1,0:T(8,128)S(1)} collective-permute-done((f32[8,1024]{1,0:T(8,128)S(1)}, f32[8,1024]{1,0:T(8,128)S(1)}, u32[]{:S(2)}, u32[]{:S(2)}) %collective-permute-start.12) | collective-permute-done | bytes 32800 | tf_op jit(solution)/shard_map/ppermute | solution.py:248
  80.0 0.7 bus_kernel.1
  80.7 16.3 %all_to_all.11 = f32[16,8,128]{2,1,0:T(8,128)S(1)} all-to-all(f32[16,8,128]{2,1,0:T(8,128)S(1)} %bus_kernel.1), channel_id=1, replica_groups=mesh['line'=16,'out'=16] {'line'}, dimensions={0} | all-to-all | bytes 131072 | tf_op jit(solution)/shard_map/all_to_all | solution.py:308
  97.0 0.6 reduce_sum.19
  (31 shorter events, 0.9 us)
Async XLA Ops:
  3.0 3.1 %collective-permute-start = (f32[8,1024]{1,0:T(8,128)}, f32[8,1024]{1,0:T(8,128)S(1)}, u32[]{:S(2)}, u32[]{:S(2)}) collective-permute-start(f32[8,1024]{1,0:T(8,128)} %flows_kernel.1.x_ref), channel_id=1, source_target_pairs={{0,8},{1,9},{2,10},{3,11},{4,12},{5,13},{6,14},{7,15},{8,0},{9,1},... | collective-permute-start | bytes 98312 | tf_op jit(solution)/shard_map/ppermute | solution.py:248
  4.3 0.8 copy-start.2
  6.1 2.8 %collective-permute-start.1 = (f32[8,1024]{1,0:T(8,128)S(1)}, f32[8,1024]{1,0:T(8,128)S(1)}, u32[]{:S(2)}, u32[]{:S(2)}) collective-permute-start(f32[8,1024]{1,0:T(8,128)S(1)} %add.42), channel_id=1, source_target_pairs={{0,1},{1,0},{2,3},{3,2},{4,5},{5,4},{6,7},{7,6},{8,9},{9,8},{10,11... | collective-permute-start | bytes 98312 | tf_op jit(solution)/shard_map/ppermute | solution.py:248
  8.9 4.3 %collective-permute-start.2 = (f32[8,1024]{1,0:T(8,128)S(1)}, f32[8,1024]{1,0:T(8,128)S(1)}, u32[]{:S(2)}, u32[]{:S(2)}) collective-permute-start(f32[8,1024]{1,0:T(8,128)S(1)} %add.43), channel_id=1, source_target_pairs={{0,2},{1,3},{2,0},{3,1},{4,6},{5,7},{6,4},{7,5},{8,10},{9,11},{10,... | collective-permute-start | bytes 98312 | tf_op jit(solution)/shard_map/ppermute | solution.py:248
  12.6 23.0 %copy-start = (f32[1024,512]{1,0:T(8,128)S(1)}, f32[1024,512]{1,0:T(8,128)}, u32[]{:S(2)}) copy-start(f32[1024,512]{1,0:T(8,128)} %x_ref.1) | copy-start | bytes 6291460
  13.2 6.3 %collective-permute-start.3 = (f32[8,1024]{1,0:T(8,128)S(1)}, f32[8,1024]{1,0:T(8,128)S(1)}, u32[]{:S(2)}, u32[]{:S(2)}) collective-permute-start(f32[8,1024]{1,0:T(8,128)S(1)} %add.44), channel_id=1, source_target_pairs={{0,7},{1,6},{2,5},{3,4},{4,3},{5,2},{6,1},{7,0},{8,15},{9,14},{10,... | collective-permute-start | bytes 98312 | tf_op jit(solution)/shard_map/ppermute | solution.py:248
  19.9 19.0 %copy-start.1 = (f32[1024,1024]{1,0:T(8,128)S(1)}, f32[1024,1024]{1,0:T(8,128)}, u32[]{:S(2)}) copy-start(f32[1024,1024]{1,0:T(8,128)} %factors_ref.1) | copy-start | bytes 12582916
  19.9 6.2 %collective-permute-start.4 = (f32[8,1024]{1,0:T(8,128)S(1)}, f32[8,1024]{1,0:T(8,128)S(1)}, u32[]{:S(2)}, u32[]{:S(2)}) collective-permute-start(f32[8,1024]{1,0:T(8,128)S(1)} %select_kernel.1), channel_id=1, source_target_pairs={{0,16},{16,0},{32,48},{48,32},{64,80},{80,64},{96,112},{112,96},{1... | collective-permute-start | bytes 98312 | tf_op jit(solution)/shard_map/ppermute | solution.py:254
  26.0 4.9 %collective-permute-start.5 = (f32[8,1024]{1,0:T(8,128)S(1)}, f32[8,1024]{1,0:T(8,128)S(1)}, u32[]{:S(2)}, u32[]{:S(2)}) collective-permute-start(f32[8,1024]{1,0:T(8,128)S(1)} %add.47), channel_id=1, source_target_pairs={{0,144},{1,145},{2,146},{3,147},{4,148},{5,149},{6,150},{7,151},{8... | collective-permute-start | bytes 98312 | tf_op jit(solution)/shard_map/ppermute | solution.py:248
  31.0 4.6 %collective-permute-start.6 = (f32[8,1024]{1,0:T(8,128)S(1)}, f32[8,1024]{1,0:T(8,128)S(1)}, u32[]{:S(2)}, u32[]{:S(2)}) collective-permute-start(f32[8,1024]{1,0:T(8,128)S(1)} %add.48), channel_id=1, source_target_pairs={{0,112},{1,113},{2,114},{3,115},{4,116},{5,117},{6,118},{7,119},{8... | collective-permute-start | bytes 98312 | tf_op jit(solution)/shard_map/ppermute | solution.py:248
  35.5 3.3 %collective-permute-start.7 = (f32[8,1024]{1,0:T(8,128)S(1)}, f32[8,1024]{1,0:T(8,128)S(1)}, u32[]{:S(2)}, u32[]{:S(2)}) collective-permute-start(f32[8,1024]{1,0:T(8,128)S(1)} %add.49), channel_id=1, source_target_pairs={{0,48},{1,49},{2,50},{3,51},{4,52},{5,53},{6,54},{7,55},{8,56},{9,... | collective-permute-start | bytes 98312 | tf_op jit(solution)/shard_map/ppermute | solution.py:248
  49.2 1.4 %collective-permute-start.8 = (f32[8,1024]{1,0:T(8,128)S(1)}, f32[8,1024]{1,0:T(8,128)S(1)}, u32[]{:S(2)}, u32[]{:S(2)}) collective-permute-start(f32[8,1024]{1,0:T(8,128)S(1)} %get-tuple-element.21), channel_id=1, source_target_pairs={{0,16},{16,0},{32,48},{48,32},{64,80},{80,64},{96,112},{112,96},{1... | collective-permute-start | bytes 98312 | tf_op jit(solution)/shard_map/ppermute | solution.py:254
  64.6 2.9 %collective-permute-start.9 = (f32[8,1024]{1,0:T(8,128)S(1)}, f32[8,1024]{1,0:T(8,128)S(1)}, u32[]{:S(2)}, u32[]{:S(2)}) collective-permute-start(f32[8,1024]{1,0:T(8,128)S(1)} %place_kernel.1), channel_id=1, source_target_pairs={{0,8},{1,9},{2,10},{3,11},{4,12},{5,13},{6,14},{7,15},{8,0},{9,1},... | collective-permute-start | bytes 98312 | tf_op jit(solution)/shard_map/ppermute | solution.py:248
  67.4 2.8 %collective-permute-start.10 = (f32[8,1024]{1,0:T(8,128)S(1)}, f32[8,1024]{1,0:T(8,128)S(1)}, u32[]{:S(2)}, u32[]{:S(2)}) collective-permute-start(f32[8,1024]{1,0:T(8,128)S(1)} %add.52), channel_id=1, source_target_pairs={{0,1},{1,0},{2,3},{3,2},{4,5},{5,4},{6,7},{7,6},{8,9},{9,8},{10,11... | collective-permute-start | bytes 98312 | tf_op jit(solution)/shard_map/ppermute | solution.py:248
  70.3 3.7 %collective-permute-start.11 = (f32[8,1024]{1,0:T(8,128)S(1)}, f32[8,1024]{1,0:T(8,128)S(1)}, u32[]{:S(2)}, u32[]{:S(2)}) collective-permute-start(f32[8,1024]{1,0:T(8,128)S(1)} %add.53), channel_id=1, source_target_pairs={{0,2},{1,3},{2,0},{3,1},{4,6},{5,7},{6,4},{7,5},{8,10},{9,11},{10,... | collective-permute-start | bytes 98312 | tf_op jit(solution)/shard_map/ppermute | solution.py:248
  73.9 6.1 %collective-permute-start.12 = (f32[8,1024]{1,0:T(8,128)S(1)}, f32[8,1024]{1,0:T(8,128)S(1)}, u32[]{:S(2)}, u32[]{:S(2)}) collective-permute-start(f32[8,1024]{1,0:T(8,128)S(1)} %add.54), channel_id=1, source_target_pairs={{0,7},{1,6},{2,5},{3,4},{4,3},{5,2},{6,1},{7,0},{8,15},{9,14},{10,... | collective-permute-start | bytes 98312 | tf_op jit(solution)/shard_map/ppermute | solution.py:248

commit v6 on v5

--- a/solution.py
+++ b/solution.py
@@ -79,7 +79,11 @@
         out_ref[p, :, :own] = terms[:, p * own : (p + 1) * own]
 
 
-def inverse_kernel(index_ref, out_ref):
+def inverse_kernel(index_ref, limit_ref, out_ref, limit_out_ref):
+    for lb in range(limit_out_ref.shape[0] // LANES):
+        here = slice(lb * LANES, (lb + 1) * LANES)
+        limit = (0.5 / SOFTNESS) * limit_ref[:, here]
+        limit_out_ref[here, :] = jnp.transpose(jnp.broadcast_to(limit, (LANES, LANES)))
     width = index_ref.shape[1]
     lane = lax.broadcasted_iota(jnp.int32, (LANES, LANES), 1)
     row = lax.broadcasted_iota(jnp.int32, (LANES, LANES), 0)
@@ -184,7 +188,8 @@
 
 def call(kernel, shape, *operands, dtype=jnp.float32, mib=8, far=0, scratch=()):
     size = sum(a.size * 4 for a in operands)
-    out_shape = [jax.ShapeDtypeStruct(s, dtype) for s in shape]
+    kinds = dtype if isinstance(dtype, tuple) else [dtype] * len(shape)
+    out_shape = [jax.ShapeDtypeStruct(s, kind) for s, kind in zip(shape, kinds)]
     result = pl.pallas_call(
         kernel,
         out_shape=out_shape,
@@ -242,7 +247,6 @@
     out_start = lax.axis_index("out") * width
     index = lax.dynamic_slice_in_dim(outage_lines, out_start, width, 0) - line * rows
     index = index.reshape(1, width)
-    limits = jnp.broadcast_to((0.5 / SOFTNESS) * line_limits[:, None], (rows, LANES))
 
     def moved(x, move):
         return lax.ppermute(x, ("line", "out"), pairs_over((lines, outs), move))
@@ -267,7 +271,13 @@
             pltpu.SemaphoreType.DMA((CHUNKS + 1,)),
         ],
     )
-    inverse = call(inverse_kernel, [(1, rows)], index, dtype=jnp.int32)
+    inverse, limits = call(
+        inverse_kernel,
+        [(1, rows), (rows, LANES)],
+        index,
+        line_limits.reshape(1, rows),
+        dtype=(jnp.int32, jnp.float32),
+    )
     flows = call(copy_kernel, [(hours, rows)], flows) + moved(flows, over_out[0])
     for move in over_out[1:]:
         flows = add_move(flows, move)

time: 97.9 us -> 98 us (level)
  no operation moved by 1% of the time
where the time goes in v6:
time: 98 us; the launch traced here: 97.7 us
  blocking collectives  30.2 us (31%)
  starting transfers between devices  24.6 us (25%)
  waiting for transfers between devices  21.8 us (22%)
  Pallas kernels  18 us (18%)
  local copies, waits for them, and re-layouts  1.51 us (2%)
  other arithmetic  1.39 us (1%)
    ppermute x11, waiting for transfers between devices, moved(): return lax.ppermute(x, ('line', 'out'), pairs_over((lines, outs), move))  21.8 us
    ppermute x11, starting transfers between devices, moved(): return lax.ppermute(x, ('line', 'out'), pairs_over((lines, outs), move))  19.8 us
    pallas_call x10, Pallas kernels, call(): pl.pallas_call(kernel, out_shape=out_shape, in_specs=[FAR] * far + [VMEM]...  18 us
    all_to_all x1, blocking collectives, local(): gradient = lax.all_to_all(pieces, 'line', 0, 0, tiled=True).sum(0)  16.6 us
    all_to_all x1, blocking collectives, local(): lax.all_to_all(copies, 'line', 0, 0, axis_index_groups=[list(range(c, lin...  13.7 us
    ppermute x2, starting transfers between devices, other_core(): return lax.ppermute(x, 'line', [(i, i ^ 1) for i in range(lines)])  4.75 us
  transfers between devices with their start and end apart: 13, of which 10 were waited for; matrix products, arithmetic and copies ran while one was open for 1% of the time, Pallas kernels for 4%

profile of v6, /device:TPU:33, one launch (start us, length us, event | category | flops | bytes accessed | tf_op | source)
XLA Modules:
  0.0 97.7 jit_solution(13629212229900646964)
XLA Ops:
  0.0 3.0 %flows_kernel.1.x_ref = f32[8,1024]{1,0:T(8,128)} custom-call(f32[8,512]{1,0:T(8,128)} %injections_hbm.1, f32[1024,512]{1,0:T(8,128)} %x_ref.1), custom_call_target="tpu_custom_call" | custom-call | bytes 2113536 | tf_op jit(solution)/shard_map/flows_kernel/pallas_call | solution.py:193
  3.0 1.3 %collective-permute-start = (f32[8,1024]{1,0:T(8,128)}, f32[8,1024]{1,0:T(8,128)S(1)}, u32[]{:S(2)}, u32[]{:S(2)}) collective-permute-start(f32[8,1024]{1,0:T(8,128)} %flows_kernel.1.x_ref), channel_id=1, source_target_pairs={{0,8},{1,9},{2,10},{3,11},{4,12},{5,13},{6,14},{7,15},{8,0},{9,1},... | collective-permute-start | bytes 98312 | tf_op jit(solution)/shard_map/ppermute | solution.py:252
  4.3 0.8 copy-done.2
  5.1 1.0 collective-permute-done
  6.1 2.8 %collective-permute-done.1 = f32[8,1024]{1,0:T(8,128)S(1)} collective-permute-done((f32[8,1024]{1,0:T(8,128)S(1)}, f32[8,1024]{1,0:T(8,128)S(1)}, u32[]{:S(2)}, u32[]{:S(2)}) %collective-permute-start.1) | collective-permute-done | bytes 32800 | tf_op jit(solution)/shard_map/ppermute | solution.py:252
  8.9 3.0 %collective-permute-start.2 = (f32[8,1024]{1,0:T(8,128)S(1)}, f32[8,1024]{1,0:T(8,128)S(1)}, u32[]{:S(2)}, u32[]{:S(2)}) collective-permute-start(f32[8,1024]{1,0:T(8,128)S(1)} %add.43), channel_id=1, source_target_pairs={{0,2},{1,3},{2,0},{3,1},{4,6},{5,7},{6,4},{7,5},{8,10},{9,11},{10,... | collective-permute-start | bytes 98312 | tf_op jit(solution)/shard_map/ppermute | solution.py:252
  11.9 1.3 %collective-permute-done.2 = f32[8,1024]{1,0:T(8,128)S(1)} collective-permute-done((f32[8,1024]{1,0:T(8,128)S(1)}, f32[8,1024]{1,0:T(8,128)S(1)}, u32[]{:S(2)}, u32[]{:S(2)}) %collective-permute-start.2) | collective-permute-done | bytes 32800 | tf_op jit(solution)/shard_map/ppermute | solution.py:252
  13.2 4.9 %collective-permute-start.3 = (f32[8,1024]{1,0:T(8,128)S(1)}, f32[8,1024]{1,0:T(8,128)S(1)}, u32[]{:S(2)}, u32[]{:S(2)}) collective-permute-start(f32[8,1024]{1,0:T(8,128)S(1)} %add.44), channel_id=1, source_target_pairs={{0,7},{1,6},{2,5},{3,4},{4,3},{5,2},{6,1},{7,0},{8,15},{9,14},{10,... | collective-permute-start | bytes 98312 | tf_op jit(solution)/shard_map/ppermute | solution.py:252
  18.1 0.7 dynamic-slice_subtract_fusion
  18.8 0.7 copy-done.3
  19.5 0.8 inverse_kernel.1
  20.5 4.5 %collective-permute-start.4 = (f32[8,1024]{1,0:T(8,128)S(1)}, f32[8,1024]{1,0:T(8,128)S(1)}, u32[]{:S(2)}, u32[]{:S(2)}) collective-permute-start(f32[8,1024]{1,0:T(8,128)S(1)} %select_kernel.1), channel_id=1, source_target_pairs={{0,16},{16,0},{32,48},{48,32},{64,80},{80,64},{96,112},{112,96},{1... | collective-permute-start | bytes 98312 | tf_op jit(solution)/shard_map/ppermute | solution.py:258
  25.0 1.1 %spread_kernel.1.flow_ref = f32[8,1024,128]{2,1,0:T(8,128)S(1)} custom-call(f32[8,1024]{1,0:T(8,128)S(1)} %add.45.values_ref.flow_ref), custom_call_target="tpu_custom_call" | custom-call | bytes 32768 | tf_op jit(solution)/shard_map/spread_kernel/pallas_call | solution.py:193
  26.2 2.7 %collective-permute-start.5 = (f32[8,1024]{1,0:T(8,128)S(1)}, f32[8,1024]{1,0:T(8,128)S(1)}, u32[]{:S(2)}, u32[]{:S(2)}) collective-permute-start(f32[8,1024]{1,0:T(8,128)S(1)} %add.47), channel_id=1, source_target_pairs={{0,144},{1,145},{2,146},{3,147},{4,148},{5,149},{6,150},{7,151},{8... | collective-permute-start | bytes 98312 | tf_op jit(solution)/shard_map/ppermute | solution.py:252
  28.9 2.2 %collective-permute-done.5 = f32[8,1024]{1,0:T(8,128)S(1)} collective-permute-done((f32[8,1024]{1,0:T(8,128)S(1)}, f32[8,1024]{1,0:T(8,128)S(1)}, u32[]{:S(2)}, u32[]{:S(2)}) %collective-permute-start.5) | collective-permute-done | bytes 32800 | tf_op jit(solution)/shard_map/ppermute | solution.py:252
  31.1 2.6 %collective-permute-start.6 = (f32[8,1024]{1,0:T(8,128)S(1)}, f32[8,1024]{1,0:T(8,128)S(1)}, u32[]{:S(2)}, u32[]{:S(2)}) collective-permute-start(f32[8,1024]{1,0:T(8,128)S(1)} %add.48), channel_id=1, source_target_pairs={{0,112},{1,113},{2,114},{3,115},{4,116},{5,117},{6,118},{7,119},{8... | collective-permute-start | bytes 98312 | tf_op jit(solution)/shard_map/ppermute | solution.py:252
  33.7 1.9 %collective-permute-done.6 = f32[8,1024]{1,0:T(8,128)S(1)} collective-permute-done((f32[8,1024]{1,0:T(8,128)S(1)}, f32[8,1024]{1,0:T(8,128)S(1)}, u32[]{:S(2)}, u32[]{:S(2)}) %collective-permute-start.6) | collective-permute-done | bytes 32800 | tf_op jit(solution)/shard_map/ppermute | solution.py:252
  35.7 0.5 thirds_kernel.1.factors_ref
  36.2 2.8 %collective-permute-done.7 = f32[8,1024]{1,0:T(8,128)S(1)} collective-permute-done((f32[8,1024]{1,0:T(8,128)S(1)}, f32[8,1024]{1,0:T(8,128)S(1)}, u32[]{:S(2)}, u32[]{:S(2)}) %collective-permute-start.7) | collective-permute-done | bytes 32800 | tf_op jit(solution)/shard_map/ppermute | solution.py:252
  39.0 10.3 %overload_kernel.1 = (f32[8,1024,128]{2,1,0:T(8,128)S(1)}, f32[8,1024]{1,0:T(8,128)S(1)}) custom-call(f32[1024,1024]{1,0:T(8,128)S(1)} %copy-done.1, f32[8,1024,128]{2,1,0:T(8,128)S(1)} %spread_kernel.1.flow_ref, f32[1024,128]{1,0:T(8,128)S(1)} %get-tuple-element.22.limit_ref, f32[8,1024]{1,0:T(8,128)S(1)} %add.50.out_flow_ref), custom_call_target="tpu_custom_call" | custom-call | bytes 8945664 | tf_op jit(solution)/shard_map/overload_kernel/pallas_call | solution.py:193
  49.6 1.1 %row_kernel.1.rows_ref = f32[8,1024]{1,0:T(8,128)S(1)} custom-call(f32[8,1024,128]{2,1,0:T(8,128)S(1)} %get-tuple-element.26.sums_ref), custom_call_target="tpu_custom_call" | custom-call | bytes 4194304 | tf_op jit(solution)/shard_map/row_kernel/pallas_call | solution.py:193
  50.8 13.7 %all_to_all.10 = f32[8,8,1024]{2,1,0:T(8,128)S(1)} all-to-all(f32[8,8,1024]{2,1,0:T(8,128)S(1)} %broadcast_in_dim.3), channel_id=1, replica_groups={{0,32,64,96,128,160,192,224},{16,48,80,112,144,176,208,240},{1,33,65,97..., dimensions={0} | all-to-all | bytes 524288 | tf_op jit(solution)/shard_map/all_to_all | solution.py:311
  64.7 0.4 collective-permute-start.9
  65.1 2.5 %collective-permute-done.9 = f32[8,1024]{1,0:T(8,128)S(1)} collective-permute-done((f32[8,1024]{1,0:T(8,128)S(1)}, f32[8,1024]{1,0:T(8,128)S(1)}, u32[]{:S(2)}, u32[]{:S(2)}) %collective-permute-start.9) | collective-permute-done | bytes 32800 | tf_op jit(solution)/shard_map/ppermute | solution.py:252
  67.5 2.8 %collective-permute-done.10 = f32[8,1024]{1,0:T(8,128)S(1)} collective-permute-done((f32[8,1024]{1,0:T(8,128)S(1)}, f32[8,1024]{1,0:T(8,128)S(1)}, u32[]{:S(2)}, u32[]{:S(2)}) %collective-permute-start.10) | collective-permute-done | bytes 32800 | tf_op jit(solution)/shard_map/ppermute | solution.py:252
  70.4 0.4 collective-permute-start.11
  70.7 3.3 %collective-permute-done.11 = f32[8,1024]{1,0:T(8,128)S(1)} collective-permute-done((f32[8,1024]{1,0:T(8,128)S(1)}, f32[8,1024]{1,0:T(8,128)S(1)}, u32[]{:S(2)}, u32[]{:S(2)}) %collective-permute-start.11) | collective-permute-done | bytes 32800 | tf_op jit(solution)/shard_map/ppermute | solution.py:252
  74.0 4.5 %collective-permute-start.12 = (f32[8,1024]{1,0:T(8,128)S(1)}, f32[8,1024]{1,0:T(8,128)S(1)}, u32[]{:S(2)}, u32[]{:S(2)}) collective-permute-start(f32[8,1024]{1,0:T(8,128)S(1)} %add.54), channel_id=1, source_target_pairs={{0,7},{1,6},{2,5},{3,4},{4,3},{5,2},{6,1},{7,0},{8,15},{9,14},{10,... | collective-permute-start | bytes 98312 | tf_op jit(solution)/shard_map/ppermute | solution.py:252
  78.5 1.3 %collective-permute-done.12 = f32[8,1024]{1,0:T(8,128)S(1)} collective-permute-done((f32[8,1024]{1,0:T(8,128)S(1)}, f32[8,1024]{1,0:T(8,128)S(1)}, u32[]{:S(2)}, u32[]{:S(2)}) %collective-permute-start.12) | collective-permute-done | bytes 32800 | tf_op jit(solution)/shard_map/ppermute | solution.py:252
  79.8 0.7 bus_kernel.1
  80.5 16.6 %all_to_all.11 = f32[16,8,128]{2,1,0:T(8,128)S(1)} all-to-all(f32[16,8,128]{2,1,0:T(8,128)S(1)} %bus_kernel.1), channel_id=1, replica_groups=mesh['line'=16,'out'=16] {'line'}, dimensions={0} | all-to-all | bytes 131072 | tf_op jit(solution)/shard_map/all_to_all | solution.py:318
  97.1 0.6 reduce_sum.19
  (31 shorter events, 0.7 us)
Async XLA Ops:
  3.0 3.1 %collective-permute-start = (f32[8,1024]{1,0:T(8,128)}, f32[8,1024]{1,0:T(8,128)S(1)}, u32[]{:S(2)}, u32[]{:S(2)}) collective-permute-start(f32[8,1024]{1,0:T(8,128)} %flows_kernel.1.x_ref), channel_id=1, source_target_pairs={{0,8},{1,9},{2,10},{3,11},{4,12},{5,13},{6,14},{7,15},{8,0},{9,1},... | collective-permute-start | bytes 98312 | tf_op jit(solution)/shard_map/ppermute | solution.py:252
  4.3 0.8 copy-start.2
  6.1 2.8 %collective-permute-start.1 = (f32[8,1024]{1,0:T(8,128)S(1)}, f32[8,1024]{1,0:T(8,128)S(1)}, u32[]{:S(2)}, u32[]{:S(2)}) collective-permute-start(f32[8,1024]{1,0:T(8,128)S(1)} %add.42), channel_id=1, source_target_pairs={{0,1},{1,0},{2,3},{3,2},{4,5},{5,4},{6,7},{7,6},{8,9},{9,8},{10,11... | collective-permute-start | bytes 98312 | tf_op jit(solution)/shard_map/ppermute | solution.py:252
  8.9 4.3 %collective-permute-start.2 = (f32[8,1024]{1,0:T(8,128)S(1)}, f32[8,1024]{1,0:T(8,128)S(1)}, u32[]{:S(2)}, u32[]{:S(2)}) collective-permute-start(f32[8,1024]{1,0:T(8,128)S(1)} %add.43), channel_id=1, source_target_pairs={{0,2},{1,3},{2,0},{3,1},{4,6},{5,7},{6,4},{7,5},{8,10},{9,11},{10,... | collective-permute-start | bytes 98312 | tf_op jit(solution)/shard_map/ppermute | solution.py:252
  11.9 23.8 %copy-start = (f32[1024,512]{1,0:T(8,128)S(1)}, f32[1024,512]{1,0:T(8,128)}, u32[]{:S(2)}) copy-start(f32[1024,512]{1,0:T(8,128)} %x_ref.1) | copy-start | bytes 6291460
  13.2 7.1 %collective-permute-start.3 = (f32[8,1024]{1,0:T(8,128)S(1)}, f32[8,1024]{1,0:T(8,128)S(1)}, u32[]{:S(2)}, u32[]{:S(2)}) collective-permute-start(f32[8,1024]{1,0:T(8,128)S(1)} %add.44), channel_id=1, source_target_pairs={{0,7},{1,6},{2,5},{3,4},{4,3},{5,2},{6,1},{7,0},{8,15},{9,14},{10,... | collective-permute-start | bytes 98312 | tf_op jit(solution)/shard_map/ppermute | solution.py:252
  18.8 0.7 copy-start.3
  20.5 18.5 %copy-start.1 = (f32[1024,1024]{1,0:T(8,128)S(1)}, f32[1024,1024]{1,0:T(8,128)}, u32[]{:S(2)}) copy-start(f32[1024,1024]{1,0:T(8,128)} %factors_ref.1) | copy-start | bytes 12582916
  20.5 5.6 %collective-permute-start.4 = (f32[8,1024]{1,0:T(8,128)S(1)}, f32[8,1024]{1,0:T(8,128)S(1)}, u32[]{:S(2)}, u32[]{:S(2)}) collective-permute-start(f32[8,1024]{1,0:T(8,128)S(1)} %select_kernel.1), channel_id=1, source_target_pairs={{0,16},{16,0},{32,48},{48,32},{64,80},{80,64},{96,112},{112,96},{1... | collective-permute-start | bytes 98312 | tf_op jit(solution)/shard_map/ppermute | solution.py:258
  26.2 4.9 %collective-permute-start.5 = (f32[8,1024]{1,0:T(8,128)S(1)}, f32[8,1024]{1,0:T(8,128)S(1)}, u32[]{:S(2)}, u32[]{:S(2)}) collective-permute-start(f32[8,1024]{1,0:T(8,128)S(1)} %add.47), channel_id=1, source_target_pairs={{0,144},{1,145},{2,146},{3,147},{4,148},{5,149},{6,150},{7,151},{8... | collective-permute-start | bytes 98312 | tf_op jit(solution)/shard_map/ppermute | solution.py:252
  31.1 4.6 %collective-permute-start.6 = (f32[8,1024]{1,0:T(8,128)S(1)}, f32[8,1024]{1,0:T(8,128)S(1)}, u32[]{:S(2)}, u32[]{:S(2)}) collective-permute-start(f32[8,1024]{1,0:T(8,128)S(1)} %add.48), channel_id=1, source_target_pairs={{0,112},{1,113},{2,114},{3,115},{4,116},{5,117},{6,118},{7,119},{8... | collective-permute-start | bytes 98312 | tf_op jit(solution)/shard_map/ppermute | solution.py:252
  35.6 3.3 %collective-permute-start.7 = (f32[8,1024]{1,0:T(8,128)S(1)}, f32[8,1024]{1,0:T(8,128)S(1)}, u32[]{:S(2)}, u32[]{:S(2)}) collective-permute-start(f32[8,1024]{1,0:T(8,128)S(1)} %add.49), channel_id=1, source_target_pairs={{0,48},{1,49},{2,50},{3,51},{4,52},{5,53},{6,54},{7,55},{8,56},{9,... | collective-permute-start | bytes 98312 | tf_op jit(solution)/shard_map/ppermute | solution.py:252
  49.3 1.4 %collective-permute-start.8 = (f32[8,1024]{1,0:T(8,128)S(1)}, f32[8,1024]{1,0:T(8,128)S(1)}, u32[]{:S(2)}, u32[]{:S(2)}) collective-permute-start(f32[8,1024]{1,0:T(8,128)S(1)} %get-tuple-element.25), channel_id=1, source_target_pairs={{0,16},{16,0},{32,48},{48,32},{64,80},{80,64},{96,112},{112,96},{1... | collective-permute-start | bytes 98312 | tf_op jit(solution)/shard_map/ppermute | solution.py:258
  64.7 2.9 %collective-permute-start.9 = (f32[8,1024]{1,0:T(8,128)S(1)}, f32[8,1024]{1,0:T(8,128)S(1)}, u32[]{:S(2)}, u32[]{:S(2)}) collective-permute-start(f32[8,1024]{1,0:T(8,128)S(1)} %place_kernel.1), channel_id=1, source_target_pairs={{0,8},{1,9},{2,10},{3,11},{4,12},{5,13},{6,14},{7,15},{8,0},{9,1},... | collective-permute-start | bytes 98312 | tf_op jit(solution)/shard_map/ppermute | solution.py:252
  67.5 2.8 %collective-permute-start.10 = (f32[8,1024]{1,0:T(8,128)S(1)}, f32[8,1024]{1,0:T(8,128)S(1)}, u32[]{:S(2)}, u32[]{:S(2)}) collective-permute-start(f32[8,1024]{1,0:T(8,128)S(1)} %add.52), channel_id=1, source_target_pairs={{0,1},{1,0},{2,3},{3,2},{4,5},{5,4},{6,7},{7,6},{8,9},{9,8},{10,11... | collective-permute-start | bytes 98312 | tf_op jit(solution)/shard_map/ppermute | solution.py:252
  70.4 3.7 %collective-permute-start.11 = (f32[8,1024]{1,0:T(8,128)S(1)}, f32[8,1024]{1,0:T(8,128)S(1)}, u32[]{:S(2)}, u32[]{:S(2)}) collective-permute-start(f32[8,1024]{1,0:T(8,128)S(1)} %add.53), channel_id=1, source_target_pairs={{0,2},{1,3},{2,0},{3,1},{4,6},{5,7},{6,4},{7,5},{8,10},{9,11},{10,... | collective-permute-start | bytes 98312 | tf_op jit(solution)/shard_map/ppermute | solution.py:252
  74.0 5.8 %collective-permute-start.12 = (f32[8,1024]{1,0:T(8,128)S(1)}, f32[8,1024]{1,0:T(8,128)S(1)}, u32[]{:S(2)}, u32[]{:S(2)}) collective-permute-start(f32[8,1024]{1,0:T(8,128)S(1)} %add.54), channel_id=1, source_target_pairs={{0,7},{1,6},{2,5},{3,4},{4,3},{5,2},{6,1},{7,0},{8,15},{9,14},{10,... | collective-permute-start | bytes 98312 | tf_op jit(solution)/shard_map/ppermute | solution.py:252

commit v7 on v6

--- a/solution.py
+++ b/solution.py
@@ -138,10 +138,7 @@
     blocks = width // LANES
     parts = range(TILES)
     tile = TILES * SUB
-    for h in range(hours):
-        for kb in range(blocks):
-            piece = (0.5 / SOFTNESS) * out_flow_ref[h : h + 1, kb * LANES : (kb + 1) * LANES]
-            wide[h * blocks + kb] = jnp.broadcast_to(piece, (SUB, LANES))
+    wide[...] = (0.5 / SOFTNESS) * out_flow_ref[...]
     total[...] = jnp.zeros_like(total)
 
     def advance(step, carry):
@@ -154,7 +151,7 @@
             minus = [flow[r] - limit[r] for r in parts]
             across = [None for r in parts]
             for kb in range(blocks):
-                out_flow = wide[h * blocks + kb]
+                out_flow = wide[h : h + 1, kb * LANES : (kb + 1) * LANES]
                 gathered = None
                 for r in parts:
                     factor = factors_ref[at[r], kb * LANES : (kb + 1) * LANES]
@@ -278,8 +275,9 @@
         line_limits.reshape(1, rows),
         dtype=(jnp.int32, jnp.float32),
     )
-    flows = call(copy_kernel, [(hours, rows)], flows) + moved(flows, over_out[0])
-    for move in over_out[1:]:
+    back = over_out[::-1]
+    flows = call(copy_kernel, [(hours, rows)], flows) + moved(flows, back[0])
+    for move in back[1:]:
         flows = add_move(flows, move)
     flows, inverse, limits = lax.optimization_barrier((flows, inverse, limits))
     flow_out = call(select_kernel, [(hours, width)], flows, index)
@@ -300,7 +298,7 @@
         flow_out,
         mib=24,
         scratch=[
-            pltpu.VMEM((hours * blocks, SUB, LANES), jnp.float32),
+            pltpu.VMEM((hours, width), jnp.float32),
             pltpu.VMEM((hours * blocks, SUB, LANES), jnp.float32),
         ],
     )

time: 98 us -> 97.7 us (level)
  starting transfers between devices: 24.6 us -> 22.8 us
  waiting for transfers between devices: 21.8 us -> 23.5 us
    ppermute x11, waiting for transfers between devices: 21.8 us -> 23.5 us  [moved(): return lax.ppermute(x, ('line', 'out'), pairs_over((lines, outs), move))]
    ppermute x11, starting transfers between devices: 19.8 us -> 18.1 us  [moved(): return lax.ppermute(x, ('line', 'out'), pairs_over((lines, outs), move))]
where the time goes in v7:
time: 97.7 us; the launch traced here: 97.4 us
  blocking collectives  30 us (31%)
  waiting for transfers between devices  23.5 us (24%)
  starting transfers between devices  22.8 us (23%)
  Pallas kernels  17.9 us (18%)
  local copies, waits for them, and re-layouts  1.51 us (2%)
  other arithmetic  1.39 us (1%)
    ppermute x11, waiting for transfers between devices, moved(): return lax.ppermute(x, ('line', 'out'), pairs_over((lines, outs), move))  23.5 us
    ppermute x11, starting transfers between devices, moved(): return lax.ppermute(x, ('line', 'out'), pairs_over((lines, outs), move))  18.1 us
    pallas_call x10, Pallas kernels, call(): pl.pallas_call(kernel, out_shape=out_shape, in_specs=[FAR] * far + [VMEM]...  17.9 us
    all_to_all x1, blocking collectives, local(): gradient = lax.all_to_all(pieces, 'line', 0, 0, tiled=True).sum(0)  16.3 us
    all_to_all x1, blocking collectives, local(): lax.all_to_all(copies, 'line', 0, 0, axis_index_groups=[list(range(c, lin...  13.7 us
    ppermute x2, starting transfers between devices, other_core(): return lax.ppermute(x, 'line', [(i, i ^ 1) for i in range(lines)])  4.71 us
  transfers between devices with their start and end apart: 13, of which 10 were waited for; matrix products, arithmetic and copies ran while one was open for 1% of the time, Pallas kernels for 4%

profile of v7, /device:TPU:33, one launch (start us, length us, event | category | flops | bytes accessed | tf_op | source)
XLA Modules:
  0.0 97.4 jit_solution(13824148820509177543)
XLA Ops:
  0.0 3.0 %flows_kernel.1.x_ref = f32[8,1024]{1,0:T(8,128)} custom-call(f32[8,512]{1,0:T(8,128)} %injections_hbm.1, f32[1024,512]{1,0:T(8,128)} %x_ref.1), custom_call_target="tpu_custom_call" | custom-call | bytes 2113536 | tf_op jit(solution)/shard_map/flows_kernel/pallas_call | solution.py:190
  3.0 5.7 %collective-permute-start = (f32[8,1024]{1,0:T(8,128)}, f32[8,1024]{1,0:T(8,128)S(1)}, u32[]{:S(2)}, u32[]{:S(2)}) collective-permute-start(f32[8,1024]{1,0:T(8,128)} %flows_kernel.1.x_ref), channel_id=1, source_target_pairs={{0,7},{1,6},{2,5},{3,4},{4,3},{5,2},{6,1},{7,0},{8,15},{9,14},{10,... | collective-permute-start | bytes 98312 | tf_op jit(solution)/shard_map/ppermute | solution.py:249
  8.7 0.8 copy-done.2
  9.5 0.7 collective-permute-done
  10.2 0.3 collective-permute-start.1
  10.5 3.4 %collective-permute-done.1 = f32[8,1024]{1,0:T(8,128)S(1)} collective-permute-done((f32[8,1024]{1,0:T(8,128)S(1)}, f32[8,1024]{1,0:T(8,128)S(1)}, u32[]{:S(2)}, u32[]{:S(2)}) %collective-permute-start.1) | collective-permute-done | bytes 32800 | tf_op jit(solution)/shard_map/ppermute | solution.py:249
  13.9 2.7 %collective-permute-done.2 = f32[8,1024]{1,0:T(8,128)S(1)} collective-permute-done((f32[8,1024]{1,0:T(8,128)S(1)}, f32[8,1024]{1,0:T(8,128)S(1)}, u32[]{:S(2)}, u32[]{:S(2)}) %collective-permute-start.2) | collective-permute-done | bytes 32800 | tf_op jit(solution)/shard_map/ppermute | solution.py:249
  16.7 1.2 %collective-permute-start.3 = (f32[8,1024]{1,0:T(8,128)S(1)}, f32[8,1024]{1,0:T(8,128)S(1)}, u32[]{:S(2)}, u32[]{:S(2)}) collective-permute-start(f32[8,1024]{1,0:T(8,128)S(1)} %add.44), channel_id=1, source_target_pairs={{0,8},{1,9},{2,10},{3,11},{4,12},{5,13},{6,14},{7,15},{8,0},{9,1},... | collective-permute-start | bytes 98312 | tf_op jit(solution)/shard_map/ppermute | solution.py:249
  17.9 0.7 dynamic-slice_subtract_fusion
  18.6 0.7 copy-done.3
  19.2 0.8 inverse_kernel.1
  20.2 4.4 %collective-permute-start.4 = (f32[8,1024]{1,0:T(8,128)S(1)}, f32[8,1024]{1,0:T(8,128)S(1)}, u32[]{:S(2)}, u32[]{:S(2)}) collective-permute-start(f32[8,1024]{1,0:T(8,128)S(1)} %select_kernel.1), channel_id=1, source_target_pairs={{0,16},{16,0},{32,48},{48,32},{64,80},{80,64},{96,112},{112,96},{1... | collective-permute-start | bytes 98312 | tf_op jit(solution)/shard_map/ppermute | solution.py:255
  24.7 1.1 %spread_kernel.1.flow_ref = f32[8,1024,128]{2,1,0:T(8,128)S(1)} custom-call(f32[8,1024]{1,0:T(8,128)S(1)} %add.45.values_ref.flow_ref), custom_call_target="tpu_custom_call" | custom-call | bytes 32768 | tf_op jit(solution)/shard_map/spread_kernel/pallas_call | solution.py:190
  25.9 2.7 %collective-permute-start.5 = (f32[8,1024]{1,0:T(8,128)S(1)}, f32[8,1024]{1,0:T(8,128)S(1)}, u32[]{:S(2)}, u32[]{:S(2)}) collective-permute-start(f32[8,1024]{1,0:T(8,128)S(1)} %add.47), channel_id=1, source_target_pairs={{0,144},{1,145},{2,146},{3,147},{4,148},{5,149},{6,150},{7,151},{8... | collective-permute-start | bytes 98312 | tf_op jit(solution)/shard_map/ppermute | solution.py:249
  28.6 2.2 %collective-permute-done.5 = f32[8,1024]{1,0:T(8,128)S(1)} collective-permute-done((f32[8,1024]{1,0:T(8,128)S(1)}, f32[8,1024]{1,0:T(8,128)S(1)}, u32[]{:S(2)}, u32[]{:S(2)}) %collective-permute-start.5) | collective-permute-done | bytes 32800 | tf_op jit(solution)/shard_map/ppermute | solution.py:249
  30.8 2.6 %collective-permute-start.6 = (f32[8,1024]{1,0:T(8,128)S(1)}, f32[8,1024]{1,0:T(8,128)S(1)}, u32[]{:S(2)}, u32[]{:S(2)}) collective-permute-start(f32[8,1024]{1,0:T(8,128)S(1)} %add.48), channel_id=1, source_target_pairs={{0,112},{1,113},{2,114},{3,115},{4,116},{5,117},{6,118},{7,119},{8... | collective-permute-start | bytes 98312 | tf_op jit(solution)/shard_map/ppermute | solution.py:249
  33.4 1.9 %collective-permute-done.6 = f32[8,1024]{1,0:T(8,128)S(1)} collective-permute-done((f32[8,1024]{1,0:T(8,128)S(1)}, f32[8,1024]{1,0:T(8,128)S(1)}, u32[]{:S(2)}, u32[]{:S(2)}) %collective-permute-start.6) | collective-permute-done | bytes 32800 | tf_op jit(solution)/shard_map/ppermute | solution.py:249
  35.4 0.5 thirds_kernel.1.factors_ref
  35.9 2.8 %collective-permute-done.7 = f32[8,1024]{1,0:T(8,128)S(1)} collective-permute-done((f32[8,1024]{1,0:T(8,128)S(1)}, f32[8,1024]{1,0:T(8,128)S(1)}, u32[]{:S(2)}, u32[]{:S(2)}) %collective-permute-start.7) | collective-permute-done | bytes 32800 | tf_op jit(solution)/shard_map/ppermute | solution.py:249
  38.7 10.3 %overload_kernel.1 = (f32[8,1024,128]{2,1,0:T(8,128)S(1)}, f32[8,1024]{1,0:T(8,128)S(1)}) custom-call(f32[1024,1024]{1,0:T(8,128)S(1)} %copy-done.1, f32[8,1024,128]{2,1,0:T(8,128)S(1)} %spread_kernel.1.flow_ref, f32[1024,128]{1,0:T(8,128)S(1)} %get-tuple-element.22.limit_ref, f32[8,1024]{1,0:T(8,128)S(1)} %add.50.out_flow_ref), custom_call_target="tpu_custom_call" | custom-call | bytes 8945664 | tf_op jit(solution)/shard_map/overload_kernel/pallas_call | solution.py:190
  49.2 1.1 %row_kernel.1.rows_ref = f32[8,1024]{1,0:T(8,128)S(1)} custom-call(f32[8,1024,128]{2,1,0:T(8,128)S(1)} %get-tuple-element.26.sums_ref), custom_call_target="tpu_custom_call" | custom-call | bytes 4194304 | tf_op jit(solution)/shard_map/row_kernel/pallas_call | solution.py:190
  50.5 13.7 %all_to_all.10 = f32[8,8,1024]{2,1,0:T(8,128)S(1)} all-to-all(f32[8,8,1024]{2,1,0:T(8,128)S(1)} %broadcast_in_dim.3), channel_id=1, replica_groups={{0,32,64,96,128,160,192,224},{16,48,80,112,144,176,208,240},{1,33,65,97..., dimensions={0} | all-to-all | bytes 524288 | tf_op jit(solution)/shard_map/all_to_all | solution.py:309
  64.3 0.4 collective-permute-start.9
  64.7 2.5 %collective-permute-done.9 = f32[8,1024]{1,0:T(8,128)S(1)} collective-permute-done((f32[8,1024]{1,0:T(8,128)S(1)}, f32[8,1024]{1,0:T(8,128)S(1)}, u32[]{:S(2)}, u32[]{:S(2)}) %collective-permute-start.9) | collective-permute-done | bytes 32800 | tf_op jit(solution)/shard_map/ppermute | solution.py:249
  67.2 2.8 %collective-permute-done.10 = f32[8,1024]{1,0:T(8,128)S(1)} collective-permute-done((f32[8,1024]{1,0:T(8,128)S(1)}, f32[8,1024]{1,0:T(8,128)S(1)}, u32[]{:S(2)}, u32[]{:S(2)}) %collective-permute-start.10) | collective-permute-done | bytes 32800 | tf_op jit(solution)/shard_map/ppermute | solution.py:249
  70.1 0.5 collective-permute-start.11
  70.5 3.2 %collective-permute-done.11 = f32[8,1024]{1,0:T(8,128)S(1)} collective-permute-done((f32[8,1024]{1,0:T(8,128)S(1)}, f32[8,1024]{1,0:T(8,128)S(1)}, u32[]{:S(2)}, u32[]{:S(2)}) %collective-permute-start.11) | collective-permute-done | bytes 32800 | tf_op jit(solution)/shard_map/ppermute | solution.py:249
  73.7 4.7 %collective-permute-start.12 = (f32[8,1024]{1,0:T(8,128)S(1)}, f32[8,1024]{1,0:T(8,128)S(1)}, u32[]{:S(2)}, u32[]{:S(2)}) collective-permute-start(f32[8,1024]{1,0:T(8,128)S(1)} %add.54), channel_id=1, source_target_pairs={{0,7},{1,6},{2,5},{3,4},{4,3},{5,2},{6,1},{7,0},{8,15},{9,14},{10,... | collective-permute-start | bytes 98312 | tf_op jit(solution)/shard_map/ppermute | solution.py:249
  78.5 1.3 %collective-permute-done.12 = f32[8,1024]{1,0:T(8,128)S(1)} collective-permute-done((f32[8,1024]{1,0:T(8,128)S(1)}, f32[8,1024]{1,0:T(8,128)S(1)}, u32[]{:S(2)}, u32[]{:S(2)}) %collective-permute-start.12) | collective-permute-done | bytes 32800 | tf_op jit(solution)/shard_map/ppermute | solution.py:249
  79.8 0.7 bus_kernel.1
  80.5 16.3 %all_to_all.11 = f32[16,8,128]{2,1,0:T(8,128)S(1)} all-to-all(f32[16,8,128]{2,1,0:T(8,128)S(1)} %bus_kernel.1), channel_id=1, replica_groups=mesh['line'=16,'out'=16] {'line'}, dimensions={0} | all-to-all | bytes 131072 | tf_op jit(solution)/shard_map/all_to_all | solution.py:316
  96.8 0.6 reduce_sum.19
  (31 shorter events, 0.7 us)
Async XLA Ops:
  3.0 7.2 %collective-permute-start = (f32[8,1024]{1,0:T(8,128)}, f32[8,1024]{1,0:T(8,128)S(1)}, u32[]{:S(2)}, u32[]{:S(2)}) collective-permute-start(f32[8,1024]{1,0:T(8,128)} %flows_kernel.1.x_ref), channel_id=1, source_target_pairs={{0,7},{1,6},{2,5},{3,4},{4,3},{5,2},{6,1},{7,0},{8,15},{9,14},{10,... | collective-permute-start | bytes 98312 | tf_op jit(solution)/shard_map/ppermute | solution.py:249
  8.7 0.8 copy-start.2
  10.2 3.7 %collective-permute-start.1 = (f32[8,1024]{1,0:T(8,128)S(1)}, f32[8,1024]{1,0:T(8,128)S(1)}, u32[]{:S(2)}, u32[]{:S(2)}) collective-permute-start(f32[8,1024]{1,0:T(8,128)S(1)} %add.42), channel_id=1, source_target_pairs={{0,2},{1,3},{2,0},{3,1},{4,6},{5,7},{6,4},{7,5},{8,10},{9,11},{10,... | collective-permute-start | bytes 98312 | tf_op jit(solution)/shard_map/ppermute | solution.py:249
  13.9 2.8 %collective-permute-start.2 = (f32[8,1024]{1,0:T(8,128)S(1)}, f32[8,1024]{1,0:T(8,128)S(1)}, u32[]{:S(2)}, u32[]{:S(2)}) collective-permute-start(f32[8,1024]{1,0:T(8,128)S(1)} %add.43), channel_id=1, source_target_pairs={{0,1},{1,0},{2,3},{3,2},{4,5},{5,4},{6,7},{7,6},{8,9},{9,8},{10,11... | collective-permute-start | bytes 98312 | tf_op jit(solution)/shard_map/ppermute | solution.py:249
  13.9 21.5 %copy-start = (f32[1024,512]{1,0:T(8,128)S(1)}, f32[1024,512]{1,0:T(8,128)}, u32[]{:S(2)}) copy-start(f32[1024,512]{1,0:T(8,128)} %x_ref.1) | copy-start | bytes 6291460
  16.7 3.4 %collective-permute-start.3 = (f32[8,1024]{1,0:T(8,128)S(1)}, f32[8,1024]{1,0:T(8,128)S(1)}, u32[]{:S(2)}, u32[]{:S(2)}) collective-permute-start(f32[8,1024]{1,0:T(8,128)S(1)} %add.44), channel_id=1, source_target_pairs={{0,8},{1,9},{2,10},{3,11},{4,12},{5,13},{6,14},{7,15},{8,0},{9,1},... | collective-permute-start | bytes 98312 | tf_op jit(solution)/shard_map/ppermute | solution.py:249
  18.6 0.7 copy-start.3
  20.2 18.5 %copy-start.1 = (f32[1024,1024]{1,0:T(8,128)S(1)}, f32[1024,1024]{1,0:T(8,128)}, u32[]{:S(2)}) copy-start(f32[1024,1024]{1,0:T(8,128)} %factors_ref.1) | copy-start | bytes 12582916
  20.2 5.6 %collective-permute-start.4 = (f32[8,1024]{1,0:T(8,128)S(1)}, f32[8,1024]{1,0:T(8,128)S(1)}, u32[]{:S(2)}, u32[]{:S(2)}) collective-permute-start(f32[8,1024]{1,0:T(8,128)S(1)} %select_kernel.1), channel_id=1, source_target_pairs={{0,16},{16,0},{32,48},{48,32},{64,80},{80,64},{96,112},{112,96},{1... | collective-permute-start | bytes 98312 | tf_op jit(solution)/shard_map/ppermute | solution.py:255
  25.9 4.9 %collective-permute-start.5 = (f32[8,1024]{1,0:T(8,128)S(1)}, f32[8,1024]{1,0:T(8,128)S(1)}, u32[]{:S(2)}, u32[]{:S(2)}) collective-permute-start(f32[8,1024]{1,0:T(8,128)S(1)} %add.47), channel_id=1, source_target_pairs={{0,144},{1,145},{2,146},{3,147},{4,148},{5,149},{6,150},{7,151},{8... | collective-permute-start | bytes 98312 | tf_op jit(solution)/shard_map/ppermute | solution.py:249
  30.8 4.6 %collective-permute-start.6 = (f32[8,1024]{1,0:T(8,128)S(1)}, f32[8,1024]{1,0:T(8,128)S(1)}, u32[]{:S(2)}, u32[]{:S(2)}) collective-permute-start(f32[8,1024]{1,0:T(8,128)S(1)} %add.48), channel_id=1, source_target_pairs={{0,112},{1,113},{2,114},{3,115},{4,116},{5,117},{6,118},{7,119},{8... | collective-permute-start | bytes 98312 | tf_op jit(solution)/shard_map/ppermute | solution.py:249
  35.4 3.3 %collective-permute-start.7 = (f32[8,1024]{1,0:T(8,128)S(1)}, f32[8,1024]{1,0:T(8,128)S(1)}, u32[]{:S(2)}, u32[]{:S(2)}) collective-permute-start(f32[8,1024]{1,0:T(8,128)S(1)} %add.49), channel_id=1, source_target_pairs={{0,48},{1,49},{2,50},{3,51},{4,52},{5,53},{6,54},{7,55},{8,56},{9,... | collective-permute-start | bytes 98312 | tf_op jit(solution)/shard_map/ppermute | solution.py:249
  49.0 1.4 %collective-permute-start.8 = (f32[8,1024]{1,0:T(8,128)S(1)}, f32[8,1024]{1,0:T(8,128)S(1)}, u32[]{:S(2)}, u32[]{:S(2)}) collective-permute-start(f32[8,1024]{1,0:T(8,128)S(1)} %get-tuple-element.25), channel_id=1, source_target_pairs={{0,16},{16,0},{32,48},{48,32},{64,80},{80,64},{96,112},{112,96},{1... | collective-permute-start | bytes 98312 | tf_op jit(solution)/shard_map/ppermute | solution.py:255
  64.3 2.9 %collective-permute-start.9 = (f32[8,1024]{1,0:T(8,128)S(1)}, f32[8,1024]{1,0:T(8,128)S(1)}, u32[]{:S(2)}, u32[]{:S(2)}) collective-permute-start(f32[8,1024]{1,0:T(8,128)S(1)} %place_kernel.1), channel_id=1, source_target_pairs={{0,8},{1,9},{2,10},{3,11},{4,12},{5,13},{6,14},{7,15},{8,0},{9,1},... | collective-permute-start | bytes 98312 | tf_op jit(solution)/shard_map/ppermute | solution.py:249
  67.2 2.8 %collective-permute-start.10 = (f32[8,1024]{1,0:T(8,128)S(1)}, f32[8,1024]{1,0:T(8,128)S(1)}, u32[]{:S(2)}, u32[]{:S(2)}) collective-permute-start(f32[8,1024]{1,0:T(8,128)S(1)} %add.52), channel_id=1, source_target_pairs={{0,1},{1,0},{2,3},{3,2},{4,5},{5,4},{6,7},{7,6},{8,9},{9,8},{10,11... | collective-permute-start | bytes 98312 | tf_op jit(solution)/shard_map/ppermute | solution.py:249
  70.1 3.7 %collective-permute-start.11 = (f32[8,1024]{1,0:T(8,128)S(1)}, f32[8,1024]{1,0:T(8,128)S(1)}, u32[]{:S(2)}, u32[]{:S(2)}) collective-permute-start(f32[8,1024]{1,0:T(8,128)S(1)} %add.53), channel_id=1, source_target_pairs={{0,2},{1,3},{2,0},{3,1},{4,6},{5,7},{6,4},{7,5},{8,10},{9,11},{10,... | collective-permute-start | bytes 98312 | tf_op jit(solution)/shard_map/ppermute | solution.py:249
  73.7 6.1 %collective-permute-start.12 = (f32[8,1024]{1,0:T(8,128)S(1)}, f32[8,1024]{1,0:T(8,128)S(1)}, u32[]{:S(2)}, u32[]{:S(2)}) collective-permute-start(f32[8,1024]{1,0:T(8,128)S(1)} %add.54), channel_id=1, source_target_pairs={{0,7},{1,6},{2,5},{3,4},{4,3},{5,2},{6,1},{7,0},{8,15},{9,14},{10,... | collective-permute-start | bytes 98312 | tf_op jit(solution)/shard_map/ppermute | solution.py:249

commit v8 on v7

--- a/solution.py
+++ b/solution.py
@@ -255,6 +255,7 @@
         return lax.ppermute(x, "line", [(i, i ^ 1) for i in range(lines)])
 
     over_out, over_line = out_moves(outs), line_moves(lines)
+    over_line = [over_line[1], over_line[0], *over_line[2:]]
     flows = call(
         flows_kernel,
         [(hours, rows)],

time: 97.7 us -> 97.7 us (level)
  no operation moved by 1% of the time
where the time goes in v8:
time: 97.7 us; the launch traced here: 97.4 us
  blocking collectives  30 us (31%)
  waiting for transfers between devices  23.4 us (24%)
  starting transfers between devices  23 us (24%)
  Pallas kernels  17.9 us (18%)
  local copies, waits for them, and re-layouts  1.51 us (2%)
  other arithmetic  1.39 us (1%)
    ppermute x11, waiting for transfers between devices, moved(): return lax.ppermute(x, ('line', 'out'), pairs_over((lines, outs), move))  23.4 us
    ppermute x11, starting transfers between devices, moved(): return lax.ppermute(x, ('line', 'out'), pairs_over((lines, outs), move))  18.3 us
    pallas_call x10, Pallas kernels, call(): pl.pallas_call(kernel, out_shape=out_shape, in_specs=[FAR] * far + [VMEM]...  17.9 us
    all_to_all x1, blocking collectives, local(): gradient = lax.all_to_all(pieces, 'line', 0, 0, tiled=True).sum(0)  16.3 us
    all_to_all x1, blocking collectives, local(): lax.all_to_all(copies, 'line', 0, 0, axis_index_groups=[list(range(c, lin...  13.7 us
    ppermute x2, starting transfers between devices, other_core(): return lax.ppermute(x, 'line', [(i, i ^ 1) for i in range(lines)])  4.71 us
  transfers between devices with their start and end apart: 13, of which 10 were waited for; matrix products, arithmetic and copies ran while one was open for 1% of the time, Pallas kernels for 4%

profile of v8, /device:TPU:33, one launch (start us, length us, event | category | flops | bytes accessed | tf_op | source)
XLA Modules:
  0.0 97.4 jit_solution(6920340895971694448)
XLA Ops:
  0.0 3.0 %flows_kernel.1.x_ref = f32[8,1024]{1,0:T(8,128)} custom-call(f32[8,512]{1,0:T(8,128)} %injections_hbm.1, f32[1024,512]{1,0:T(8,128)} %x_ref.1), custom_call_target="tpu_custom_call" | custom-call | bytes 2113536 | tf_op jit(solution)/shard_map/flows_kernel/pallas_call | solution.py:190
  3.0 5.7 %collective-permute-start = (f32[8,1024]{1,0:T(8,128)}, f32[8,1024]{1,0:T(8,128)S(1)}, u32[]{:S(2)}, u32[]{:S(2)}) collective-permute-start(f32[8,1024]{1,0:T(8,128)} %flows_kernel.1.x_ref), channel_id=1, source_target_pairs={{0,7},{1,6},{2,5},{3,4},{4,3},{5,2},{6,1},{7,0},{8,15},{9,14},{10,... | collective-permute-start | bytes 98312 | tf_op jit(solution)/shard_map/ppermute | solution.py:249
  8.7 0.8 copy-done.2
  9.5 0.7 collective-permute-done
  10.2 0.3 collective-permute-start.1
  10.5 3.4 %collective-permute-done.1 = f32[8,1024]{1,0:T(8,128)S(1)} collective-permute-done((f32[8,1024]{1,0:T(8,128)S(1)}, f32[8,1024]{1,0:T(8,128)S(1)}, u32[]{:S(2)}, u32[]{:S(2)}) %collective-permute-start.1) | collective-permute-done | bytes 32800 | tf_op jit(solution)/shard_map/ppermute | solution.py:249
  13.9 2.7 %collective-permute-done.2 = f32[8,1024]{1,0:T(8,128)S(1)} collective-permute-done((f32[8,1024]{1,0:T(8,128)S(1)}, f32[8,1024]{1,0:T(8,128)S(1)}, u32[]{:S(2)}, u32[]{:S(2)}) %collective-permute-start.2) | collective-permute-done | bytes 32800 | tf_op jit(solution)/shard_map/ppermute | solution.py:249
  16.7 1.2 %collective-permute-start.3 = (f32[8,1024]{1,0:T(8,128)S(1)}, f32[8,1024]{1,0:T(8,128)S(1)}, u32[]{:S(2)}, u32[]{:S(2)}) collective-permute-start(f32[8,1024]{1,0:T(8,128)S(1)} %add.44), channel_id=1, source_target_pairs={{0,8},{1,9},{2,10},{3,11},{4,12},{5,13},{6,14},{7,15},{8,0},{9,1},... | collective-permute-start | bytes 98312 | tf_op jit(solution)/shard_map/ppermute | solution.py:249
  17.9 0.7 dynamic-slice_subtract_fusion
  18.6 0.7 copy-done.3
  19.2 0.8 inverse_kernel.1
  20.2 4.4 %collective-permute-start.4 = (f32[8,1024]{1,0:T(8,128)S(1)}, f32[8,1024]{1,0:T(8,128)S(1)}, u32[]{:S(2)}, u32[]{:S(2)}) collective-permute-start(f32[8,1024]{1,0:T(8,128)S(1)} %select_kernel.1), channel_id=1, source_target_pairs={{0,16},{16,0},{32,48},{48,32},{64,80},{80,64},{96,112},{112,96},{1... | collective-permute-start | bytes 98312 | tf_op jit(solution)/shard_map/ppermute | solution.py:255
  24.7 1.1 %spread_kernel.1.flow_ref = f32[8,1024,128]{2,1,0:T(8,128)S(1)} custom-call(f32[8,1024]{1,0:T(8,128)S(1)} %add.45.values_ref.flow_ref), custom_call_target="tpu_custom_call" | custom-call | bytes 32768 | tf_op jit(solution)/shard_map/spread_kernel/pallas_call | solution.py:190
  25.9 2.7 %collective-permute-start.5 = (f32[8,1024]{1,0:T(8,128)S(1)}, f32[8,1024]{1,0:T(8,128)S(1)}, u32[]{:S(2)}, u32[]{:S(2)}) collective-permute-start(f32[8,1024]{1,0:T(8,128)S(1)} %add.47), channel_id=1, source_target_pairs={{0,112},{1,113},{2,114},{3,115},{4,116},{5,117},{6,118},{7,119},{8... | collective-permute-start | bytes 98312 | tf_op jit(solution)/shard_map/ppermute | solution.py:249
  28.6 1.9 %collective-permute-done.5 = f32[8,1024]{1,0:T(8,128)S(1)} collective-permute-done((f32[8,1024]{1,0:T(8,128)S(1)}, f32[8,1024]{1,0:T(8,128)S(1)}, u32[]{:S(2)}, u32[]{:S(2)}) %collective-permute-start.5) | collective-permute-done | bytes 32800 | tf_op jit(solution)/shard_map/ppermute | solution.py:249
  30.5 2.8 %collective-permute-start.6 = (f32[8,1024]{1,0:T(8,128)S(1)}, f32[8,1024]{1,0:T(8,128)S(1)}, u32[]{:S(2)}, u32[]{:S(2)}) collective-permute-start(f32[8,1024]{1,0:T(8,128)S(1)} %add.48), channel_id=1, source_target_pairs={{0,144},{1,145},{2,146},{3,147},{4,148},{5,149},{6,150},{7,151},{8... | collective-permute-start | bytes 98312 | tf_op jit(solution)/shard_map/ppermute | solution.py:249
  33.3 2.0 %collective-permute-done.6 = f32[8,1024]{1,0:T(8,128)S(1)} collective-permute-done((f32[8,1024]{1,0:T(8,128)S(1)}, f32[8,1024]{1,0:T(8,128)S(1)}, u32[]{:S(2)}, u32[]{:S(2)}) %collective-permute-start.6) | collective-permute-done | bytes 32800 | tf_op jit(solution)/shard_map/ppermute | solution.py:249
  35.4 0.5 thirds_kernel.1.factors_ref
  35.9 2.8 %collective-permute-done.7 = f32[8,1024]{1,0:T(8,128)S(1)} collective-permute-done((f32[8,1024]{1,0:T(8,128)S(1)}, f32[8,1024]{1,0:T(8,128)S(1)}, u32[]{:S(2)}, u32[]{:S(2)}) %collective-permute-start.7) | collective-permute-done | bytes 32800 | tf_op jit(solution)/shard_map/ppermute | solution.py:249
  38.7 10.3 %overload_kernel.1 = (f32[8,1024,128]{2,1,0:T(8,128)S(1)}, f32[8,1024]{1,0:T(8,128)S(1)}) custom-call(f32[1024,1024]{1,0:T(8,128)S(1)} %copy-done.1, f32[8,1024,128]{2,1,0:T(8,128)S(1)} %spread_kernel.1.flow_ref, f32[1024,128]{1,0:T(8,128)S(1)} %get-tuple-element.22.limit_ref, f32[8,1024]{1,0:T(8,128)S(1)} %add.50.out_flow_ref), custom_call_target="tpu_custom_call" | custom-call | bytes 8945664 | tf_op jit(solution)/shard_map/overload_kernel/pallas_call | solution.py:190
  49.2 1.1 %row_kernel.1.rows_ref = f32[8,1024]{1,0:T(8,128)S(1)} custom-call(f32[8,1024,128]{2,1,0:T(8,128)S(1)} %get-tuple-element.26.sums_ref), custom_call_target="tpu_custom_call" | custom-call | bytes 4194304 | tf_op jit(solution)/shard_map/row_kernel/pallas_call | solution.py:190
  50.5 13.7 %all_to_all.10 = f32[8,8,1024]{2,1,0:T(8,128)S(1)} all-to-all(f32[8,8,1024]{2,1,0:T(8,128)S(1)} %broadcast_in_dim.3), channel_id=1, replica_groups={{0,32,64,96,128,160,192,224},{16,48,80,112,144,176,208,240},{1,33,65,97..., dimensions={0} | all-to-all | bytes 524288 | tf_op jit(solution)/shard_map/all_to_all | solution.py:310
  64.3 0.4 collective-permute-start.9
  64.7 2.5 %collective-permute-done.9 = f32[8,1024]{1,0:T(8,128)S(1)} collective-permute-done((f32[8,1024]{1,0:T(8,128)S(1)}, f32[8,1024]{1,0:T(8,128)S(1)}, u32[]{:S(2)}, u32[]{:S(2)}) %collective-permute-start.9) | collective-permute-done | bytes 32800 | tf_op jit(solution)/shard_map/ppermute | solution.py:249
  67.2 2.8 %collective-permute-done.10 = f32[8,1024]{1,0:T(8,128)S(1)} collective-permute-done((f32[8,1024]{1,0:T(8,128)S(1)}, f32[8,1024]{1,0:T(8,128)S(1)}, u32[]{:S(2)}, u32[]{:S(2)}) %collective-permute-start.10) | collective-permute-done | bytes 32800 | tf_op jit(solution)/shard_map/ppermute | solution.py:249
  70.1 0.5 collective-permute-start.11
  70.5 3.2 %collective-permute-done.11 = f32[8,1024]{1,0:T(8,128)S(1)} collective-permute-done((f32[8,1024]{1,0:T(8,128)S(1)}, f32[8,1024]{1,0:T(8,128)S(1)}, u32[]{:S(2)}, u32[]{:S(2)}) %collective-permute-start.11) | collective-permute-done | bytes 32800 | tf_op jit(solution)/shard_map/ppermute | solution.py:249
  73.7 4.7 %collective-permute-start.12 = (f32[8,1024]{1,0:T(8,128)S(1)}, f32[8,1024]{1,0:T(8,128)S(1)}, u32[]{:S(2)}, u32[]{:S(2)}) collective-permute-start(f32[8,1024]{1,0:T(8,128)S(1)} %add.54), channel_id=1, source_target_pairs={{0,7},{1,6},{2,5},{3,4},{4,3},{5,2},{6,1},{7,0},{8,15},{9,14},{10,... | collective-permute-start | bytes 98312 | tf_op jit(solution)/shard_map/ppermute | solution.py:249
  78.5 1.3 %collective-permute-done.12 = f32[8,1024]{1,0:T(8,128)S(1)} collective-permute-done((f32[8,1024]{1,0:T(8,128)S(1)}, f32[8,1024]{1,0:T(8,128)S(1)}, u32[]{:S(2)}, u32[]{:S(2)}) %collective-permute-start.12) | collective-permute-done | bytes 32800 | tf_op jit(solution)/shard_map/ppermute | solution.py:249
  79.8 0.7 bus_kernel.1
  80.5 16.3 %all_to_all.11 = f32[16,8,128]{2,1,0:T(8,128)S(1)} all-to-all(f32[16,8,128]{2,1,0:T(8,128)S(1)} %bus_kernel.1), channel_id=1, replica_groups=mesh['line'=16,'out'=16] {'line'}, dimensions={0} | all-to-all | bytes 131072 | tf_op jit(solution)/shard_map/all_to_all | solution.py:317
  96.8 0.6 reduce_sum.19
  (31 shorter events, 0.7 us)
Async XLA Ops:
  3.0 7.2 %collective-permute-start = (f32[8,1024]{1,0:T(8,128)}, f32[8,1024]{1,0:T(8,128)S(1)}, u32[]{:S(2)}, u32[]{:S(2)}) collective-permute-start(f32[8,1024]{1,0:T(8,128)} %flows_kernel.1.x_ref), channel_id=1, source_target_pairs={{0,7},{1,6},{2,5},{3,4},{4,3},{5,2},{6,1},{7,0},{8,15},{9,14},{10,... | collective-permute-start | bytes 98312 | tf_op jit(solution)/shard_map/ppermute | solution.py:249
  8.7 0.8 copy-start.2
  10.2 3.7 %collective-permute-start.1 = (f32[8,1024]{1,0:T(8,128)S(1)}, f32[8,1024]{1,0:T(8,128)S(1)}, u32[]{:S(2)}, u32[]{:S(2)}) collective-permute-start(f32[8,1024]{1,0:T(8,128)S(1)} %add.42), channel_id=1, source_target_pairs={{0,2},{1,3},{2,0},{3,1},{4,6},{5,7},{6,4},{7,5},{8,10},{9,11},{10,... | collective-permute-start | bytes 98312 | tf_op jit(solution)/shard_map/ppermute | solution.py:249
  13.9 2.8 %collective-permute-start.2 = (f32[8,1024]{1,0:T(8,128)S(1)}, f32[8,1024]{1,0:T(8,128)S(1)}, u32[]{:S(2)}, u32[]{:S(2)}) collective-permute-start(f32[8,1024]{1,0:T(8,128)S(1)} %add.43), channel_id=1, source_target_pairs={{0,1},{1,0},{2,3},{3,2},{4,5},{5,4},{6,7},{7,6},{8,9},{9,8},{10,11... | collective-permute-start | bytes 98312 | tf_op jit(solution)/shard_map/ppermute | solution.py:249
  13.9 21.5 %copy-start = (f32[1024,512]{1,0:T(8,128)S(1)}, f32[1024,512]{1,0:T(8,128)}, u32[]{:S(2)}) copy-start(f32[1024,512]{1,0:T(8,128)} %x_ref.1) | copy-start | bytes 6291460
  16.7 3.4 %collective-permute-start.3 = (f32[8,1024]{1,0:T(8,128)S(1)}, f32[8,1024]{1,0:T(8,128)S(1)}, u32[]{:S(2)}, u32[]{:S(2)}) collective-permute-start(f32[8,1024]{1,0:T(8,128)S(1)} %add.44), channel_id=1, source_target_pairs={{0,8},{1,9},{2,10},{3,11},{4,12},{5,13},{6,14},{7,15},{8,0},{9,1},... | collective-permute-start | bytes 98312 | tf_op jit(solution)/shard_map/ppermute | solution.py:249
  18.6 0.7 copy-start.3
  20.2 18.5 %copy-start.1 = (f32[1024,1024]{1,0:T(8,128)S(1)}, f32[1024,1024]{1,0:T(8,128)}, u32[]{:S(2)}) copy-start(f32[1024,1024]{1,0:T(8,128)} %factors_ref.1) | copy-start | bytes 12582916
  20.2 5.6 %collective-permute-start.4 = (f32[8,1024]{1,0:T(8,128)S(1)}, f32[8,1024]{1,0:T(8,128)S(1)}, u32[]{:S(2)}, u32[]{:S(2)}) collective-permute-start(f32[8,1024]{1,0:T(8,128)S(1)} %select_kernel.1), channel_id=1, source_target_pairs={{0,16},{16,0},{32,48},{48,32},{64,80},{80,64},{96,112},{112,96},{1... | collective-permute-start | bytes 98312 | tf_op jit(solution)/shard_map/ppermute | solution.py:255
  25.9 4.6 %collective-permute-start.5 = (f32[8,1024]{1,0:T(8,128)S(1)}, f32[8,1024]{1,0:T(8,128)S(1)}, u32[]{:S(2)}, u32[]{:S(2)}) collective-permute-start(f32[8,1024]{1,0:T(8,128)S(1)} %add.47), channel_id=1, source_target_pairs={{0,112},{1,113},{2,114},{3,115},{4,116},{5,117},{6,118},{7,119},{8... | collective-permute-start | bytes 98312 | tf_op jit(solution)/shard_map/ppermute | solution.py:249
  30.5 4.8 %collective-permute-start.6 = (f32[8,1024]{1,0:T(8,128)S(1)}, f32[8,1024]{1,0:T(8,128)S(1)}, u32[]{:S(2)}, u32[]{:S(2)}) collective-permute-start(f32[8,1024]{1,0:T(8,128)S(1)} %add.48), channel_id=1, source_target_pairs={{0,144},{1,145},{2,146},{3,147},{4,148},{5,149},{6,150},{7,151},{8... | collective-permute-start | bytes 98312 | tf_op jit(solution)/shard_map/ppermute | solution.py:249
  35.4 3.3 %collective-permute-start.7 = (f32[8,1024]{1,0:T(8,128)S(1)}, f32[8,1024]{1,0:T(8,128)S(1)}, u32[]{:S(2)}, u32[]{:S(2)}) collective-permute-start(f32[8,1024]{1,0:T(8,128)S(1)} %add.49), channel_id=1, source_target_pairs={{0,48},{1,49},{2,50},{3,51},{4,52},{5,53},{6,54},{7,55},{8,56},{9,... | collective-permute-start | bytes 98312 | tf_op jit(solution)/shard_map/ppermute | solution.py:249
  49.0 1.4 %collective-permute-start.8 = (f32[8,1024]{1,0:T(8,128)S(1)}, f32[8,1024]{1,0:T(8,128)S(1)}, u32[]{:S(2)}, u32[]{:S(2)}) collective-permute-start(f32[8,1024]{1,0:T(8,128)S(1)} %get-tuple-element.25), channel_id=1, source_target_pairs={{0,16},{16,0},{32,48},{48,32},{64,80},{80,64},{96,112},{112,96},{1... | collective-permute-start | bytes 98312 | tf_op jit(solution)/shard_map/ppermute | solution.py:255
  64.3 2.9 %collective-permute-start.9 = (f32[8,1024]{1,0:T(8,128)S(1)}, f32[8,1024]{1,0:T(8,128)S(1)}, u32[]{:S(2)}, u32[]{:S(2)}) collective-permute-start(f32[8,1024]{1,0:T(8,128)S(1)} %place_kernel.1), channel_id=1, source_target_pairs={{0,8},{1,9},{2,10},{3,11},{4,12},{5,13},{6,14},{7,15},{8,0},{9,1},... | collective-permute-start | bytes 98312 | tf_op jit(solution)/shard_map/ppermute | solution.py:249
  67.2 2.8 %collective-permute-start.10 = (f32[8,1024]{1,0:T(8,128)S(1)}, f32[8,1024]{1,0:T(8,128)S(1)}, u32[]{:S(2)}, u32[]{:S(2)}) collective-permute-start(f32[8,1024]{1,0:T(8,128)S(1)} %add.52), channel_id=1, source_target_pairs={{0,1},{1,0},{2,3},{3,2},{4,5},{5,4},{6,7},{7,6},{8,9},{9,8},{10,11... | collective-permute-start | bytes 98312 | tf_op jit(solution)/shard_map/ppermute | solution.py:249
  70.1 3.7 %collective-permute-start.11 = (f32[8,1024]{1,0:T(8,128)S(1)}, f32[8,1024]{1,0:T(8,128)S(1)}, u32[]{:S(2)}, u32[]{:S(2)}) collective-permute-start(f32[8,1024]{1,0:T(8,128)S(1)} %add.53), channel_id=1, source_target_pairs={{0,2},{1,3},{2,0},{3,1},{4,6},{5,7},{6,4},{7,5},{8,10},{9,11},{10,... | collective-permute-start | bytes 98312 | tf_op jit(solution)/shard_map/ppermute | solution.py:249
  73.7 6.1 %collective-permute-start.12 = (f32[8,1024]{1,0:T(8,128)S(1)}, f32[8,1024]{1,0:T(8,128)S(1)}, u32[]{:S(2)}, u32[]{:S(2)}) collective-permute-start(f32[8,1024]{1,0:T(8,128)S(1)} %add.54), channel_id=1, source_target_pairs={{0,7},{1,6},{2,5},{3,4},{4,3},{5,2},{6,1},{7,0},{8,15},{9,14},{10,... | collective-permute-start | bytes 98312 | tf_op jit(solution)/shard_map/ppermute | solution.py:249
